TPU v7x, 128 devices: a whole 4x4x4 slice. The times are simulated.
128 devices in a mesh: grp: 16 (over z, y), inner: 8 (over x, core).
Axes of the slice: x: 4, y: 4, z: 4, core: 2. Of those that a mesh axis runs over, the one named last changes fastest.
Arguments:
- grid_in: bfloat16 [262144, 474], P(('grp', 'inner')), may hold values from -6 to 6
- g2m_geom: float32 [4, 524288], P(None, ('grp', 'inner')), may hold values from -6 to 6
- g2m_src: int32 [524288], P(('grp', 'inner')), may hold values from 0 to 2047
- g2m_dst: int32 [524288, 1], P(('grp', 'inner')), may hold values from 0 to 127, as said below
- g2m_node: int32 [524288], P(('grp', 'inner')), may hold values from 0 to 319
- mesh_emb: bfloat16 [40960, 512], P(('grp', 'inner')), may hold values from -6 to 6
- mesh_send: int32 [327680], P(('grp', 'inner')), may hold values from 0 to 3199
- mesh_recv: int32 [327680], P(('grp', 'inner')), may hold values from 0 to 319
- w_in1: bfloat16 [474, 512], replicated, may hold values from -0.25 to 0.25
- b_in: float32 [512], replicated, may hold values from -3 to 3
- w_in2: bfloat16 [512, 512], replicated, may hold values from -0.25 to 0.25
- w_g2m: bfloat16 [512, 512], replicated, may hold values from -0.25 to 0.25
- w_geo: float32 [4, 512], replicated, may hold values from -3 to 3
- b_g2m: float32 [512], replicated, may hold values from -3 to 3
- w_enc1: bfloat16 [512, 512], replicated, may hold values from -0.125 to 0.125
- b_enc: float32 [512], replicated, may hold values from -3 to 3
- w_enc2: bfloat16 [512, 512], replicated, may hold values from -0.25 to 0.25
- w_snd: bfloat16 [512, 512], replicated, may hold values from -0.25 to 0.25
- w_rcv: bfloat16 [512, 512], replicated, may hold values from -0.25 to 0.25
- b_edge: float32 [512], replicated, may hold values from -3 to 3
- w_edge: bfloat16 [512, 512], replicated, may hold values from -0.25 to 0.25
- w_p1: bfloat16 [512, 512], replicated, may hold values from -0.125 to 0.125
- w_p2: bfloat16 [512, 512], replicated, may hold values from -0.25 to 0.25
- b_p: float32 [512], replicated, may hold values from -3 to 3
- w_p3: bfloat16 [512, 512], replicated, may hold values from -0.25 to 0.25
Outputs:
- mesh_out: bfloat16 [40960, 512], P(('grp', 'inner'))
Inputs may be any that keep to these rules, and one draw needn't show every extreme that they name: `g2m_src`: grid node of an edge within its own block of 2048 rows. `g2m_dst`: an edge of band b names a band from b - 2 to b + 2; in each aligned block of 4096 edges (the edges of one band) the band itself is named exactly 2048 times and no other band more than 2048 times.
All inputs are finite; a program needn't handle non-finite values.
Results may differ from a plain program's by a relative error of at most 0.02.
Values may be sent and summed in bfloat16 or wider, within the bound.
No kernel may reach another device: no remote copies, remote signals or barrier semaphores. Data moves between devices by JAX's collectives and lax.ppermute only.
A program may use at most 64 MiB of HBM per device.

v0:
```python
import jax
import jax.numpy as jnp
from jax import lax
from jax.sharding import PartitionSpec as P


def passed_along(value, axis, by):
    devices = lax.axis_size(axis)
    pairs = [(i, i + by) for i in range(devices) if 0 <= i + by < devices]
    return lax.ppermute(value, axis, pairs)


def extended_2(block, sides, width):
    for axis, dim in sides:
        count = lax.axis_size(axis)
        forward = [(i, i + 1) for i in range(count - 1)]
        backward = [(target, source) for source, target in forward]
        low = lax.ppermute(
            lax.slice_in_dim(block, block.shape[dim] - width, None, axis=dim), axis, forward
        )
        high = lax.ppermute(lax.slice_in_dim(block, 0, width, axis=dim), axis, backward)
        block = jnp.concatenate([low, block, high], axis=dim)
    return block


def on_device(
    grid_in,
    g2m_geom,
    g2m_src,
    g2m_dst,
    g2m_node,
    mesh_emb,
    mesh_send,
    mesh_recv,
    w_in1,
    b_in,
    w_in2,
    w_g2m,
    w_geo,
    b_g2m,
    w_enc1,
    b_enc,
    w_enc2,
    w_snd,
    w_rcv,
    b_edge,
    w_edge,
    w_p1,
    w_p2,
    b_p,
    w_p3,
):
    places = lax.axis_size("inner")
    nodes_here = mesh_emb.shape[0]
    band = lax.axis_index(("grp", "inner"))
    grid_hid = jax.nn.silu(
        jnp.dot(grid_in, w_in1, preferred_element_type=jnp.float32) + b_in
    ).astype(jnp.bfloat16)
    grid_lat = jnp.dot(grid_hid, w_in2, preferred_element_type=jnp.float32).astype(jnp.bfloat16)
    picked = grid_lat[g2m_src]
    geom_term = lax.dot_general(
        g2m_geom, w_geo, (((0,), (0,)), ((), ())), precision=lax.Precision.HIGHEST
    )
    msg = jax.nn.silu(
        jnp.dot(picked, w_g2m, preferred_element_type=jnp.float32) + geom_term + b_g2m
    ).astype(jnp.bfloat16)
    column = g2m_dst[:, 0] - band + 2
    target = column * nodes_here + g2m_node
    node_ids = jnp.arange(nodes_here, dtype=jnp.int32)

    def band_sum(which):
        select = (node_ids[:, None] + which * nodes_here == target[None, :]).astype(jnp.bfloat16)
        return jnp.dot(select, msg, preferred_element_type=jnp.float32)

    partial_sums = [band_sum(which) for which in range(5)]
    near_above = passed_along(partial_sums[3], ("grp", "inner"), 1)
    near_below = passed_along(partial_sums[1], ("grp", "inner"), -1)
    far_above = passed_along(partial_sums[4], ("grp", "inner"), 2)
    far_below = passed_along(partial_sums[0], ("grp", "inner"), -2)
    agg_g = (partial_sums[2] + near_above + near_below + far_above + far_below).astype(jnp.bfloat16)
    enc = jax.nn.silu(jnp.dot(agg_g, w_enc1, preferred_element_type=jnp.float32) + b_enc).astype(
        jnp.bfloat16
    )
    mesh_lat = (
        mesh_emb.astype(jnp.float32) + jnp.dot(enc, w_enc2, preferred_element_type=jnp.float32)
    ).astype(jnp.bfloat16)
    senders = jnp.dot(mesh_lat, w_snd, preferred_element_type=jnp.float32).astype(jnp.bfloat16)
    receivers = jnp.dot(mesh_lat, w_rcv, preferred_element_type=jnp.float32).astype(jnp.bfloat16)
    piece = lax.all_gather(senders, "inner", axis=0, tiled=True)
    picks = (mesh_send[:, None] == jnp.arange(piece.shape[0], dtype=jnp.int32)[None, :]).astype(
        jnp.bfloat16
    )
    gathered = jnp.dot(picks, piece, preferred_element_type=jnp.float32)
    extended = extended_2(senders, (("grp", 0),), nodes_here)
    rims = jnp.concatenate([extended[:nodes_here], extended[2 * nodes_here :]], axis=0)
    rim_picks = (
        mesh_send[:, None]
        == places * nodes_here + jnp.arange(2 * nodes_here, dtype=jnp.int32)[None, :]
    ).astype(jnp.bfloat16)
    send_rows = gathered + jnp.dot(rim_picks, rims, preferred_element_type=jnp.float32)
    select_recv = (node_ids[:, None] == mesh_recv[None, :]).astype(jnp.bfloat16)
    recv_rows = lax.dot_general(
        select_recv, receivers, (((0,), (0,)), ((), ())), preferred_element_type=jnp.float32
    )
    edge_hid = jax.nn.silu(send_rows + recv_rows + b_edge).astype(jnp.bfloat16)
    edge_lat = jnp.dot(edge_hid, w_edge, preferred_element_type=jnp.float32).astype(jnp.bfloat16)
    agg_m = jnp.dot(select_recv, edge_lat, preferred_element_type=jnp.float32).astype(jnp.bfloat16)
    node_hid = jax.nn.silu(
        jnp.dot(agg_m, w_p1, preferred_element_type=jnp.float32)
        + jnp.dot(mesh_lat, w_p2, preferred_element_type=jnp.float32)
        + b_p
    ).astype(jnp.bfloat16)
    return (
        mesh_lat.astype(jnp.float32) + jnp.dot(node_hid, w_p3, preferred_element_type=jnp.float32)
    ).astype(jnp.bfloat16)


def solution(mesh):
    return jax.shard_map(
        on_device,
        mesh=mesh,
        in_specs=(
            P(("grp", "inner"), None),
            P(None, ("grp", "inner")),
            P(("grp", "inner")),
            P(("grp", "inner"), None),
            P(("grp", "inner")),
            P(("grp", "inner"), None),
            P(("grp", "inner")),
            P(("grp", "inner")),
            P(),
            P(),
            P(),
            P(),
            P(),
            P(),
            P(),
            P(),
            P(),
            P(),
            P(),
            P(),
            P(),
            P(),
            P(),
            P(),
            P(),
        ),
        out_specs=P(("grp", "inner"), None),
        check_vma=False,
    )
```

profile of v0, /device:TPU:96, one launch (start us, length us, event | category | flops | bytes accessed | tf_op | source)
XLA Modules:
  0.0 151.6 jit_solution(5416438398066807134)
XLA Ops:
  6.5 0.9 fusion.64
  7.4 0.7 add_multiply_fusion
  8.1 0.7 add.168
  8.9 5.4 %convolution_convert_fusion.1 = bf16[2048,512]{1,0:T(8,128)(2,1)} fusion(bf16[512,512]{1,0:T(8,128)(2,1)} %param.35, bf16[2048,474]{0,1:T(8,128)(2,1)S(1)} %copy-done, bf16[474,512]{1,0:T(8,128)(2,1)} %param.33, f32[512]{0:T(512)} %param.34), kind=kOutput, calls=%fused_computation.25 | convolution fusion | flops 2075131904 | bytes 5050368 | tf_op jit(solution)/shard_map/dot_general | solution.py:59
  14.3 19.4 %gather_fusion = bf16[4096,512]{1,0:T(8,128)(2,1)} fusion(bf16[2048,512]{1,0:T(8,128)(2,1)} %convolution_convert_fusion.1, s32[4096]{0:T(1024)S(1)} %fusion.64), kind=kCustom, calls=%fused_computation | custom fusion | bytes 8404992 | tf_op jit(solution)/shard_map/gather | solution.py:60
  33.7 0.0 copy-start.11
  33.7 4.6 %fusion.70 = f32[4096,512]{1,0:T(8,128)S(1)} fusion(bf16[4096,512]{1,0:T(8,128)(2,1)} %gather_fusion, bf16[512,512]{1,0:T(8,128)(2,1)S(1)} %copy-done.3), kind=kOutput, calls=%fused_computation.72 | convolution fusion | flops 2147483648 | bytes 13107200 | tf_op jit(solution)/shard_map/dot_general | solution.py:65
  38.3 8.9 %multiply_convert_fusion = bf16[4096,512]{1,0:T(8,128)(2,1)S(1)} fusion(f32[4096,512]{1,0:T(8,128)S(1)} %fusion.70, f32[4,4096]{1,0:T(4,128)S(1)} %copy-done.8, f32[4,512]{1,0:T(4,128)S(1)} %copy-done.10, f32[512]{0:T(512)S(1)} %copy-done.11), kind=kOutput, calls=%fused_computation.4 | convolution fusion | flops 115343360 | bytes 12658688 | tf_op jit(solution)/shard_map/dot_general | solution.py:61
  47.1 1.5 %fusion.4 = f32[320,512]{1,0:T(8,128)S(1)} fusion(bf16[4096,512]{1,0:T(8,128)(2,1)S(1)} %multiply_convert_fusion, s32[4096]{0:T(1024)S(1)} %add.168), kind=kOutput, calls=%fused_computation.9 | convolution fusion | flops 1343488000 | bytes 4866048 | tf_op jit(solution)/shard_map/dot_general | solution.py:73
  48.7 7.1 %collective-permute-start.3 = (f32[320,512]{1,0:T(8,128)S(1)}, f32[320,512]{1,0:T(8,128)}, u32[]{:S(2)}, u32[]{:S(2)}) collective-permute-start(f32[320,512]{1,0:T(8,128)S(1)} %fusion.4), channel_id=1, source_target_pairs={{2,0},{3,1},{4,2},{5,3},{6,4},{7,5},{8,6},{9,7},{10,8},{11,9},{12,... | collective-permute-start | bytes 1966088 | tf_op jit(solution)/shard_map/ppermute | solution.py:10
  55.8 1.6 %fusion.9 = f32[320,512]{1,0:T(8,128)S(1)} fusion(bf16[4096,512]{1,0:T(8,128)(2,1)S(1)} %multiply_convert_fusion, s32[4096]{0:T(1024)S(1)} %add.168, s32[320]{0:T(512)S(1)} %iota_add_fusion.3), kind=kOutput, calls=%fused_computation.14 | convolution fusion | flops 1343488000 | bytes 4867328 | tf_op jit(solution)/shard_map/dot_general | solution.py:73
  57.4 1.9 %collective-permute-start = (f32[320,512]{1,0:T(8,128)S(1)}, f32[320,512]{1,0:T(8,128)}, u32[]{:S(2)}, u32[]{:S(2)}) collective-permute-start(f32[320,512]{1,0:T(8,128)S(1)} %fusion.9), channel_id=1, source_target_pairs={{0,1},{1,2},{2,3},{3,4},{4,5},{5,6},{6,7},{7,8},{8,9},{9,10},{10,1... | collective-permute-start | bytes 1966088 | tf_op jit(solution)/shard_map/ppermute | solution.py:10
  59.3 1.6 %fusion.7 = f32[320,512]{1,0:T(8,128)S(1)} fusion(bf16[4096,512]{1,0:T(8,128)(2,1)S(1)} %multiply_convert_fusion, s32[4096]{0:T(1024)S(1)} %add.168, s32[320]{0:T(512)S(1)} %iota_add_fusion.2), kind=kOutput, calls=%fused_computation.12 | convolution fusion | flops 1343488000 | bytes 4867328 | tf_op jit(solution)/shard_map/dot_general | solution.py:73
  60.9 7.9 %collective-permute-start.1 = (f32[320,512]{1,0:T(8,128)S(1)}, f32[320,512]{1,0:T(8,128)}, u32[]{:S(2)}, u32[]{:S(2)}) collective-permute-start(f32[320,512]{1,0:T(8,128)S(1)} %fusion.7), channel_id=1, source_target_pairs={{1,0},{2,1},{3,2},{4,3},{5,4},{6,5},{7,6},{8,7},{9,8},{10,9},{11,1... | collective-permute-start | bytes 1966088 | tf_op jit(solution)/shard_map/ppermute | solution.py:10
  68.8 1.6 %fusion.5 = f32[320,512]{1,0:T(8,128)S(1)} fusion(bf16[4096,512]{1,0:T(8,128)(2,1)S(1)} %multiply_convert_fusion, s32[4096]{0:T(1024)S(1)} %add.168, s32[320]{0:T(512)S(1)} %iota_add_fusion.1), kind=kOutput, calls=%fused_computation.10 | convolution fusion | flops 1343488000 | bytes 4867328 | tf_op jit(solution)/shard_map/dot_general | solution.py:73
  70.4 1.9 %collective-permute-start.2 = (f32[320,512]{1,0:T(8,128)S(1)}, f32[320,512]{1,0:T(8,128)}, u32[]{:S(2)}, u32[]{:S(2)}) collective-permute-start(f32[320,512]{1,0:T(8,128)S(1)} %fusion.5), channel_id=1, source_target_pairs={{0,2},{1,3},{2,4},{3,5},{4,6},{5,7},{6,8},{7,9},{8,10},{9,11},{10,... | collective-permute-start | bytes 1966088 | tf_op jit(solution)/shard_map/ppermute | solution.py:10
  72.3 0.0 copy-start.2
  72.4 1.3 collective-permute-done
  73.6 3.2 %collective-permute-done.1 = f32[320,512]{1,0:T(8,128)} collective-permute-done((f32[320,512]{1,0:T(8,128)S(1)}, f32[320,512]{1,0:T(8,128)}, u32[]{:S(2)}, u32[]{:S(2)}) %collective-permute-start.1) | collective-permute-done | bytes 655392 | tf_op jit(solution)/shard_map/ppermute | solution.py:10
  76.9 10.9 %collective-permute-done.2 = f32[320,512]{1,0:T(8,128)} collective-permute-done((f32[320,512]{1,0:T(8,128)S(1)}, f32[320,512]{1,0:T(8,128)}, u32[]{:S(2)}, u32[]{:S(2)}) %collective-permute-start.2) | collective-permute-done | bytes 655392 | tf_op jit(solution)/shard_map/ppermute | solution.py:10
  87.8 5.7 %multiply_convert_fusion.4 = bf16[320,512]{1,0:T(8,128)(2,1)} fusion(bf16[512,512]{1,0:T(8,128)(2,1)} %param.39, f32[320,512]{1,0:T(8,128)} %collective-permute-done.3, f32[320,512]{1,0:T(8,128)} %collective-permute-done.2, f32[320,512]{1,0:T(8,128)} %collective-permute-done.1, f32[320,512]{1,0:T(8,128)} %collective-permute-done, ...), kind=kOutput, calls=%fused_computation.57 | convolution fusion | flops 1513062400 | bytes 7687424 | tf_op jit(solution)/shard_map/dot_general | solution.py:81
  93.5 1.4 fusion.49
  94.9 1.1 convolution_convert_fusion.3
  96.0 0.0 all-gather.2.cloned.1.call-update
  96.0 1.9 %collective-permute-start.5 = (bf16[320,512]{1,0:T(8,128)(2,1)}, bf16[320,512]{1,0:T(8,128)(2,1)}, u32[]{:S(2)}, u32[]{:S(2)}) collective-permute-start(bf16[320,512]{1,0:T(8,128)(2,1)} %convolution_convert_fusion.3), channel_id=1, source_target_pairs={{8,0},{16,8},{24,16},{32,24},{40,32},{48,40},{56,48},{64,56},{72,6... | collective-permute-start | bytes 983048 | tf_op jit(solution)/shard_map/ppermute | solution.py:21
  97.9 4.1 %collective-permute-start.4 = (bf16[320,512]{1,0:T(8,128)(2,1)}, bf16[320,512]{1,0:T(8,128)(2,1)}, u32[]{:S(2)}, u32[]{:S(2)}) collective-permute-start(bf16[320,512]{1,0:T(8,128)(2,1)} %convolution_convert_fusion.3), channel_id=1, source_target_pairs={{0,8},{8,16},{16,24},{24,32},{32,40},{40,48},{48,56},{56,64},{64,7... | collective-permute-start | bytes 983048 | tf_op jit(solution)/shard_map/ppermute | solution.py:18
  102.1 5.3 %fusion.17 = f32[2560,512]{1,0:T(8,128)} fusion(s32[2560]{0:T(1024)S(1)} %copy-done.4, bf16[320,512]{1,0:T(8,128)(2,1)S(1)} %fusion.49, bf16[512,512]{1,0:T(8,128)(2,1)} %param.43), kind=kOutput, calls=%fused_computation.23 | convolution fusion | flops 1007616000 | bytes 6105088 | tf_op jit(solution)/shard_map/dot_general | solution.py:102
  107.4 11.1 %all-gather.2.cloned.1.call-done = bf16[2560,512]{1,0:T(8,128)(2,1)} async-done(((bf16[320,512]{1,0:T(8,128)(2,1)}), bf16[2560,512]{1,0:T(8,128)(2,1)}) %all-gather.2.cloned.1.call-update) | async-done | bytes 2621456 | tf_op jit(solution)/shard_map/all_gather | solution.py:89
  118.5 10.9 %fusion = f32[2560,512]{1,0:T(8,128)} fusion(bf16[2560,512]{1,0:T(8,128)(2,1)} %all-gather.2.cloned.1.call-done, s32[2560]{0:T(1024)S(1)} %copy-done.9), kind=kOutput, calls=%fused_computation.2 | convolution fusion | flops 6717440000 | bytes 7874560 | tf_op jit(solution)/shard_map/dot_general | solution.py:93
  129.4 8.8 %convolution_convert_fusion = bf16[2560,512]{1,0:T(8,128)(2,1)} fusion(bf16[512,512]{1,0:T(8,128)(2,1)S(1)} %copy-done.5, f32[2560,512]{1,0:T(8,128)} %fusion.17, f32[2560,512]{1,0:T(8,128)} %fusion, s32[640]{0:T(1024)S(1)} %iota_add_fusion, s32[2560]{0:T(1024)S(1)} %copy-done.9, f32[512]{0:T(512)S(1)} %copy-done.13, ...), kind=kOutput, calls=%fused_computation.18 | convolution fusion | flops 3034644480 | bytes 14301696 | tf_op jit(solution)/shard_map/dot_general | solution.py:106
  138.2 3.9 %fusion.51 = f32[320,512]{1,0:T(8,128)} fusion(bf16[512,512]{1,0:T(8,128)(2,1)S(1)} %copy-done.6, bf16[2560,512]{1,0:T(8,128)(2,1)} %convolution_convert_fusion, s32[2560]{0:T(1024)S(1)} %copy-done.4), kind=kOutput, calls=%fused_computation.52 | convolution fusion | flops 1007616000 | bytes 3811328 | tf_op jit(solution)/shard_map/dot_general | solution.py:109
  142.1 2.6 %fusion.50 = bf16[320,512]{1,0:T(8,128)(2,1)} fusion(bf16[512,512]{1,0:T(8,128)(2,1)S(1)} %copy-done.7, f32[320,512]{1,0:T(8,128)} %fusion.51, bf16[320,512]{1,0:T(8,128)(2,1)S(1)} %fusion.49, bf16[512,512]{1,0:T(8,128)(2,1)} %param.47, f32[512]{0:T(512)S(1)} %copy-done.14), kind=kOutput, calls=%fused_computation.49 | convolution fusion | flops 337182720 | bytes 2361344 | tf_op jit(solution)/shard_map/dot_general | solution.py:114
  (39 shorter events, 0.1 us)
Async XLA Ops:
  6.5 2.3 %copy-start = (bf16[2048,474]{0,1:T(8,128)(2,1)S(1)}, bf16[2048,474]{0,1:T(8,128)(2,1)}, u32[]{:S(2)}) copy-start(bf16[2048,474]{0,1:T(8,128)(2,1)} %param.25) | copy-start | bytes 5824516
  6.5 111.9 %all-gather.2.cloned.1.call-start = ((), (), s32[]{:S(2)}) async-start(), calls=%async_computation | async-start | bytes 2949120 | tf_op jit(solution)/shard_map/all_gather | solution.py:89
  14.3 19.4 %copy-start.3 = (bf16[512,512]{1,0:T(8,128)(2,1)S(1)}, bf16[512,512]{1,0:T(8,128)(2,1)}, u32[]{:S(2)}) copy-start(bf16[512,512]{1,0:T(8,128)(2,1)} %param.36) | copy-start | bytes 1572868
  33.6 4.6 %copy-start.8 = (f32[4,4096]{1,0:T(4,128)S(1)}, f32[4,4096]{1,0:T(4,128)}, u32[]{:S(2)}) copy-start(f32[4,4096]{1,0:T(4,128)} %param.26) | copy-start | bytes 196612
  33.6 4.6 %copy-start.10 = (f32[4,512]{1,0:T(4,128)S(1)}, f32[4,512]{1,0:T(4,128)}, u32[]{:S(2)}) copy-start(f32[4,512]{1,0:T(4,128)} %param.37) | copy-start | bytes 24580
  33.7 4.6 %copy-start.11 = (f32[512]{0:T(512)S(1)}, f32[512]{0:T(512)}, u32[]{:S(2)}) copy-start(f32[512]{0:T(512)} %param.38) | copy-start | bytes 6148
  47.1 21.6 %copy-start.15 = (bf16[4096,512]{1,0:T(8,128)(2,1)}, bf16[4096,512]{1,0:T(8,128)(2,1)S(1)}, u32[]{:S(2)}) copy-start(bf16[4096,512]{1,0:T(8,128)(2,1)S(1)} %multiply_convert_fusion) | copy-start | bytes 12582916
  48.7 23.7 %collective-permute-start.3 = (f32[320,512]{1,0:T(8,128)S(1)}, f32[320,512]{1,0:T(8,128)}, u32[]{:S(2)}, u32[]{:S(2)}) collective-permute-start(f32[320,512]{1,0:T(8,128)S(1)} %fusion.4), channel_id=1, source_target_pairs={{2,0},{3,1},{4,2},{5,3},{6,4},{7,5},{8,6},{9,7},{10,8},{11,9},{12,... | collective-permute-start | bytes 1966088 | tf_op jit(solution)/shard_map/ppermute | solution.py:10
  57.4 16.2 %collective-permute-start = (f32[320,512]{1,0:T(8,128)S(1)}, f32[320,512]{1,0:T(8,128)}, u32[]{:S(2)}, u32[]{:S(2)}) collective-permute-start(f32[320,512]{1,0:T(8,128)S(1)} %fusion.9), channel_id=1, source_target_pairs={{0,1},{1,2},{2,3},{3,4},{4,5},{5,6},{6,7},{7,8},{8,9},{9,10},{10,1... | collective-permute-start | bytes 1966088 | tf_op jit(solution)/shard_map/ppermute | solution.py:10
  60.9 16.0 %collective-permute-start.1 = (f32[320,512]{1,0:T(8,128)S(1)}, f32[320,512]{1,0:T(8,128)}, u32[]{:S(2)}, u32[]{:S(2)}) collective-permute-start(f32[320,512]{1,0:T(8,128)S(1)} %fusion.7), channel_id=1, source_target_pairs={{1,0},{2,1},{3,2},{4,3},{5,4},{6,5},{7,6},{8,7},{9,8},{10,9},{11,1... | collective-permute-start | bytes 1966088 | tf_op jit(solution)/shard_map/ppermute | solution.py:10
  68.8 19.0 %copy-start.12 = (f32[512]{0:T(512)S(1)}, f32[512]{0:T(512)}, u32[]{:S(2)}) copy-start(f32[512]{0:T(512)} %param.40) | copy-start | bytes 6148
  70.4 17.4 %collective-permute-start.2 = (f32[320,512]{1,0:T(8,128)S(1)}, f32[320,512]{1,0:T(8,128)}, u32[]{:S(2)}, u32[]{:S(2)}) collective-permute-start(f32[320,512]{1,0:T(8,128)S(1)} %fusion.5), channel_id=1, source_target_pairs={{0,2},{1,3},{2,4},{3,5},{4,6},{5,7},{6,8},{7,9},{8,10},{9,11},{10,... | collective-permute-start | bytes 1966088 | tf_op jit(solution)/shard_map/ppermute | solution.py:10
  72.3 21.2 %copy-start.1 = (bf16[512,512]{1,0:T(8,128)(2,1)S(1)}, bf16[512,512]{1,0:T(8,128)(2,1)}, u32[]{:S(2)}) copy-start(bf16[512,512]{1,0:T(8,128)(2,1)} %param.41) | copy-start | bytes 1572868
  72.3 22.6 %copy-start.2 = (bf16[512,512]{1,0:T(8,128)(2,1)S(1)}, bf16[512,512]{1,0:T(8,128)(2,1)}, u32[]{:S(2)}) copy-start(bf16[512,512]{1,0:T(8,128)(2,1)} %param.42) | copy-start | bytes 1572868
  72.3 29.8 %copy-start.4 = (s32[2560]{0:T(1024)S(1)}, s32[2560]{0:T(1024)}, u32[]{:S(2)}) copy-start(s32[2560]{0:T(1024)} %param.32) | copy-start | bytes 30724
  93.5 25.0 %copy-start.9 = (s32[2560]{0:T(1024)S(1)}, s32[2560]{0:T(1024)}, u32[]{:S(2)}) copy-start(s32[2560]{0:T(1024)} %param.31) | copy-start | bytes 30724
  96.0 33.4 %collective-permute-start.5 = (bf16[320,512]{1,0:T(8,128)(2,1)}, bf16[320,512]{1,0:T(8,128)(2,1)}, u32[]{:S(2)}, u32[]{:S(2)}) collective-permute-start(bf16[320,512]{1,0:T(8,128)(2,1)} %convolution_convert_fusion.3), channel_id=1, source_target_pairs={{8,0},{16,8},{24,16},{32,24},{40,32},{48,40},{56,48},{64,56},{72,6... | collective-permute-start | bytes 983048 | tf_op jit(solution)/shard_map/ppermute | solution.py:21
  97.9 31.5 %collective-permute-start.4 = (bf16[320,512]{1,0:T(8,128)(2,1)}, bf16[320,512]{1,0:T(8,128)(2,1)}, u32[]{:S(2)}, u32[]{:S(2)}) collective-permute-start(bf16[320,512]{1,0:T(8,128)(2,1)} %convolution_convert_fusion.3), channel_id=1, source_target_pairs={{0,8},{8,16},{16,24},{24,32},{32,40},{40,48},{48,56},{56,64},{64,7... | collective-permute-start | bytes 983048 | tf_op jit(solution)/shard_map/ppermute | solution.py:18
  107.4 22.0 %copy-start.5 = (bf16[512,512]{1,0:T(8,128)(2,1)S(1)}, bf16[512,512]{1,0:T(8,128)(2,1)}, u32[]{:S(2)}) copy-start(bf16[512,512]{1,0:T(8,128)(2,1)} %param.45) | copy-start | bytes 1572868
  107.4 22.0 %copy-start.13 = (f32[512]{0:T(512)S(1)}, f32[512]{0:T(512)}, u32[]{:S(2)}) copy-start(f32[512]{0:T(512)} %param.44) | copy-start | bytes 6148
  129.4 8.8 %copy-start.6 = (bf16[512,512]{1,0:T(8,128)(2,1)S(1)}, bf16[512,512]{1,0:T(8,128)(2,1)}, u32[]{:S(2)}) copy-start(bf16[512,512]{1,0:T(8,128)(2,1)} %param.46) | copy-start | bytes 1572868
  138.2 3.9 %copy-start.7 = (bf16[512,512]{1,0:T(8,128)(2,1)S(1)}, bf16[512,512]{1,0:T(8,128)(2,1)}, u32[]{:S(2)}) copy-start(bf16[512,512]{1,0:T(8,128)(2,1)} %param.49) | copy-start | bytes 1572868
  138.2 3.9 %copy-start.14 = (f32[512]{0:T(512)S(1)}, f32[512]{0:T(512)}, u32[]{:S(2)}) copy-start(f32[512]{0:T(512)} %param.48) | copy-start | bytes 6148
Sparse Core Ops, SparseCore 0:
  96.1 22.2 all-gather.1
where the time goes:
time: 154 us; the launch traced here: 152 us
  matrix products  64.7 us (42%)
  waiting for transfers between devices  26.5 us (17%)
  starting transfers between devices  24.9 us (16%)
  local copies, waits for them, and re-layouts  19.5 us (13%)
  between operations  13.7 us (9%)
  other arithmetic  2.34 us (2%)
    gather x1, local copies, waits for them, and re-layouts, on_device(): picked = grid_lat[g2m_src]  19.4 us
    ppermute x4, starting transfers between devices, passed_along(): return lax.ppermute(value, axis, pairs)  18.8 us
    ppermute x4, waiting for transfers between devices, passed_along(): return lax.ppermute(value, axis, pairs)  15.4 us
    all_gather x1, waiting for transfers between devices, on_device(): piece = lax.all_gather(senders, 'inner', axis=0, tiled=True)  11.1 us
    dot_general x1, matrix products, on_device(): gathered = jnp.dot(picks, piece, preferred_element_type=jnp.float32)  10.9 us
    dot_general x1, matrix products, on_device(): lax.dot_general(g2m_geom, w_geo, (((0,), (0,)), ((), ())), precision=lax....  8.87 us
    dot_general x1, matrix products, on_device(): jnp.dot(edge_hid, w_edge, preferred_element_type=jnp.float32)  8.75 us
    dot_general x4, matrix products, band_sum(): return jnp.dot(select, msg, preferred_element_type=jnp.float32)  6.19 us
  transfers between devices with their start and end apart: 7, of which 4 were waited for; matrix products, arithmetic and copies ran while one was open for 14% of the time, Pallas kernels for 0%

commit v1 on v0

v1 whole, which is shorter than its diff:
```python
import jax
import jax.numpy as jnp
from jax import lax
from jax.experimental import pallas as pl
from jax.experimental.pallas import tpu as pltpu
from jax.sharding import PartitionSpec as P

F32 = jnp.float32
BF16 = jnp.bfloat16
LANES = 128
EDGE_BLOCK = 256
BOTH = ("grp", "inner")
VMEM_BYTES = 48 * 2**20


def silu(v):
    half = v * 0.5
    return half + half * jnp.tanh(half)


def split3(v):
    high = v.astype(BF16).astype(F32)
    rest = v - high
    mid = rest.astype(BF16).astype(F32)
    return high, mid, (rest - mid).astype(BF16).astype(F32)


def dot(a, b):
    return jnp.dot(a, b, preferred_element_type=F32)


def put_rows(table, first, rows):
    parts = rows.shape[1] // LANES
    for j in range(parts):
        table[pl.ds(first * parts + j, rows.shape[0], stride=parts), :] = rows[
            :, j * LANES : (j + 1) * LANES
        ]


def message_kernel(
    src, grid_in, w_in1, b_in, w_in2, w_g2m, geom, w_geo, b_g2m, msg, table, buf_a, buf_b, w8, g8, w48
):
    w_both = dot(w_in2[...], w_g2m[...]).astype(BF16)
    w8[...] = jnp.zeros_like(w8)
    w8[0:4, :] = w_geo[...]
    w8[4:5, :] = b_g2m[...]
    high, mid, low = split3(w8[...])
    w48[...] = jnp.concatenate([high, high, high, mid, mid, low], axis=0).astype(BF16)
    g8[...] = jnp.zeros_like(g8)
    g8[0:4, :] = geom[...]
    g8[4:5, :] = jnp.ones((1, g8.shape[1]), F32)
    for k in range(grid_in.shape[0] // 256):
        hid = silu(dot(grid_in[k * 256 : (k + 1) * 256, :], w_in1[...]) + b_in[...]).astype(BF16)
        put_rows(table, k * 256, dot(hid, w_both))

    def gather(base, buf):
        for e in range(EDGE_BLOCK):
            row = pl.multiple_of(src[base + e] * 4, 4)
            buf[4 * e : 4 * e + 4, :] = table[pl.ds(row, 4), :]

    def emit(base, buf):
        base = pl.multiple_of(base, EDGE_BLOCK)
        high, mid, low = split3(g8[:, pl.ds(base, EDGE_BLOCK)])
        g48 = jnp.concatenate([high, mid, low, high, mid, high], axis=0).astype(BF16)
        geo = lax.dot_general(g48, w48[...], (((0,), (0,)), ((), ())), preferred_element_type=F32)
        for j in range(4):
            v = buf[pl.ds(j, EDGE_BLOCK, stride=4), :] + geo[:, j * LANES : (j + 1) * LANES]
            msg[pl.ds(base, EDGE_BLOCK), j * LANES : (j + 1) * LANES] = silu(v).astype(BF16)

    blocks = msg.shape[0] // EDGE_BLOCK
    gather(0, buf_a)

    def step(t, carry):
        base = t * (2 * EDGE_BLOCK)
        gather(base + EDGE_BLOCK, buf_b)
        emit(base, buf_a)
        gather(jnp.minimum(base + 2 * EDGE_BLOCK, (blocks - 1) * EDGE_BLOCK), buf_a)
        emit(base + EDGE_BLOCK, buf_b)
        return carry

    lax.fori_loop(0, blocks // 2, step, 0)


def messages(g2m_src, grid_in, w_in1, b_in, w_in2, w_g2m, geom, w_geo, b_g2m):
    edges, nodes, width = g2m_src.shape[0], grid_in.shape[0], w_in1.shape[1]
    vmem = pl.BlockSpec(memory_space=pltpu.VMEM)
    return pl.pallas_call(
        message_kernel,
        out_shape=jax.ShapeDtypeStruct((edges, width), BF16),
        in_specs=[pl.BlockSpec(memory_space=pltpu.SMEM)] + [vmem] * 8,
        out_specs=vmem,
        scratch_shapes=[
            pltpu.VMEM((4 * nodes, LANES), F32),
            pltpu.VMEM((4 * EDGE_BLOCK, LANES), F32),
            pltpu.VMEM((4 * EDGE_BLOCK, LANES), F32),
            pltpu.VMEM((8, width), F32),
            pltpu.VMEM((8, edges), F32),
            pltpu.VMEM((48, width), BF16),
        ],
        compiler_params=pltpu.CompilerParams(vmem_limit_bytes=VMEM_BYTES),
        name="messages",
    )(g2m_src, grid_in, w_in1, b_in.reshape(1, -1), w_in2, w_g2m, geom, w_geo, b_g2m.reshape(1, -1))


def encoder_kernel(own, near, one, two, emb, w_enc1, b_enc, w_enc2, w_snd, w_rcv, b_edge, lat, snd, rcv):
    total = own[...] + near[...].astype(F32) + one[...].astype(F32) + two[...].astype(F32)
    enc = silu(dot(total.astype(BF16), w_enc1[...]) + b_enc[...]).astype(BF16)
    mesh_lat = (emb[...].astype(F32) + dot(enc, w_enc2[...])).astype(BF16)
    lat[...] = mesh_lat
    snd[...] = dot(mesh_lat, w_snd[...]).astype(BF16)
    rcv[...] = dot(mesh_lat, w_rcv[...]) + b_edge[...]


def encoder(own, near, one, two, emb, w_enc1, b_enc, w_enc2, w_snd, w_rcv, b_edge):
    vmem = pl.BlockSpec(memory_space=pltpu.VMEM)
    rows, width = emb.shape
    return pl.pallas_call(
        encoder_kernel,
        out_shape=[
            jax.ShapeDtypeStruct((rows, width), BF16),
            jax.ShapeDtypeStruct((rows, width), BF16),
            jax.ShapeDtypeStruct((rows, width), F32),
        ],
        in_specs=[vmem] * 11,
        out_specs=[vmem] * 3,
        compiler_params=pltpu.CompilerParams(vmem_limit_bytes=VMEM_BYTES),
        name="encoder",
    )(own, near, one, two, emb, w_enc1, b_enc.reshape(1, -1), w_enc2, w_snd, w_rcv, b_edge.reshape(1, -1))


def processor_kernel(
    place, send, recv, *refs
):
    shards = refs[:10]
    rcv, recv_row, lat, w_edge, w_p1, w_p2, b_p, w_p3, out, table, rtable, buf_a, buf_b, hid = refs[10:]
    rows = lat.shape[0]
    for k in range(10):
        put_rows(table, place[k], shards[k][...].astype(F32))
    put_rows(rtable, 0, rcv[...])

    def gather(base, buf):
        for e in range(EDGE_BLOCK):
            s = pl.multiple_of(send[base + e] * 4, 4)
            r = pl.multiple_of(recv[base + e] * 4, 4)
            buf[4 * e : 4 * e + 4, :] = table[pl.ds(s, 4), :] + rtable[pl.ds(r, 4), :]

    def emit(base, buf):
        base = pl.multiple_of(base, EDGE_BLOCK)
        for j in range(4):
            v = buf[pl.ds(j, EDGE_BLOCK, stride=4), :]
            hid[pl.ds(base, EDGE_BLOCK), j * LANES : (j + 1) * LANES] = silu(v).astype(BF16)

    blocks = hid.shape[0] // EDGE_BLOCK
    gather(0, buf_a)

    def step(t, carry):
        base = t * (2 * EDGE_BLOCK)
        gather(base + EDGE_BLOCK, buf_b)
        emit(base, buf_a)
        gather(jnp.minimum(base + 2 * EDGE_BLOCK, (blocks - 1) * EDGE_BLOCK), buf_a)
        emit(base + EDGE_BLOCK, buf_b)
        return carry

    lax.fori_loop(0, blocks // 2, step, 0)
    ids = lax.broadcasted_iota(jnp.int32, (rows, hid.shape[0]), 0)
    select = jnp.where(ids == recv_row[...], 1.0, 0.0).astype(BF16)
    agg = dot(dot(select, hid[...]).astype(BF16), w_edge[...]).astype(BF16)
    mesh_lat = lat[...]
    node = silu(dot(agg, w_p1[...]) + dot(mesh_lat, w_p2[...]) + b_p[...]).astype(BF16)
    out[...] = (mesh_lat.astype(F32) + dot(node, w_p3[...])).astype(BF16)


def processor(place, send, recv, shards, rcv, lat, w_edge, w_p1, w_p2, b_p, w_p3):
    vmem = pl.BlockSpec(memory_space=pltpu.VMEM)
    smem = pl.BlockSpec(memory_space=pltpu.SMEM)
    rows, width = lat.shape
    edges = send.shape[0]
    return pl.pallas_call(
        processor_kernel,
        out_shape=jax.ShapeDtypeStruct((rows, width), BF16),
        in_specs=[smem] * 3 + [vmem] * 18,
        out_specs=vmem,
        scratch_shapes=[
            pltpu.VMEM((4 * 10 * rows, LANES), F32),
            pltpu.VMEM((4 * rows, LANES), F32),
            pltpu.VMEM((4 * EDGE_BLOCK, LANES), F32),
            pltpu.VMEM((4 * EDGE_BLOCK, LANES), F32),
            pltpu.VMEM((edges, width), BF16),
        ],
        compiler_params=pltpu.CompilerParams(vmem_limit_bytes=VMEM_BYTES),
        name="processor",
    )(
        place, send, recv, *shards, rcv, recv.reshape(1, -1), lat, w_edge, w_p1, w_p2, b_p.reshape(1, -1), w_p3
    )


def on_device(
    grid_in,
    g2m_geom,
    g2m_src,
    g2m_dst,
    g2m_node,
    mesh_emb,
    mesh_send,
    mesh_recv,
    w_in1,
    b_in,
    w_in2,
    w_g2m,
    w_geo,
    b_g2m,
    w_enc1,
    b_enc,
    w_enc2,
    w_snd,
    w_rcv,
    b_edge,
    w_edge,
    w_p1,
    w_p2,
    b_p,
    w_p3,
):
    groups, places = lax.axis_size("grp"), lax.axis_size("inner")
    bands = groups * places
    nodes_here = mesh_emb.shape[0]
    band = lax.axis_index(BOTH)
    place = lax.axis_index("inner")
    core = place % 2

    def by_parity(even, odd):
        pairs = [(b, b + (odd if b % 2 else even)) for b in range(bands)]
        pairs = [pair for pair in pairs if 0 <= pair[1] < bands]
        return lambda value: lax.ppermute(value, BOTH, pairs)

    def along_x(value, by):
        return lax.ppermute(value, "inner", [(i, (i + 2 * by) % places) for i in range(places)])

    def along_groups(value, by):
        pairs = [(i, i + by) for i in range(groups) if 0 <= i + by < groups]
        return lax.ppermute(value, "grp", pairs)

    other_core = by_parity(1, -1)

    msg = messages(g2m_src, grid_in, w_in1, b_in, w_in2, w_g2m, g2m_geom, w_geo, b_g2m)
    target = (g2m_dst[:, 0] - band + 2) * nodes_here + g2m_node
    node_ids = jnp.arange(nodes_here, dtype=jnp.int32)

    def band_sum(which):
        select = (node_ids[:, None] + which * nodes_here == target[None, :]).astype(BF16)
        return dot(select, msg)

    crossing = other_core(band_sum(jnp.where(core == 0, 1, 3)).astype(BF16))
    two = by_parity(-2, 2)(band_sum(jnp.where(core == 0, 0, 4)).astype(BF16))
    joint = band_sum(jnp.where(core == 0, 4, 0)) + crossing.astype(F32)
    one = by_parity(2, -2)(joint.astype(BF16))
    near = other_core(band_sum(jnp.where(core == 0, 3, 1)).astype(BF16))
    own = band_sum(2)
    mesh_lat, senders, receivers = encoder(
        own, near, one, two, mesh_emb, w_enc1, b_enc, w_enc2, w_snd, w_rcv, b_edge
    )

    right = along_x(senders, 1)
    left = along_x(senders, -1)
    far = along_x(senders, 2)
    low = along_groups(senders, 1)
    high = along_groups(senders, -1)
    shards = [senders, right, left, far]
    shards = shards + [other_core(shard) for shard in shards] + [low, high]
    mine = [place, (place - 2) % places, (place + 2) % places, (place + 4) % places]
    where = mine + [p + 1 - 2 * core for p in mine] + [places, places + 1]
    starts = jnp.stack([jnp.asarray(p, jnp.int32) for p in where]) * nodes_here
    return processor(
        starts, mesh_send, mesh_recv, shards, receivers, mesh_lat, w_edge, w_p1, w_p2, b_p, w_p3
    )


def solution(mesh):
    split = P(BOTH)
    rows = P(BOTH, None)
    return jax.shard_map(
        on_device,
        mesh=mesh,
        in_specs=(rows, P(None, BOTH), split, rows, split, rows, split, split) + (P(),) * 17,
        out_specs=rows,
        check_vma=False,
    )
```

time: 154 us -> 93.2 us (0.61); the launches traced: 152 us -> 92.7 us
  matrix products: 64.7 us -> 16.7 us
  Pallas kernels: 0 us -> 24.7 us
  between operations: 13.7 us -> 0.56 us
  local copies, waits for them, and re-layouts: 19.5 us -> 6.71 us
  starting transfers between devices: 24.9 us -> 17.6 us
    dot_general x15 -> x5, matrix products: 64.7 us -> 16.7 us  [dot(): return jnp.dot(a, b, preferred_element_type=F32)]
    pallas_call x0 -> x3, Pallas kernels: none -> 24.7 us  [the longest x1 13 us: messages(): pl.pallas_call(message_kernel, out_shape=jax.ShapeDtypeStruct((edges, wid...]
    gather x1 -> x0, local copies, waits for them, and re-layouts: 19.4 us -> none  [on_device(): picked = grid_lat[g2m_src]]
    all_gather x1 -> x0, waiting for transfers between devices: 11.1 us -> none  [on_device(): piece = lax.all_gather(senders, 'inner', axis=0, tiled=True)]
    ppermute x6 -> x13, waiting for transfers between devices: 15.4 us -> 25 us  [the longest x3 9.96 us: along_x(): lax.ppermute(value, 'inner', [(i, (i + 2 * by) % places) for i in range(p...]
    ppermute x6 -> x13, starting transfers between devices: 24.9 us -> 17.6 us  [the longest x8 10.5 us: by_parity(): return lambda value: lax.ppermute(value, BOTH, pairs)]
    unnamed x32 -> x53, local copies, waits for them, and re-layouts: 0.08 us -> 6.61 us
  transfers between devices with their start and end apart: 7 -> 13, of which waited for: 4 -> 3; matrix products, arithmetic and copies ran while one was open for 14% -> 14% of each run, Pallas kernels for 0% -> 0%
where the time goes in v1:
time: 93.2 us; the launch traced here: 92.7 us
  waiting for transfers between devices  25 us (27%)
  Pallas kernels  24.7 us (27%)
  starting transfers between devices  17.6 us (19%)
  matrix products  16.7 us (18%)
  local copies, waits for them, and re-layouts  6.71 us (7%)
  other arithmetic  1.49 us (2%)
    dot_general x5, matrix products, dot(): return jnp.dot(a, b, preferred_element_type=F32)  16.7 us
    pallas_call x1, Pallas kernels, messages(): pl.pallas_call(message_kernel, out_shape=jax.ShapeDtypeStruct((edges, wid...  13 us
    pallas_call x1, Pallas kernels, processor(): pl.pallas_call(processor_kernel, out_shape=jax.ShapeDtypeStruct((rows, wi...  10.6 us
    ppermute x8, starting transfers between devices, by_parity(): return lambda value: lax.ppermute(value, BOTH, pairs)  10.5 us
    ppermute x3, waiting for transfers between devices, along_x(): lax.ppermute(value, 'inner', [(i, (i + 2 * by) % places) for i in range(p...  9.96 us
    ppermute x8, waiting for transfers between devices, by_parity(): return lambda value: lax.ppermute(value, BOTH, pairs)  9.43 us
    unnamed x53, local copies, waits for them, and re-layouts  6.61 us
    ppermute x2, waiting for transfers between devices, along_groups(): return lax.ppermute(value, 'grp', pairs)  5.6 us
  transfers between devices with their start and end apart: 13, of which 3 were waited for; matrix products, arithmetic and copies ran while one was open for 14% of the time, Pallas kernels for 0%

profile of v1, /device:TPU:96, one launch (start us, length us, event | category | flops | bytes accessed | tf_op | source)
XLA Modules:
  0.0 92.7 jit_solution(18041205758303938433)
XLA Ops:
  0.1 2.9 %copy.26.grid_in = bf16[2048,474]{1,0:T(8,128)(2,1)S(1)} copy(bf16[2048,474]{0,1:T(8,128)(2,1)} %param.25) | data formatting | bytes 3883008 | tf_op args[0]
  3.0 0.7 add_multiply_fusion
  3.8 0.7 add.118
  4.5 0.0 copy-start.11
  4.6 1.0 %copy-done.11 = bf16[474,512]{1,0:T(8,128)(2,1)S(1)} copy-done((bf16[474,512]{1,0:T(8,128)(2,1)S(1)}, bf16[474,512]{1,0:T(8,128)(2,1)}, u32[]{:S(2)}) %copy-start.11) | copy-done | bytes 485400
  5.6 13.0 %messages.1 = bf16[4096,512]{1,0:T(8,128)(2,1)} custom-call(s32[4096]{0:T(1024)S(1)} %copy-done.17, bf16[2048,474]{1,0:T(8,128)(2,1)S(1)} %copy.26.grid_in, bf16[474,512]{1,0:T(8,128)(2,1)S(1)} %copy-done.11, f32[1,512]{1,0:T(1,128)S(1)} %bitcast.22, bf16[512,512]{1,0:T(8,128)(2,1)S(1)} %copy-done.1, bf16[512,512]{1,0:T(8,128)(2,1)S(1)} %copy-done.2, ...), custom_call_target="tpu_custom_call" | custom-call | tf_op jit(solution)/shard_map/messages/pallas_call | solution.py:87
  18.6 3.7 %fusion.20 = bf16[320,512]{1,0:T(8,128)(2,1)S(1)} fusion(bf16[4096,512]{1,0:T(8,128)(2,1)} %messages.1, s32[4096]{0:T(1024)S(1)} %add.118, s32[320]{0:T(512)S(1)} %iota_add_fusion.3), kind=kOutput, calls=%fused_computation.20 | convolution fusion | flops 1343651840 | bytes 4539648 | tf_op jit(solution)/shard_map/dot_general | solution.py:29
  22.4 0.1 collective-permute-start
  22.5 3.7 %fusion.23 = bf16[320,512]{1,0:T(8,128)(2,1)S(1)} fusion(bf16[4096,512]{1,0:T(8,128)(2,1)} %messages.1, s32[4096]{0:T(1024)S(1)} %add.118, s32[320]{0:T(512)S(1)} %iota_add_fusion.1), kind=kOutput, calls=%fused_computation.21 | convolution fusion | flops 1343651840 | bytes 4539648 | tf_op jit(solution)/shard_map/dot_general | solution.py:29
  26.2 0.6 collective-permute-start.1
  26.8 3.7 %fusion.26 = bf16[320,512]{1,0:T(8,128)(2,1)S(1)} fusion(bf16[4096,512]{1,0:T(8,128)(2,1)} %messages.1, s32[4096]{0:T(1024)S(1)} %add.118, s32[320]{0:T(512)S(1)} %iota_add_fusion), kind=kOutput, calls=%fused_computation.22 | convolution fusion | flops 1343651840 | bytes 4539648 | tf_op jit(solution)/shard_map/dot_general | solution.py:29
  30.5 7.0 %collective-permute-start.3 = (bf16[320,512]{1,0:T(8,128)(2,1)S(1)}, bf16[320,512]{1,0:T(8,128)(2,1)S(1)}, u32[]{:S(2)}, u32[]{:S(2)}) collective-permute-start(bf16[320,512]{1,0:T(8,128)(2,1)S(1)} %fusion.26), channel_id=1, source_target_pairs={{1,3},{2,0},{3,5},{4,2},{5,7},{6,4},{7,9},{8,6},{9,11},{10,8},{11,... | collective-permute-start | bytes 983048 | tf_op jit(solution)/shard_map/ppermute | solution.py:234
  37.6 3.9 %add_convert_fusion = bf16[320,512]{1,0:T(8,128)(2,1)S(1)} fusion(bf16[320,512]{1,0:T(8,128)(2,1)S(1)} %collective-permute-done.1, bf16[4096,512]{1,0:T(8,128)(2,1)} %messages.1, s32[4096]{0:T(1024)S(1)} %add.118, s32[320]{0:T(512)S(1)} %iota_add_fusion.2), kind=kOutput, calls=%fused_computation.23 | convolution fusion | flops 1343979520 | bytes 4867328 | tf_op jit(solution)/shard_map/dot_general | solution.py:29
  41.5 0.0 copy-start.3
  41.5 0.0 copy-start.4
  41.6 2.2 %collective-permute-start.2 = (bf16[320,512]{1,0:T(8,128)(2,1)S(1)}, bf16[320,512]{1,0:T(8,128)(2,1)S(1)}, u32[]{:S(2)}, u32[]{:S(2)}) collective-permute-start(bf16[320,512]{1,0:T(8,128)(2,1)S(1)} %add_convert_fusion), channel_id=1, source_target_pairs={{0,2},{2,4},{3,1},{4,6},{5,3},{6,8},{7,5},{8,10},{9,7},{10,12},{11... | collective-permute-start | bytes 983048 | tf_op jit(solution)/shard_map/ppermute | solution.py:234
  43.8 1.6 %fusion.8.own = f32[320,512]{1,0:T(8,128)S(1)} fusion(bf16[4096,512]{1,0:T(8,128)(2,1)S(1)} %copy-done.25, s32[4096]{0:T(1024)S(1)} %add.118, s32[320]{0:T(512)S(1)} %iota_add_fusion.4), kind=kOutput, calls=%fused_computation.8 | convolution fusion | flops 1343488000 | bytes 4867328 | tf_op jit(solution)/shard_map/dot_general | solution.py:29
  45.5 9.4 %collective-permute-done.2.one = bf16[320,512]{1,0:T(8,128)(2,1)S(1)} collective-permute-done((bf16[320,512]{1,0:T(8,128)(2,1)S(1)}, bf16[320,512]{1,0:T(8,128)(2,1)S(1)}, u32[]{:S(2)}, u32[]{:S(2)}) %collective-permute-start.2) | collective-permute-done | bytes 327712 | tf_op jit(solution)/shard_map/ppermute | solution.py:234
  55.0 1.0 %encoder.1 = (bf16[320,512]{1,0:T(8,128)(2,1)S(1)}, bf16[320,512]{1,0:T(8,128)(2,1)S(1)}, f32[320,512]{1,0:T(8,128)S(1)}) custom-call(f32[320,512]{1,0:T(8,128)S(1)} %fusion.8.own, bf16[320,512]{1,0:T(8,128)(2,1)S(1)} %collective-permute-done.near, bf16[320,512]{1,0:T(8,128)(2,1)S(1)} %collective-permute-done.2.one, ...), custom_call_target="tpu_custom_call" | custom-call | tf_op jit(solution)/shard_map/encoder/pallas_call | solution.py:117
  56.0 0.8 copy-done
  56.9 3.2 %collective-permute-start.5 = (bf16[320,512]{1,0:T(8,128)(2,1)S(1)}, bf16[320,512]{1,0:T(8,128)(2,1)S(1)}, u32[]{:S(2)}, u32[]{:S(2)}) collective-permute-start(bf16[320,512]{1,0:T(8,128)(2,1)S(1)} %get-tuple-element.8.refs_0_), channel_id=1, source_target_pairs={{0,6},{1,7},{2,0},{3,1},{4,2},{5,3},{6,4},{7,5},{8,14},{9,15},{10,... | collective-permute-start | bytes 983048 | tf_op jit(solution)/shard_map/ppermute | solution.py:237
  60.1 1.9 %collective-permute-start.11 = (bf16[320,512]{1,0:T(8,128)(2,1)S(1)}, bf16[320,512]{1,0:T(8,128)(2,1)}, u32[]{:S(2)}, u32[]{:S(2)}) collective-permute-start(bf16[320,512]{1,0:T(8,128)(2,1)S(1)} %get-tuple-element.8.refs_0_), channel_id=1, source_target_pairs={{0,8},{8,16},{16,24},{24,32},{32,40},{40,48},{48,56},{56,64},{64,7... | collective-permute-start | bytes 983048 | tf_op jit(solution)/shard_map/ppermute | solution.py:241
  62.0 10.0 %collective-permute-done.4.refs_1_ = bf16[320,512]{1,0:T(8,128)(2,1)S(1)} collective-permute-done((bf16[320,512]{1,0:T(8,128)(2,1)S(1)}, bf16[320,512]{1,0:T(8,128)(2,1)S(1)}, u32[]{:S(2)}, u32[]{:S(2)}) %collective-permute-start.4) | collective-permute-done | bytes 327712 | tf_op jit(solution)/shard_map/ppermute | solution.py:237
  72.0 1.9 %collective-permute-start.12 = (bf16[320,512]{1,0:T(8,128)(2,1)S(1)}, bf16[320,512]{1,0:T(8,128)(2,1)}, u32[]{:S(2)}, u32[]{:S(2)}) collective-permute-start(bf16[320,512]{1,0:T(8,128)(2,1)S(1)} %get-tuple-element.8.refs_0_), channel_id=1, source_target_pairs={{8,0},{16,8},{24,16},{32,24},{40,32},{48,40},{56,48},{64,56},{72,6... | collective-permute-start | bytes 983048 | tf_op jit(solution)/shard_map/ppermute | solution.py:241
  73.9 0.1 collective-permute-start.8
  74.0 0.5 collective-permute-start.9
  74.5 0.7 copy-done.13
  75.2 0.1 collective-permute-start.10
  75.4 0.1 stack.35
  75.5 5.6 %collective-permute-done.12.refs_9_ = bf16[320,512]{1,0:T(8,128)(2,1)} collective-permute-done((bf16[320,512]{1,0:T(8,128)(2,1)S(1)}, bf16[320,512]{1,0:T(8,128)(2,1)}, u32[]{:S(2)}, u32[]{:S(2)}) %collective-permute-start.12) | collective-permute-done | bytes 327712 | tf_op jit(solution)/shard_map/ppermute | solution.py:241
  81.1 1.0 %copy-done.14 = bf16[320,512]{1,0:T(8,128)(2,1)S(1)} copy-done((bf16[320,512]{1,0:T(8,128)(2,1)S(1)}, bf16[320,512]{1,0:T(8,128)(2,1)}, u32[]{:S(2)}) %copy-start.14) | copy-done | bytes 327704
  82.1 10.6 %processor.1 = bf16[320,512]{1,0:T(8,128)(2,1)} custom-call(s32[10]{0:T(128)S(1)} %broadcast_multiply_fusion.place, s32[2560]{0:T(1024)S(1)} %copy-done.18, s32[2560]{0:T(1024)S(1)} %copy-done.16, bf16[320,512]{1,0:T(8,128)(2,1)S(1)} %get-tuple-element.8.refs_0_, bf16[320,512]{1,0:T(8,128)(2,1)S(1)} %collective-permute-done.4.refs_1_, ...), custom_call_target="tpu_custom_call" | custom-call | tf_op jit(solution)/shard_map/processor/pallas_call | solution.py:178
  (65 shorter events, 0.2 us)
Async XLA Ops:
  0.0 4.5 %copy-start.2 = (bf16[512,512]{1,0:T(8,128)(2,1)S(1)}, bf16[512,512]{1,0:T(8,128)(2,1)}, u32[]{:S(2)}) copy-start(bf16[512,512]{1,0:T(8,128)(2,1)} %w_g2m.1) | copy-start | bytes 1572868
  0.0 4.5 %copy-start.15 = (f32[4,4096]{1,0:T(4,128)S(1)}, f32[4,4096]{1,0:T(4,128)}, u32[]{:S(2)}) copy-start(f32[4,4096]{1,0:T(4,128)} %geom.1) | copy-start | bytes 196612
  0.0 4.5 %copy-start.19 = (f32[4,512]{1,0:T(4,128)S(1)}, f32[4,512]{1,0:T(4,128)}, u32[]{:S(2)}) copy-start(f32[4,512]{1,0:T(4,128)} %w_geo.1) | copy-start | bytes 24580
  0.0 4.5 %copy-start.24 = (f32[512]{0:T(512)S(1)}, f32[512]{0:T(512)}, u32[]{:S(2)}) copy-start(f32[512]{0:T(512)} %param.38) | copy-start | bytes 6148
  22.4 23.1 %collective-permute-start = (bf16[320,512]{1,0:T(8,128)(2,1)S(1)}, bf16[320,512]{1,0:T(8,128)(2,1)S(1)}, u32[]{:S(2)}, u32[]{:S(2)}) collective-permute-start(bf16[320,512]{1,0:T(8,128)(2,1)S(1)} %fusion.20), channel_id=1, source_target_pairs={{0,1},{1,0},{2,3},{3,2},{4,5},{5,4},{6,7},{7,6},{8,9},{9,8},{10,11... | collective-permute-start | bytes 983048 | tf_op jit(solution)/shard_map/ppermute | solution.py:234
  26.2 11.3 %collective-permute-start.1 = (bf16[320,512]{1,0:T(8,128)(2,1)S(1)}, bf16[320,512]{1,0:T(8,128)(2,1)S(1)}, u32[]{:S(2)}, u32[]{:S(2)}) collective-permute-start(bf16[320,512]{1,0:T(8,128)(2,1)S(1)} %fusion.23), channel_id=1, source_target_pairs={{0,1},{1,0},{2,3},{3,2},{4,5},{5,4},{6,7},{7,6},{8,9},{9,8},{10,11... | collective-permute-start | bytes 983048 | tf_op jit(solution)/shard_map/ppermute | solution.py:234
  30.5 14.9 %collective-permute-start.3 = (bf16[320,512]{1,0:T(8,128)(2,1)S(1)}, bf16[320,512]{1,0:T(8,128)(2,1)S(1)}, u32[]{:S(2)}, u32[]{:S(2)}) collective-permute-start(bf16[320,512]{1,0:T(8,128)(2,1)S(1)} %fusion.26), channel_id=1, source_target_pairs={{1,3},{2,0},{3,5},{4,2},{5,7},{6,4},{7,9},{8,6},{9,11},{10,8},{11,... | collective-permute-start | bytes 983048 | tf_op jit(solution)/shard_map/ppermute | solution.py:234
  37.6 6.3 %copy-start.25 = (bf16[4096,512]{1,0:T(8,128)(2,1)S(1)}, bf16[4096,512]{1,0:T(8,128)(2,1)}, u32[]{:S(2)}) copy-start(bf16[4096,512]{1,0:T(8,128)(2,1)} %messages.1) | copy-start | bytes 12582916
  41.5 13.4 %copy-start.3 = (bf16[512,512]{1,0:T(8,128)(2,1)S(1)}, bf16[512,512]{1,0:T(8,128)(2,1)}, u32[]{:S(2)}) copy-start(bf16[512,512]{1,0:T(8,128)(2,1)} %w_enc1.1) | copy-start | bytes 1572868
  41.5 13.4 %copy-start.4 = (bf16[512,512]{1,0:T(8,128)(2,1)S(1)}, bf16[512,512]{1,0:T(8,128)(2,1)}, u32[]{:S(2)}) copy-start(bf16[512,512]{1,0:T(8,128)(2,1)} %w_enc2.1) | copy-start | bytes 1572868
  41.5 13.4 %copy-start.5 = (bf16[512,512]{1,0:T(8,128)(2,1)S(1)}, bf16[512,512]{1,0:T(8,128)(2,1)}, u32[]{:S(2)}) copy-start(bf16[512,512]{1,0:T(8,128)(2,1)} %w_snd.1) | copy-start | bytes 1572868
  41.5 13.4 %copy-start.6 = (bf16[512,512]{1,0:T(8,128)(2,1)S(1)}, bf16[512,512]{1,0:T(8,128)(2,1)}, u32[]{:S(2)}) copy-start(bf16[512,512]{1,0:T(8,128)(2,1)} %w_rcv.1) | copy-start | bytes 1572868
  41.5 13.4 %copy-start.12 = (bf16[320,512]{1,0:T(8,128)(2,1)S(1)}, bf16[320,512]{1,0:T(8,128)(2,1)}, u32[]{:S(2)}) copy-start(bf16[320,512]{1,0:T(8,128)(2,1)} %emb.1) | copy-start | bytes 983044
  41.6 13.4 %copy-start.20 = (f32[512]{0:T(512)S(1)}, f32[512]{0:T(512)}, u32[]{:S(2)}) copy-start(f32[512]{0:T(512)} %param.40) | copy-start | bytes 6148
  41.6 13.4 %copy-start.21 = (f32[512]{0:T(512)S(1)}, f32[512]{0:T(512)}, u32[]{:S(2)}) copy-start(f32[512]{0:T(512)} %param.44) | copy-start | bytes 6148
  41.6 33.8 %copy-start.16 = (s32[2560]{0:T(1024)S(1)}, s32[2560]{0:T(1024)}, u32[]{:S(2)}) copy-start(s32[2560]{0:T(1024)} %recv.1) | copy-start | bytes 30724
  41.6 13.3 %collective-permute-start.2 = (bf16[320,512]{1,0:T(8,128)(2,1)S(1)}, bf16[320,512]{1,0:T(8,128)(2,1)S(1)}, u32[]{:S(2)}, u32[]{:S(2)}) collective-permute-start(bf16[320,512]{1,0:T(8,128)(2,1)S(1)} %add_convert_fusion), channel_id=1, source_target_pairs={{0,2},{2,4},{3,1},{4,6},{5,3},{6,8},{7,5},{8,10},{9,7},{10,12},{11... | collective-permute-start | bytes 983048 | tf_op jit(solution)/shard_map/ppermute | solution.py:234
  45.4 35.7 %copy-start.7 = (bf16[512,512]{1,0:T(8,128)(2,1)S(1)}, bf16[512,512]{1,0:T(8,128)(2,1)}, u32[]{:S(2)}) copy-start(bf16[512,512]{1,0:T(8,128)(2,1)} %refs_13_.1) | copy-start | bytes 1572868
  45.4 35.7 %copy-start.8 = (bf16[512,512]{1,0:T(8,128)(2,1)S(1)}, bf16[512,512]{1,0:T(8,128)(2,1)}, u32[]{:S(2)}) copy-start(bf16[512,512]{1,0:T(8,128)(2,1)} %refs_14_.1) | copy-start | bytes 1572868
  45.4 35.7 %copy-start.9 = (bf16[512,512]{1,0:T(8,128)(2,1)S(1)}, bf16[512,512]{1,0:T(8,128)(2,1)}, u32[]{:S(2)}) copy-start(bf16[512,512]{1,0:T(8,128)(2,1)} %refs_15_.1) | copy-start | bytes 1572868
  45.4 35.6 %copy-start.10 = (bf16[512,512]{1,0:T(8,128)(2,1)S(1)}, bf16[512,512]{1,0:T(8,128)(2,1)}, u32[]{:S(2)}) copy-start(bf16[512,512]{1,0:T(8,128)(2,1)} %refs_17_.1) | copy-start | bytes 1572868
  45.5 35.6 %copy-start.18 = (s32[2560]{0:T(1024)S(1)}, s32[2560]{0:T(1024)}, u32[]{:S(2)}) copy-start(s32[2560]{0:T(1024)} %send.1) | copy-start | bytes 30724
  45.5 35.6 %copy-start.22 = (f32[512]{0:T(512)S(1)}, f32[512]{0:T(512)}, u32[]{:S(2)}) copy-start(f32[512]{0:T(512)} %param.48) | copy-start | bytes 6148
  56.9 15.1 %collective-permute-start.4 = (bf16[320,512]{1,0:T(8,128)(2,1)S(1)}, bf16[320,512]{1,0:T(8,128)(2,1)S(1)}, u32[]{:S(2)}, u32[]{:S(2)}) collective-permute-start(bf16[320,512]{1,0:T(8,128)(2,1)S(1)} %get-tuple-element.8.refs_0_), channel_id=1, source_target_pairs={{0,2},{1,3},{2,4},{3,5},{4,6},{5,7},{6,0},{7,1},{8,10},{9,11},{10,... | collective-permute-start | bytes 983048 | tf_op jit(solution)/shard_map/ppermute | solution.py:237
  56.9 17.0 %collective-permute-start.5 = (bf16[320,512]{1,0:T(8,128)(2,1)S(1)}, bf16[320,512]{1,0:T(8,128)(2,1)S(1)}, u32[]{:S(2)}, u32[]{:S(2)}) collective-permute-start(bf16[320,512]{1,0:T(8,128)(2,1)S(1)} %get-tuple-element.8.refs_0_), channel_id=1, source_target_pairs={{0,6},{1,7},{2,0},{3,1},{4,2},{5,3},{6,4},{7,5},{8,14},{9,15},{10,... | collective-permute-start | bytes 983048 | tf_op jit(solution)/shard_map/ppermute | solution.py:237
  60.1 13.9 %collective-permute-start.6 = (bf16[320,512]{1,0:T(8,128)(2,1)S(1)}, bf16[320,512]{1,0:T(8,128)(2,1)}, u32[]{:S(2)}, u32[]{:S(2)}) collective-permute-start(bf16[320,512]{1,0:T(8,128)(2,1)S(1)} %get-tuple-element.8.refs_0_), channel_id=1, source_target_pairs={{0,4},{1,5},{2,6},{3,7},{4,0},{5,1},{6,2},{7,3},{8,12},{9,13},{10,... | collective-permute-start | bytes 983048 | tf_op jit(solution)/shard_map/ppermute | solution.py:237
  60.1 14.4 %collective-permute-start.7 = (bf16[320,512]{1,0:T(8,128)(2,1)S(1)}, bf16[320,512]{1,0:T(8,128)(2,1)S(1)}, u32[]{:S(2)}, u32[]{:S(2)}) collective-permute-start(bf16[320,512]{1,0:T(8,128)(2,1)S(1)} %get-tuple-element.8.refs_0_), channel_id=1, source_target_pairs={{0,1},{1,0},{2,3},{3,2},{4,5},{5,4},{6,7},{7,6},{8,9},{9,8},{10,11... | collective-permute-start | bytes 983048 | tf_op jit(solution)/shard_map/ppermute | solution.py:234
  60.1 15.3 %collective-permute-start.11 = (bf16[320,512]{1,0:T(8,128)(2,1)S(1)}, bf16[320,512]{1,0:T(8,128)(2,1)}, u32[]{:S(2)}, u32[]{:S(2)}) collective-permute-start(bf16[320,512]{1,0:T(8,128)(2,1)S(1)} %get-tuple-element.8.refs_0_), channel_id=1, source_target_pairs={{0,8},{8,16},{16,24},{24,32},{32,40},{40,48},{48,56},{56,64},{64,7... | collective-permute-start | bytes 983048 | tf_op jit(solution)/shard_map/ppermute | solution.py:241
  72.0 9.1 %collective-permute-start.12 = (bf16[320,512]{1,0:T(8,128)(2,1)S(1)}, bf16[320,512]{1,0:T(8,128)(2,1)}, u32[]{:S(2)}, u32[]{:S(2)}) collective-permute-start(bf16[320,512]{1,0:T(8,128)(2,1)S(1)} %get-tuple-element.8.refs_0_), channel_id=1, source_target_pairs={{8,0},{16,8},{24,16},{32,24},{40,32},{48,40},{56,48},{64,56},{72,6... | collective-permute-start | bytes 983048 | tf_op jit(solution)/shard_map/ppermute | solution.py:241
  73.9 7.1 %collective-permute-start.8 = (bf16[320,512]{1,0:T(8,128)(2,1)S(1)}, bf16[320,512]{1,0:T(8,128)(2,1)}, u32[]{:S(2)}, u32[]{:S(2)}) collective-permute-start(bf16[320,512]{1,0:T(8,128)(2,1)S(1)} %collective-permute-done.4.refs_1_), channel_id=1, source_target_pairs={{0,1},{1,0},{2,3},{3,2},{4,5},{5,4},{6,7},{7,6},{8,9},{9,8},{10,11... | collective-permute-start | bytes 983048 | tf_op jit(solution)/shard_map/ppermute | solution.py:234
  74.0 7.0 %collective-permute-start.9 = (bf16[320,512]{1,0:T(8,128)(2,1)S(1)}, bf16[320,512]{1,0:T(8,128)(2,1)}, u32[]{:S(2)}, u32[]{:S(2)}) collective-permute-start(bf16[320,512]{1,0:T(8,128)(2,1)S(1)} %collective-permute-done.5.refs_2_), channel_id=1, source_target_pairs={{0,1},{1,0},{2,3},{3,2},{4,5},{5,4},{6,7},{7,6},{8,9},{9,8},{10,11... | collective-permute-start | bytes 983048 | tf_op jit(solution)/shard_map/ppermute | solution.py:234
  75.2 5.8 %collective-permute-start.10 = (bf16[320,512]{1,0:T(8,128)(2,1)}, bf16[320,512]{1,0:T(8,128)(2,1)}, u32[]{:S(2)}, u32[]{:S(2)}) collective-permute-start(bf16[320,512]{1,0:T(8,128)(2,1)} %collective-permute-done.6.refs_3_), channel_id=1, source_target_pairs={{0,1},{1,0},{2,3},{3,2},{4,5},{5,4},{6,7},{7,6},{8,9},{9,8},{10,11... | collective-permute-start | bytes 983048 | tf_op jit(solution)/shard_map/ppermute | solution.py:234
  (7 other events, 17.1 us)

commit v2 on v1

--- a/solution.py
+++ b/solution.py
@@ -27,6 +27,10 @@
 
 def dot(a, b):
     return jnp.dot(a, b, preferred_element_type=F32)
+
+
+def dot_first(a, b):
+    return lax.dot_general(a, b, (((0,), (0,)), ((), ())), preferred_element_type=F32)
 
 
 def put_rows(table, first, rows):
@@ -49,8 +53,9 @@
     g8[...] = jnp.zeros_like(g8)
     g8[0:4, :] = geom[...]
     g8[4:5, :] = jnp.ones((1, g8.shape[1]), F32)
-    for k in range(grid_in.shape[0] // 256):
-        hid = silu(dot(grid_in[k * 256 : (k + 1) * 256, :], w_in1[...]) + b_in[...]).astype(BF16)
+    for k in range(grid_in.shape[1] // 256):
+        hid = dot_first(grid_in[:, k * 256 : (k + 1) * 256], w_in1[...])
+        hid = silu(hid + b_in[...]).astype(BF16)
         put_rows(table, k * 256, dot(hid, w_both))
 
     def gather(base, buf):
@@ -62,7 +67,7 @@
         base = pl.multiple_of(base, EDGE_BLOCK)
         high, mid, low = split3(g8[:, pl.ds(base, EDGE_BLOCK)])
         g48 = jnp.concatenate([high, mid, low, high, mid, high], axis=0).astype(BF16)
-        geo = lax.dot_general(g48, w48[...], (((0,), (0,)), ((), ())), preferred_element_type=F32)
+        geo = dot_first(g48, w48[...])
         for j in range(4):
             v = buf[pl.ds(j, EDGE_BLOCK, stride=4), :] + geo[:, j * LANES : (j + 1) * LANES]
             msg[pl.ds(base, EDGE_BLOCK), j * LANES : (j + 1) * LANES] = silu(v).astype(BF16)
@@ -82,7 +87,7 @@
 
 
 def messages(g2m_src, grid_in, w_in1, b_in, w_in2, w_g2m, geom, w_geo, b_g2m):
-    edges, nodes, width = g2m_src.shape[0], grid_in.shape[0], w_in1.shape[1]
+    edges, nodes, width = g2m_src.shape[0], grid_in.shape[1], w_in1.shape[1]
     vmem = pl.BlockSpec(memory_space=pltpu.VMEM)
     return pl.pallas_call(
         message_kernel,
@@ -233,8 +238,9 @@
         pairs = [pair for pair in pairs if 0 <= pair[1] < bands]
         return lambda value: lax.ppermute(value, BOTH, pairs)
 
-    def along_x(value, by):
-        return lax.ppermute(value, "inner", [(i, (i + 2 * by) % places) for i in range(places)])
+    def onward(value):
+        pairs = [(i, (i + (-2 if i % 2 else 2)) % places) for i in range(places)]
+        return lax.ppermute(value, "inner", pairs)
 
     def along_groups(value, by):
         pairs = [(i, i + by) for i in range(groups) if 0 <= i + by < groups]
@@ -242,33 +248,38 @@
 
     other_core = by_parity(1, -1)
 
-    msg = messages(g2m_src, grid_in, w_in1, b_in, w_in2, w_g2m, g2m_geom, w_geo, b_g2m)
-    target = (g2m_dst[:, 0] - band + 2) * nodes_here + g2m_node
+    msg = messages(g2m_src, grid_in.T, w_in1, b_in, w_in2, w_g2m, g2m_geom, w_geo, b_g2m)
+    offset = (g2m_dst[:, 0] - band) * (1 - 2 * core) + 2
+    target = offset * nodes_here + g2m_node
     node_ids = jnp.arange(nodes_here, dtype=jnp.int32)
 
     def band_sum(which):
         select = (node_ids[:, None] + which * nodes_here == target[None, :]).astype(BF16)
         return dot(select, msg)
 
-    crossing = other_core(band_sum(jnp.where(core == 0, 1, 3)).astype(BF16))
-    two = by_parity(-2, 2)(band_sum(jnp.where(core == 0, 0, 4)).astype(BF16))
-    joint = band_sum(jnp.where(core == 0, 4, 0)) + crossing.astype(F32)
+    crossing = other_core(band_sum(1).astype(BF16))
+    two = by_parity(-2, 2)(band_sum(0).astype(BF16))
+    joint = band_sum(4) + crossing.astype(F32)
     one = by_parity(2, -2)(joint.astype(BF16))
-    near = other_core(band_sum(jnp.where(core == 0, 3, 1)).astype(BF16))
+    near = other_core(band_sum(3).astype(BF16))
     own = band_sum(2)
     mesh_lat, senders, receivers = encoder(
         own, near, one, two, mesh_emb, w_enc1, b_enc, w_enc2, w_snd, w_rcv, b_edge
     )
 
-    right = along_x(senders, 1)
-    left = along_x(senders, -1)
-    far = along_x(senders, 2)
+    next_a = onward(senders)
+    partner = other_core(senders)
+    next_b = onward(partner)
     low = along_groups(senders, 1)
     high = along_groups(senders, -1)
-    shards = [senders, right, left, far]
-    shards = shards + [other_core(shard) for shard in shards] + [low, high]
-    mine = [place, (place - 2) % places, (place + 2) % places, (place + 4) % places]
-    where = mine + [p + 1 - 2 * core for p in mine] + [places, places + 1]
+    far = onward(next_a)
+    shards = [senders, partner, next_a, next_b, far]
+    shards = shards + [other_core(shard) for shard in shards[2:]] + [low, high]
+    turn = 2 * (1 - 2 * core)
+    before, far_back, after, far_on = [(place + turn * by) % places for by in (-1, -2, 1, 2)]
+    twin = 1 - 2 * core
+    where = [place, place + twin, before, before + twin, far_back]
+    where = where + [after + twin, after, far_on + twin, places, places + 1]
     starts = jnp.stack([jnp.asarray(p, jnp.int32) for p in where]) * nodes_here
     return processor(
         starts, mesh_send, mesh_recv, shards, receivers, mesh_lat, w_edge, w_p1, w_p2, b_p, w_p3

time: 93.2 us -> 90.2 us (0.968)
  the two profiles are of different devices: /device:TPU:96 before, /device:TPU:92 now
where the time goes in v2:
time: 90.2 us; the launch traced here: 89.5 us
  starting transfers between devices  26.7 us (30%)
  Pallas kernels  24.8 us (27%)
  waiting for transfers between devices  16.8 us (19%)
  matrix products  10.1 us (11%)
  local copies, waits for them, and re-layouts  9.31 us (10%)
  other arithmetic  1.48 us (2%)
    pallas_call x1, Pallas kernels, messages(): pl.pallas_call(message_kernel, out_shape=jax.ShapeDtypeStruct((edges, wid...  13.1 us
    pallas_call x1, Pallas kernels, processor(): pl.pallas_call(processor_kernel, out_shape=jax.ShapeDtypeStruct((rows, wi...  10.7 us
    dot_general x5, matrix products, dot(): return jnp.dot(a, b, preferred_element_type=F32)  10.1 us
    ppermute x3, starting transfers between devices, onward(): return lax.ppermute(value, 'inner', pairs)  9.89 us
    ppermute x2, starting transfers between devices, along_groups(): return lax.ppermute(value, 'grp', pairs)  9.33 us
    unnamed x50, local copies, waits for them, and re-layouts  9.22 us
    ppermute x2, waiting for transfers between devices, along_groups(): return lax.ppermute(value, 'grp', pairs)  8.43 us
    ppermute x8, starting transfers between devices, by_parity(): return lambda value: lax.ppermute(value, BOTH, pairs)  7.47 us
  transfers between devices with their start and end apart: 13, of which 4 were waited for; matrix products, arithmetic and copies ran while one was open for 7% of the time, Pallas kernels for 0%

profile of v2, /device:TPU:92, one launch (start us, length us, event | category | flops | bytes accessed | tf_op | source)
XLA Modules:
  0.0 89.5 jit_solution(8975092042215605217)
XLA Ops:
  0.0 0.7 add_multiply_fusion
  0.7 0.7 add.118
  1.5 1.5 %copy-done = bf16[2048,474]{0,1:T(8,128)(2,1)S(1)} copy-done((bf16[2048,474]{0,1:T(8,128)(2,1)S(1)}, bf16[2048,474]{0,1:T(8,128)(2,1)}, u32[]{:S(2)}) %copy-start) | copy-done | bytes 1941528
  3.0 1.0 %copy-done.2 = bf16[512,512]{1,0:T(8,128)(2,1)S(1)} copy-done((bf16[512,512]{1,0:T(8,128)(2,1)S(1)}, bf16[512,512]{1,0:T(8,128)(2,1)}, u32[]{:S(2)}) %copy-start.2) | copy-done | bytes 524312
  4.1 1.0 %copy-done.3 = bf16[512,512]{1,0:T(8,128)(2,1)S(1)} copy-done((bf16[512,512]{1,0:T(8,128)(2,1)S(1)}, bf16[512,512]{1,0:T(8,128)(2,1)}, u32[]{:S(2)}) %copy-start.3) | copy-done | bytes 524312
  5.1 1.0 %copy-done.12 = bf16[474,512]{1,0:T(8,128)(2,1)S(1)} copy-done((bf16[474,512]{1,0:T(8,128)(2,1)S(1)}, bf16[474,512]{1,0:T(8,128)(2,1)}, u32[]{:S(2)}) %copy-start.12) | copy-done | bytes 485400
  6.1 0.8 copy-done.14
  7.0 0.7 copy-done.16
  7.7 0.7 copy-done.18
  8.4 0.7 copy-done.22
  9.1 0.7 copy-done.23
  9.7 13.1 %messages.1 = bf16[4096,512]{1,0:T(8,128)(2,1)} custom-call(s32[4096]{0:T(1024)S(1)} %copy-done.16, bf16[474,2048]{1,0:T(8,128)(2,1)S(1)} %bitcast.20, bf16[474,512]{1,0:T(8,128)(2,1)S(1)} %copy-done.12, f32[1,512]{1,0:T(1,128)S(1)} %bitcast.24, bf16[512,512]{1,0:T(8,128)(2,1)S(1)} %copy-done.2, bf16[512,512]{1,0:T(8,128)(2,1)S(1)} %copy-done.3, ...), custom_call_target="tpu_custom_call" | custom-call | tf_op jit(solution)/shard_map/messages/pallas_call | solution.py:92
  22.9 3.9 %fusion.21 = bf16[320,512]{1,0:T(8,128)(2,1)S(1)} fusion(bf16[4096,512]{1,0:T(8,128)(2,1)} %messages.1, s32[4096]{0:T(1024)S(1)} %add.118, s32[320]{0:T(512)S(1)} %iota_add_fusion), kind=kOutput, calls=%fused_computation.20 | convolution fusion | flops 1343651840 | bytes 4539648 | tf_op jit(solution)/shard_map/dot_general | solution.py:29
  26.9 1.6 %fusion.18 = bf16[320,512]{1,0:T(8,128)(2,1)S(1)} fusion(bf16[4096,512]{1,0:T(8,128)(2,1)S(1)} %copy-done.24, s32[4096]{0:T(1024)S(1)} %add.118, s32[320]{0:T(512)S(1)} %iota_add_fusion.2), kind=kOutput, calls=%fused_computation.19 | convolution fusion | flops 1343651840 | bytes 4539648 | tf_op jit(solution)/shard_map/dot_general | solution.py:29
  28.4 0.6 collective-permute-start
  29.0 1.5 %fusion.24 = bf16[320,512]{1,0:T(8,128)(2,1)S(1)} fusion(bf16[4096,512]{1,0:T(8,128)(2,1)S(1)} %copy-done.24, s32[4096]{0:T(1024)S(1)} %add.118), kind=kOutput, calls=%fused_computation.21 | convolution fusion | flops 1343651840 | bytes 4538368 | tf_op jit(solution)/shard_map/dot_general | solution.py:29
  30.5 2.4 %collective-permute-start.3 = (bf16[320,512]{1,0:T(8,128)(2,1)S(1)}, bf16[320,512]{1,0:T(8,128)(2,1)S(1)}, u32[]{:S(2)}, u32[]{:S(2)}) collective-permute-start(bf16[320,512]{1,0:T(8,128)(2,1)S(1)} %fusion.24), channel_id=1, source_target_pairs={{1,3},{2,0},{3,5},{4,2},{5,7},{6,4},{7,9},{8,6},{9,11},{10,8},{11,... | collective-permute-start | bytes 983048 | tf_op jit(solution)/shard_map/ppermute | solution.py:239
  33.0 1.6 %add_convert_fusion = bf16[320,512]{1,0:T(8,128)(2,1)S(1)} fusion(bf16[320,512]{1,0:T(8,128)(2,1)S(1)} %collective-permute-done.1, bf16[4096,512]{1,0:T(8,128)(2,1)S(1)} %copy-done.24, s32[4096]{0:T(1024)S(1)} %add.118, s32[320]{0:T(512)S(1)} %iota_add_fusion.1), kind=kOutput, calls=%fused_computation.22 | convolution fusion | flops 1343979520 | bytes 4867328 | tf_op jit(solution)/shard_map/dot_general | solution.py:29
  34.7 3.7 %collective-permute-start.2 = (bf16[320,512]{1,0:T(8,128)(2,1)S(1)}, bf16[320,512]{1,0:T(8,128)(2,1)S(1)}, u32[]{:S(2)}, u32[]{:S(2)}) collective-permute-start(bf16[320,512]{1,0:T(8,128)(2,1)S(1)} %add_convert_fusion), channel_id=1, source_target_pairs={{0,2},{2,4},{3,1},{4,6},{5,3},{6,8},{7,5},{8,10},{9,7},{10,12},{11... | collective-permute-start | bytes 983048 | tf_op jit(solution)/shard_map/ppermute | solution.py:239
  38.4 1.6 %fusion.7.own = f32[320,512]{1,0:T(8,128)S(1)} fusion(bf16[4096,512]{1,0:T(8,128)(2,1)S(1)} %copy-done.24, s32[4096]{0:T(1024)S(1)} %add.118, s32[320]{0:T(512)S(1)} %iota_add_fusion.3), kind=kOutput, calls=%fused_computation.8 | convolution fusion | flops 1343488000 | bytes 4867328 | tf_op jit(solution)/shard_map/dot_general | solution.py:29
  40.0 3.7 %collective-permute-done.2.one = bf16[320,512]{1,0:T(8,128)(2,1)S(1)} collective-permute-done((bf16[320,512]{1,0:T(8,128)(2,1)S(1)}, bf16[320,512]{1,0:T(8,128)(2,1)S(1)}, u32[]{:S(2)}, u32[]{:S(2)}) %collective-permute-start.2) | collective-permute-done | bytes 327712 | tf_op jit(solution)/shard_map/ppermute | solution.py:239
  43.8 1.0 %encoder.1 = (bf16[320,512]{1,0:T(8,128)(2,1)S(1)}, bf16[320,512]{1,0:T(8,128)(2,1)S(1)}, f32[320,512]{1,0:T(8,128)S(1)}) custom-call(f32[320,512]{1,0:T(8,128)S(1)} %fusion.7.own, bf16[320,512]{1,0:T(8,128)(2,1)S(1)} %collective-permute-done.near, bf16[320,512]{1,0:T(8,128)(2,1)S(1)} %collective-permute-done.2.one, ...), custom_call_target="tpu_custom_call" | custom-call | tf_op jit(solution)/shard_map/encoder/pallas_call | solution.py:122
  44.8 0.9 copy-done.1
  45.7 4.4 %collective-permute-start.5 = (bf16[320,512]{1,0:T(8,128)(2,1)S(1)}, bf16[320,512]{1,0:T(8,128)(2,1)S(1)}, u32[]{:S(2)}, u32[]{:S(2)}) collective-permute-start(bf16[320,512]{1,0:T(8,128)(2,1)S(1)} %get-tuple-element.8.refs_0_), channel_id=1, source_target_pairs={{0,2},{1,7},{2,4},{3,1},{4,6},{5,3},{6,0},{7,5},{8,10},{9,15},{10,... | collective-permute-start | bytes 983048 | tf_op jit(solution)/shard_map/ppermute | solution.py:243
  50.1 4.6 %collective-permute-done.5.refs_2_ = bf16[320,512]{1,0:T(8,128)(2,1)S(1)} collective-permute-done((bf16[320,512]{1,0:T(8,128)(2,1)S(1)}, bf16[320,512]{1,0:T(8,128)(2,1)S(1)}, u32[]{:S(2)}, u32[]{:S(2)}) %collective-permute-start.5) | collective-permute-done | bytes 327712 | tf_op jit(solution)/shard_map/ppermute | solution.py:243
  54.7 2.5 %collective-permute-start.7 = (bf16[320,512]{1,0:T(8,128)(2,1)S(1)}, bf16[320,512]{1,0:T(8,128)(2,1)}, u32[]{:S(2)}, u32[]{:S(2)}) collective-permute-start(bf16[320,512]{1,0:T(8,128)(2,1)S(1)} %collective-permute-done.5.refs_2_), channel_id=1, source_target_pairs={{0,2},{1,7},{2,4},{3,1},{4,6},{5,3},{6,0},{7,5},{8,10},{9,15},{10,... | collective-permute-start | bytes 983048 | tf_op jit(solution)/shard_map/ppermute | solution.py:243
  57.2 3.0 %collective-permute-start.6 = (bf16[320,512]{1,0:T(8,128)(2,1)S(1)}, bf16[320,512]{1,0:T(8,128)(2,1)}, u32[]{:S(2)}, u32[]{:S(2)}) collective-permute-start(bf16[320,512]{1,0:T(8,128)(2,1)S(1)} %collective-permute-done.4.refs_1_), channel_id=1, source_target_pairs={{0,2},{1,7},{2,4},{3,1},{4,6},{5,3},{6,0},{7,5},{8,10},{9,15},{10,... | collective-permute-start | bytes 983048 | tf_op jit(solution)/shard_map/ppermute | solution.py:243
  60.2 7.4 %collective-permute-start.11 = (bf16[320,512]{1,0:T(8,128)(2,1)S(1)}, bf16[320,512]{1,0:T(8,128)(2,1)}, u32[]{:S(2)}, u32[]{:S(2)}) collective-permute-start(bf16[320,512]{1,0:T(8,128)(2,1)S(1)} %get-tuple-element.8.refs_0_), channel_id=1, source_target_pairs={{0,8},{8,16},{16,24},{24,32},{32,40},{40,48},{48,56},{56,64},{64,7... | collective-permute-start | bytes 983048 | tf_op jit(solution)/shard_map/ppermute | solution.py:247
  67.6 1.9 %collective-permute-start.12 = (bf16[320,512]{1,0:T(8,128)(2,1)S(1)}, bf16[320,512]{1,0:T(8,128)(2,1)}, u32[]{:S(2)}, u32[]{:S(2)}) collective-permute-start(bf16[320,512]{1,0:T(8,128)(2,1)S(1)} %get-tuple-element.8.refs_0_), channel_id=1, source_target_pairs={{8,0},{16,8},{24,16},{32,24},{40,32},{48,40},{56,48},{64,56},{72,6... | collective-permute-start | bytes 983048 | tf_op jit(solution)/shard_map/ppermute | solution.py:247
  70.3 1.8 %collective-permute-done.11.refs_8_ = bf16[320,512]{1,0:T(8,128)(2,1)} collective-permute-done((bf16[320,512]{1,0:T(8,128)(2,1)S(1)}, bf16[320,512]{1,0:T(8,128)(2,1)}, u32[]{:S(2)}, u32[]{:S(2)}) %collective-permute-start.11) | collective-permute-done | bytes 327712 | tf_op jit(solution)/shard_map/ppermute | solution.py:247
  72.2 6.6 %collective-permute-done.12.refs_9_ = bf16[320,512]{1,0:T(8,128)(2,1)} collective-permute-done((bf16[320,512]{1,0:T(8,128)(2,1)S(1)}, bf16[320,512]{1,0:T(8,128)(2,1)}, u32[]{:S(2)}, u32[]{:S(2)}) %collective-permute-start.12) | collective-permute-done | bytes 327712 | tf_op jit(solution)/shard_map/ppermute | solution.py:247
  78.8 10.7 %processor.1 = bf16[320,512]{1,0:T(8,128)(2,1)} custom-call(s32[10]{0:T(128)S(1)} %broadcast_multiply_fusion.place, s32[2560]{0:T(1024)S(1)} %copy-done.17, s32[2560]{0:T(1024)S(1)} %copy-done.15, bf16[320,512]{1,0:T(8,128)(2,1)S(1)} %get-tuple-element.8.refs_0_, bf16[320,512]{1,0:T(8,128)(2,1)S(1)} %collective-permute-done.4.refs_1_, ...), custom_call_target="tpu_custom_call" | custom-call | tf_op jit(solution)/shard_map/processor/pallas_call | solution.py:183
  (61 shorter events, 1.0 us)
Async XLA Ops:
  1.5 1.5 %copy-start = (bf16[2048,474]{0,1:T(8,128)(2,1)S(1)}, bf16[2048,474]{0,1:T(8,128)(2,1)}, u32[]{:S(2)}) copy-start(bf16[2048,474]{0,1:T(8,128)(2,1)} %param.25) | copy-start | bytes 5824516
  3.0 1.0 %copy-start.2 = (bf16[512,512]{1,0:T(8,128)(2,1)S(1)}, bf16[512,512]{1,0:T(8,128)(2,1)}, u32[]{:S(2)}) copy-start(bf16[512,512]{1,0:T(8,128)(2,1)} %w_in2.1) | copy-start | bytes 1572868
  4.1 1.0 %copy-start.3 = (bf16[512,512]{1,0:T(8,128)(2,1)S(1)}, bf16[512,512]{1,0:T(8,128)(2,1)}, u32[]{:S(2)}) copy-start(bf16[512,512]{1,0:T(8,128)(2,1)} %w_g2m.1) | copy-start | bytes 1572868
  5.1 1.0 %copy-start.12 = (bf16[474,512]{1,0:T(8,128)(2,1)S(1)}, bf16[474,512]{1,0:T(8,128)(2,1)}, u32[]{:S(2)}) copy-start(bf16[474,512]{1,0:T(8,128)(2,1)} %w_in1.1) | copy-start | bytes 1456132
  22.9 4.0 %copy-start.24 = (bf16[4096,512]{1,0:T(8,128)(2,1)S(1)}, bf16[4096,512]{1,0:T(8,128)(2,1)}, u32[]{:S(2)}) copy-start(bf16[4096,512]{1,0:T(8,128)(2,1)} %messages.1) | copy-start | bytes 12582916
  26.8 6.2 %collective-permute-start.1 = (bf16[320,512]{1,0:T(8,128)(2,1)S(1)}, bf16[320,512]{1,0:T(8,128)(2,1)S(1)}, u32[]{:S(2)}, u32[]{:S(2)}) collective-permute-start(bf16[320,512]{1,0:T(8,128)(2,1)S(1)} %fusion.21), channel_id=1, source_target_pairs={{0,1},{1,0},{2,3},{3,2},{4,5},{5,4},{6,7},{7,6},{8,9},{9,8},{10,11... | collective-permute-start | bytes 983048 | tf_op jit(solution)/shard_map/ppermute | solution.py:239
  28.4 11.6 %collective-permute-start = (bf16[320,512]{1,0:T(8,128)(2,1)S(1)}, bf16[320,512]{1,0:T(8,128)(2,1)S(1)}, u32[]{:S(2)}, u32[]{:S(2)}) collective-permute-start(bf16[320,512]{1,0:T(8,128)(2,1)S(1)} %fusion.18), channel_id=1, source_target_pairs={{0,1},{1,0},{2,3},{3,2},{4,5},{5,4},{6,7},{7,6},{8,9},{9,8},{10,11... | collective-permute-start | bytes 983048 | tf_op jit(solution)/shard_map/ppermute | solution.py:239
  30.5 9.5 %collective-permute-start.3 = (bf16[320,512]{1,0:T(8,128)(2,1)S(1)}, bf16[320,512]{1,0:T(8,128)(2,1)S(1)}, u32[]{:S(2)}, u32[]{:S(2)}) collective-permute-start(bf16[320,512]{1,0:T(8,128)(2,1)S(1)} %fusion.24), channel_id=1, source_target_pairs={{1,3},{2,0},{3,5},{4,2},{5,7},{6,4},{7,9},{8,6},{9,11},{10,8},{11,... | collective-permute-start | bytes 983048 | tf_op jit(solution)/shard_map/ppermute | solution.py:239
  34.6 9.2 %copy-start.4 = (bf16[512,512]{1,0:T(8,128)(2,1)S(1)}, bf16[512,512]{1,0:T(8,128)(2,1)}, u32[]{:S(2)}) copy-start(bf16[512,512]{1,0:T(8,128)(2,1)} %w_enc1.1) | copy-start | bytes 1572868
  34.6 9.2 %copy-start.5 = (bf16[512,512]{1,0:T(8,128)(2,1)S(1)}, bf16[512,512]{1,0:T(8,128)(2,1)}, u32[]{:S(2)}) copy-start(bf16[512,512]{1,0:T(8,128)(2,1)} %w_enc2.1) | copy-start | bytes 1572868
  34.6 9.2 %copy-start.6 = (bf16[512,512]{1,0:T(8,128)(2,1)S(1)}, bf16[512,512]{1,0:T(8,128)(2,1)}, u32[]{:S(2)}) copy-start(bf16[512,512]{1,0:T(8,128)(2,1)} %w_snd.1) | copy-start | bytes 1572868
  34.6 9.2 %copy-start.7 = (bf16[512,512]{1,0:T(8,128)(2,1)S(1)}, bf16[512,512]{1,0:T(8,128)(2,1)}, u32[]{:S(2)}) copy-start(bf16[512,512]{1,0:T(8,128)(2,1)} %w_rcv.1) | copy-start | bytes 1572868
  34.6 9.2 %copy-start.13 = (bf16[320,512]{1,0:T(8,128)(2,1)S(1)}, bf16[320,512]{1,0:T(8,128)(2,1)}, u32[]{:S(2)}) copy-start(bf16[320,512]{1,0:T(8,128)(2,1)} %emb.1) | copy-start | bytes 983044
  34.6 9.2 %copy-start.19 = (f32[512]{0:T(512)S(1)}, f32[512]{0:T(512)}, u32[]{:S(2)}) copy-start(f32[512]{0:T(512)} %param.40) | copy-start | bytes 6148
  34.6 9.2 %copy-start.20 = (f32[512]{0:T(512)S(1)}, f32[512]{0:T(512)}, u32[]{:S(2)}) copy-start(f32[512]{0:T(512)} %param.44) | copy-start | bytes 6148
  34.6 35.6 %copy-start.15 = (s32[2560]{0:T(1024)S(1)}, s32[2560]{0:T(1024)}, u32[]{:S(2)}) copy-start(s32[2560]{0:T(1024)} %recv.1) | copy-start | bytes 30724
  34.7 9.1 %collective-permute-start.2 = (bf16[320,512]{1,0:T(8,128)(2,1)S(1)}, bf16[320,512]{1,0:T(8,128)(2,1)S(1)}, u32[]{:S(2)}, u32[]{:S(2)}) collective-permute-start(bf16[320,512]{1,0:T(8,128)(2,1)S(1)} %add_convert_fusion), channel_id=1, source_target_pairs={{0,2},{2,4},{3,1},{4,6},{5,3},{6,8},{7,5},{8,10},{9,7},{10,12},{11... | collective-permute-start | bytes 983048 | tf_op jit(solution)/shard_map/ppermute | solution.py:239
  39.9 38.8 %copy-start.8 = (bf16[512,512]{1,0:T(8,128)(2,1)S(1)}, bf16[512,512]{1,0:T(8,128)(2,1)}, u32[]{:S(2)}) copy-start(bf16[512,512]{1,0:T(8,128)(2,1)} %refs_13_.1) | copy-start | bytes 1572868
  40.0 38.8 %copy-start.9 = (bf16[512,512]{1,0:T(8,128)(2,1)S(1)}, bf16[512,512]{1,0:T(8,128)(2,1)}, u32[]{:S(2)}) copy-start(bf16[512,512]{1,0:T(8,128)(2,1)} %refs_14_.1) | copy-start | bytes 1572868
  40.0 38.8 %copy-start.10 = (bf16[512,512]{1,0:T(8,128)(2,1)S(1)}, bf16[512,512]{1,0:T(8,128)(2,1)}, u32[]{:S(2)}) copy-start(bf16[512,512]{1,0:T(8,128)(2,1)} %refs_15_.1) | copy-start | bytes 1572868
  40.0 38.8 %copy-start.11 = (bf16[512,512]{1,0:T(8,128)(2,1)S(1)}, bf16[512,512]{1,0:T(8,128)(2,1)}, u32[]{:S(2)}) copy-start(bf16[512,512]{1,0:T(8,128)(2,1)} %refs_17_.1) | copy-start | bytes 1572868
  40.0 38.8 %copy-start.17 = (s32[2560]{0:T(1024)S(1)}, s32[2560]{0:T(1024)}, u32[]{:S(2)}) copy-start(s32[2560]{0:T(1024)} %send.1) | copy-start | bytes 30724
  40.0 38.8 %copy-start.21 = (f32[512]{0:T(512)S(1)}, f32[512]{0:T(512)}, u32[]{:S(2)}) copy-start(f32[512]{0:T(512)} %param.48) | copy-start | bytes 6148
  45.7 9.0 %collective-permute-start.5 = (bf16[320,512]{1,0:T(8,128)(2,1)S(1)}, bf16[320,512]{1,0:T(8,128)(2,1)S(1)}, u32[]{:S(2)}, u32[]{:S(2)}) collective-permute-start(bf16[320,512]{1,0:T(8,128)(2,1)S(1)} %get-tuple-element.8.refs_0_), channel_id=1, source_target_pairs={{0,2},{1,7},{2,4},{3,1},{4,6},{5,3},{6,0},{7,5},{8,10},{9,15},{10,... | collective-permute-start | bytes 983048 | tf_op jit(solution)/shard_map/ppermute | solution.py:243
  50.1 7.1 %collective-permute-start.4 = (bf16[320,512]{1,0:T(8,128)(2,1)S(1)}, bf16[320,512]{1,0:T(8,128)(2,1)S(1)}, u32[]{:S(2)}, u32[]{:S(2)}) collective-permute-start(bf16[320,512]{1,0:T(8,128)(2,1)S(1)} %get-tuple-element.8.refs_0_), channel_id=1, source_target_pairs={{0,1},{1,0},{2,3},{3,2},{4,5},{5,4},{6,7},{7,6},{8,9},{9,8},{10,11... | collective-permute-start | bytes 983048 | tf_op jit(solution)/shard_map/ppermute | solution.py:239
  54.7 14.9 %collective-permute-start.7 = (bf16[320,512]{1,0:T(8,128)(2,1)S(1)}, bf16[320,512]{1,0:T(8,128)(2,1)}, u32[]{:S(2)}, u32[]{:S(2)}) collective-permute-start(bf16[320,512]{1,0:T(8,128)(2,1)S(1)} %collective-permute-done.5.refs_2_), channel_id=1, source_target_pairs={{0,2},{1,7},{2,4},{3,1},{4,6},{5,3},{6,0},{7,5},{8,10},{9,15},{10,... | collective-permute-start | bytes 983048 | tf_op jit(solution)/shard_map/ppermute | solution.py:243
  57.2 12.9 %collective-permute-start.6 = (bf16[320,512]{1,0:T(8,128)(2,1)S(1)}, bf16[320,512]{1,0:T(8,128)(2,1)}, u32[]{:S(2)}, u32[]{:S(2)}) collective-permute-start(bf16[320,512]{1,0:T(8,128)(2,1)S(1)} %collective-permute-done.4.refs_1_), channel_id=1, source_target_pairs={{0,2},{1,7},{2,4},{3,1},{4,6},{5,3},{6,0},{7,5},{8,10},{9,15},{10,... | collective-permute-start | bytes 983048 | tf_op jit(solution)/shard_map/ppermute | solution.py:243
  60.2 12.0 %collective-permute-start.11 = (bf16[320,512]{1,0:T(8,128)(2,1)S(1)}, bf16[320,512]{1,0:T(8,128)(2,1)}, u32[]{:S(2)}, u32[]{:S(2)}) collective-permute-start(bf16[320,512]{1,0:T(8,128)(2,1)S(1)} %get-tuple-element.8.refs_0_), channel_id=1, source_target_pairs={{0,8},{8,16},{16,24},{24,32},{32,40},{40,48},{48,56},{56,64},{64,7... | collective-permute-start | bytes 983048 | tf_op jit(solution)/shard_map/ppermute | solution.py:247
  67.6 11.2 %collective-permute-start.12 = (bf16[320,512]{1,0:T(8,128)(2,1)S(1)}, bf16[320,512]{1,0:T(8,128)(2,1)}, u32[]{:S(2)}, u32[]{:S(2)}) collective-permute-start(bf16[320,512]{1,0:T(8,128)(2,1)S(1)} %get-tuple-element.8.refs_0_), channel_id=1, source_target_pairs={{8,0},{16,8},{24,16},{32,24},{40,32},{48,40},{56,48},{64,56},{72,6... | collective-permute-start | bytes 983048 | tf_op jit(solution)/shard_map/ppermute | solution.py:247
  69.5 9.3 %collective-permute-start.8 = (bf16[320,512]{1,0:T(8,128)(2,1)S(1)}, bf16[320,512]{1,0:T(8,128)(2,1)}, u32[]{:S(2)}, u32[]{:S(2)}) collective-permute-start(bf16[320,512]{1,0:T(8,128)(2,1)S(1)} %collective-permute-done.5.refs_2_), channel_id=1, source_target_pairs={{0,1},{1,0},{2,3},{3,2},{4,5},{5,4},{6,7},{7,6},{8,9},{9,8},{10,11... | collective-permute-start | bytes 983048 | tf_op jit(solution)/shard_map/ppermute | solution.py:239
  69.6 9.2 %collective-permute-start.10 = (bf16[320,512]{1,0:T(8,128)(2,1)}, bf16[320,512]{1,0:T(8,128)(2,1)}, u32[]{:S(2)}, u32[]{:S(2)}) collective-permute-start(bf16[320,512]{1,0:T(8,128)(2,1)} %collective-permute-done.7.refs_4_), channel_id=1, source_target_pairs={{0,1},{1,0},{2,3},{3,2},{4,5},{5,4},{6,7},{7,6},{8,9},{9,8},{10,11... | collective-permute-start | bytes 983048 | tf_op jit(solution)/shard_map/ppermute | solution.py:239
  70.1 8.7 %collective-permute-start.9 = (bf16[320,512]{1,0:T(8,128)(2,1)}, bf16[320,512]{1,0:T(8,128)(2,1)}, u32[]{:S(2)}, u32[]{:S(2)}) collective-permute-start(bf16[320,512]{1,0:T(8,128)(2,1)} %collective-permute-done.6.refs_3_), channel_id=1, source_target_pairs={{0,1},{1,0},{2,3},{3,2},{4,5},{5,4},{6,7},{7,6},{8,9},{9,8},{10,11... | collective-permute-start | bytes 983048 | tf_op jit(solution)/shard_map/ppermute | solution.py:239
  (6 other events, 4.5 us)

commit v3 on v2

v3 whole, which is shorter than its diff:
```python
import jax
import jax.numpy as jnp
from jax import lax
from jax.experimental import pallas as pl
from jax.experimental.pallas import tpu as pltpu
from jax.sharding import PartitionSpec as P

F32 = jnp.float32
BF16 = jnp.bfloat16
LANES = 128
EDGE_BLOCK = 256
BOTH = ("grp", "inner")
MESSAGE_VMEM = 60 * 2**20


def silu(v):
    half = v * 0.5
    return half + half * jnp.tanh(half)


def split3(v):
    high = v.astype(BF16).astype(F32)
    rest = v - high
    mid = rest.astype(BF16).astype(F32)
    return high, mid, (rest - mid).astype(BF16).astype(F32)


def dot(a, b):
    return jnp.dot(a, b, preferred_element_type=F32)


def dot_first(a, b):
    return lax.dot_general(a, b, (((0,), (0,)), ((), ())), preferred_element_type=F32)


def one_hot(ids, rows):
    numbers = lax.broadcasted_iota(jnp.int32, (rows, ids.shape[1]), 0)
    return jnp.where(numbers == ids, 1.0, 0.0).astype(BF16)


def put_rows(table, first, rows):
    parts = rows.shape[1] // LANES
    for j in range(parts):
        table[pl.ds(first * parts + j, rows.shape[0], stride=parts), :] = rows[
            :, j * LANES : (j + 1) * LANES
        ]


def message_kernel(
    scalars, src_hbm, grid_hbm, w_in1_hbm, b_in_hbm, w_in2_hbm, w_g2m_hbm, geom_hbm, w_geo_hbm, b_g2m_hbm, dst_hbm, node_hbm,
    back2, back1, own, on1, on2,
    src, grid_in, w_in1, b_in, w_in2, w_g2m, geom, w_geo, b_g2m, dst, node, table, buf_a, buf_b, w8, g8, w48, w_both, msg_a, msg_b, sums, sems,
):
    nodes, edges = grid_in.shape[1], src.shape[0]
    bands, rows = 5, own.shape[0]
    chunk = 512
    chunks = nodes // chunk
    here = [
        (w_in1_hbm, w_in1), (b_in_hbm, b_in), (w_in2_hbm, w_in2), (w_g2m_hbm, w_g2m), (src_hbm, src),
        (geom_hbm, geom), (w_geo_hbm, w_geo), (b_g2m_hbm, b_g2m), (dst_hbm, dst), (node_hbm, node),
    ]
    copies = [pltpu.make_async_copy(a, b, sems.at[i]) for i, (a, b) in enumerate(here)]
    grids = []
    for k in range(chunks):
        part = pl.ds(k * chunk, chunk)
        grids.append(
            pltpu.make_async_copy(grid_hbm.at[:, part], grid_in.at[:, part], sems.at[len(here) + k])
        )
    order = [copies[2], copies[3], copies[0], copies[1], grids[0], grids[1]] + copies[4:] + grids[2:]
    for copy in order:
        copy.start()
    copies[2].wait()
    copies[3].wait()
    w_both[...] = dot(w_in2[...], w_g2m[...]).astype(BF16)
    copies[0].wait()
    copies[1].wait()
    for k in range(chunks):
        grids[k].wait()
        hid = dot_first(grid_in[:, k * chunk : (k + 1) * chunk], w_in1[...])
        hid = silu(hid + b_in[...]).astype(BF16)
        put_rows(table, k * chunk, dot(hid, w_both[...]))

    for copy in copies[4:]:
        copy.wait()
    node[...] = ((dst[...] - scalars[0]) * scalars[1] + 2) * scalars[2] + node[...]
    w8[...] = jnp.zeros_like(w8)
    w8[0:4, :] = w_geo[...]
    w8[4:5, :] = b_g2m[...]
    high, mid, low = split3(w8[...])
    w48[...] = jnp.concatenate([high, high, high, mid, mid, low], axis=0).astype(BF16)
    g8[...] = jnp.zeros_like(g8)
    g8[0:4, :] = geom[...]
    g8[4:5, :] = jnp.ones((1, g8.shape[1]), F32)
    sums[...] = jnp.zeros_like(sums)
    msg_b[...] = jnp.zeros_like(msg_b)

    def gather(base, buf):
        for e in range(EDGE_BLOCK):
            row = pl.multiple_of(src[base + e] * 4, 4)
            buf[4 * e : 4 * e + 4, :] = table[pl.ds(row, 4), :]

    def emit(base, half, buf):
        base = pl.multiple_of(base, EDGE_BLOCK)
        high, mid, low = split3(g8[:, pl.ds(base, EDGE_BLOCK)])
        g48 = jnp.concatenate([high, mid, low, high, mid, high], axis=0).astype(BF16)
        geo = dot_first(g48, w48[...])
        for j in range(4):
            lanes = slice(j * LANES, (j + 1) * LANES)
            v = buf[pl.ds(j, EDGE_BLOCK, stride=4), :] + geo[:, lanes]
            (msg_a, msg_b)[half][:, lanes] = silu(v).astype(BF16)

    def scatter(base, half):
        base = pl.multiple_of(jnp.maximum(base, 0), EDGE_BLOCK)
        select = one_hot(node[:, pl.ds(base, EDGE_BLOCK)], bands * rows)
        sums[...] += dot(select, (msg_a, msg_b)[half][...])

    blocks = edges // EDGE_BLOCK
    gather(0, buf_a)

    def step(t, carry):
        base = pl.multiple_of(t * (2 * EDGE_BLOCK), 2 * EDGE_BLOCK)
        gather(base + EDGE_BLOCK, buf_b)
        emit(base, 0, buf_a)
        scatter(base - EDGE_BLOCK, 1)
        gather(jnp.minimum(base + 2 * EDGE_BLOCK, (blocks - 1) * EDGE_BLOCK), buf_a)
        emit(base + EDGE_BLOCK, 1, buf_b)
        scatter(base, 0)
        return carry

    lax.fori_loop(0, blocks // 2, step, 0)
    scatter(edges - EDGE_BLOCK, 1)
    for which, out in enumerate((back2, back1, own, on1, on2)):
        out[...] = sums[which * rows : (which + 1) * rows, :].astype(out.dtype)


def band_sums(scalars, rows, *arrays):
    g2m_src, grid_in, w_in1 = arrays[:3]
    edges, nodes, width = g2m_src.shape[0], grid_in.shape[1], w_in1.shape[1]
    vmem = pl.BlockSpec(memory_space=pltpu.VMEM)
    smem = pl.BlockSpec(memory_space=pltpu.SMEM)
    hbm = pl.BlockSpec(memory_space=pltpu.HBM)
    return pl.pallas_call(
        message_kernel,
        out_shape=[jax.ShapeDtypeStruct((rows, width), dtype) for dtype in (BF16, BF16, F32, BF16, F32)],
        in_specs=[smem] + [hbm] * len(arrays),
        out_specs=[vmem] * 5,
        scratch_shapes=[pltpu.SMEM((edges,), jnp.int32)]
        + [pltpu.VMEM(a.shape, a.dtype) for a in arrays[1:]]
        + [
            pltpu.VMEM((4 * nodes, LANES), F32),
            pltpu.VMEM((4 * EDGE_BLOCK, LANES), F32),
            pltpu.VMEM((4 * EDGE_BLOCK, LANES), F32),
            pltpu.VMEM((8, width), F32),
            pltpu.VMEM((8, edges), F32),
            pltpu.VMEM((48, width), BF16),
            pltpu.VMEM((width, width), BF16),
            pltpu.VMEM((EDGE_BLOCK, width), BF16),
            pltpu.VMEM((EDGE_BLOCK, width), BF16),
            pltpu.VMEM((5 * rows, width), F32),
            pltpu.SemaphoreType.DMA((len(arrays) + 3,)),
        ],
        compiler_params=pltpu.CompilerParams(vmem_limit_bytes=MESSAGE_VMEM),
        name="band_sums",
    )(scalars, *arrays)


def encoder_kernel(own, near, one, two, emb, w_enc1, b_enc, w_enc2, w_snd, lat, snd):
    total = own[...] + near[...].astype(F32) + one[...].astype(F32) + two[...].astype(F32)
    enc = silu(dot(total.astype(BF16), w_enc1[...]) + b_enc[...]).astype(BF16)
    mesh_lat = (emb[...].astype(F32) + dot(enc, w_enc2[...])).astype(BF16)
    lat[...] = mesh_lat
    snd[...] = dot(mesh_lat, w_snd[...]).astype(BF16)


def encoder(own, near, one, two, emb, w_enc1, b_enc, w_enc2, w_snd):
    vmem = pl.BlockSpec(memory_space=pltpu.VMEM)
    rows, width = emb.shape
    return pl.pallas_call(
        encoder_kernel,
        out_shape=[jax.ShapeDtypeStruct((rows, width), BF16)] * 2,
        in_specs=[vmem] * 9,
        out_specs=[vmem] * 2,
        compiler_params=pltpu.CompilerParams(vmem_limit_bytes=16 * 2**20),
        name="encoder",
    )(own, near, one, two, emb, w_enc1, b_enc.reshape(1, -1), w_enc2, w_snd)


def receiver_kernel(recv, lat, w_rcv, w_edge, w_p1, w_p2, b_p, recv_rows, w_ep, lat_p2):
    receivers = dot(lat[...], w_rcv[...]).astype(BF16)
    for k in range(recv_rows.shape[0] // 512):
        part = slice(k * 512, (k + 1) * 512)
        select = one_hot(recv[:, part], lat.shape[0])
        recv_rows[part, :] = dot_first(select, receivers).astype(BF16)
    w_ep[...] = dot(w_edge[...], w_p1[...]).astype(BF16)
    lat_p2[...] = dot(lat[...], w_p2[...]) + b_p[...]


def receiver_side(recv, lat, w_rcv, w_edge, w_p1, w_p2, b_p):
    vmem = pl.BlockSpec(memory_space=pltpu.VMEM)
    rows, width = lat.shape
    edges = recv.shape[0]
    return pl.pallas_call(
        receiver_kernel,
        out_shape=[
            jax.ShapeDtypeStruct((edges, width), BF16),
            jax.ShapeDtypeStruct((width, width), BF16),
            jax.ShapeDtypeStruct((rows, width), F32),
        ],
        in_specs=[vmem] * 7,
        out_specs=[vmem] * 3,
        compiler_params=pltpu.CompilerParams(vmem_limit_bytes=16 * 2**20),
        cost_estimate=pl.CostEstimate(flops=2 * 10**9, bytes_accessed=6 * 10**6, transcendentals=0),
        name="receiver_side",
    )(recv.reshape(1, -1), lat, w_rcv, w_edge, w_p1, w_p2, b_p.reshape(1, -1))


def processor_kernel(place, send, recv, b_edge, recv_rows, lat, lat_p2, w_ep, w_p3, *refs):
    shards = refs[:10]
    out, table, buf_a, buf_b, hid, agg = refs[10:]
    rows = lat.shape[0]
    for k in range(10):
        put_rows(table, place[k], shards[k][...].astype(F32))
    agg[...] = jnp.zeros_like(agg)

    def gather(base, buf):
        for e in range(EDGE_BLOCK):
            row = pl.multiple_of(send[base + e] * 4, 4)
            buf[4 * e : 4 * e + 4, :] = table[pl.ds(row, 4), :]

    def emit(base, half, buf):
        base = pl.multiple_of(base, EDGE_BLOCK)
        for j in range(4):
            lanes = slice(j * LANES, (j + 1) * LANES)
            v = buf[pl.ds(j, EDGE_BLOCK, stride=4), :] + b_edge[:, lanes]
            v = v + recv_rows[pl.ds(base, EDGE_BLOCK), lanes].astype(F32)
            hid[half * EDGE_BLOCK : (half + 1) * EDGE_BLOCK, lanes] = silu(v).astype(BF16)

    blocks = send.shape[0] // EDGE_BLOCK
    gather(0, buf_a)

    def step(t, carry):
        base = pl.multiple_of(t * (2 * EDGE_BLOCK), 2 * EDGE_BLOCK)
        gather(base + EDGE_BLOCK, buf_b)
        emit(base, 0, buf_a)
        gather(jnp.minimum(base + 2 * EDGE_BLOCK, (blocks - 1) * EDGE_BLOCK), buf_a)
        emit(base + EDGE_BLOCK, 1, buf_b)
        agg[...] += dot(one_hot(recv[:, pl.ds(base, 2 * EDGE_BLOCK)], rows), hid[...])
        return carry

    lax.fori_loop(0, blocks // 2, step, 0)
    node = silu(dot(agg[...].astype(BF16), w_ep[...]) + lat_p2[...]).astype(BF16)
    out[...] = (lat[...].astype(F32) + dot(node, w_p3[...])).astype(BF16)


def processor(place, send, recv, b_edge, recv_rows, lat, lat_p2, w_ep, w_p3, shards):
    vmem = pl.BlockSpec(memory_space=pltpu.VMEM)
    smem = pl.BlockSpec(memory_space=pltpu.SMEM)
    rows, width = lat.shape
    return pl.pallas_call(
        processor_kernel,
        out_shape=jax.ShapeDtypeStruct((rows, width), BF16),
        in_specs=[smem] * 2 + [vmem] * (7 + len(shards)),
        out_specs=vmem,
        scratch_shapes=[
            pltpu.VMEM((4 * 10 * rows, LANES), F32),
            pltpu.VMEM((4 * EDGE_BLOCK, LANES), F32),
            pltpu.VMEM((4 * EDGE_BLOCK, LANES), F32),
            pltpu.VMEM((2 * EDGE_BLOCK, width), BF16),
            pltpu.VMEM((rows, width), F32),
        ],
        compiler_params=pltpu.CompilerParams(vmem_limit_bytes=24 * 2**20),
        name="processor",
    )(
        place, send, recv.reshape(1, -1), b_edge.reshape(1, -1), recv_rows, lat, lat_p2, w_ep, w_p3, *shards
    )


def on_device(
    grid_in,
    g2m_geom,
    g2m_src,
    g2m_dst,
    g2m_node,
    mesh_emb,
    mesh_send,
    mesh_recv,
    w_in1,
    b_in,
    w_in2,
    w_g2m,
    w_geo,
    b_g2m,
    w_enc1,
    b_enc,
    w_enc2,
    w_snd,
    w_rcv,
    b_edge,
    w_edge,
    w_p1,
    w_p2,
    b_p,
    w_p3,
):
    groups, places = lax.axis_size("grp"), lax.axis_size("inner")
    bands = groups * places
    nodes_here = mesh_emb.shape[0]
    band = lax.axis_index(BOTH)
    place = lax.axis_index("inner")
    core = place % 2

    def by_parity(even, odd):
        pairs = [(b, b + (odd if b % 2 else even)) for b in range(bands)]
        pairs = [pair for pair in pairs if 0 <= pair[1] < bands]
        return lambda value: lax.ppermute(value, BOTH, pairs)

    def onward(value):
        pairs = [(i, (i + (-2 if i % 2 else 2)) % places) for i in range(places)]
        return lax.ppermute(value, "inner", pairs)

    def across(value):
        return lax.ppermute(value, "inner", [(i, (i + 4) % places) for i in range(places)])

    def along_groups(value, by):
        pairs = [(i, i + by) for i in range(groups) if 0 <= i + by < groups]
        return lax.ppermute(value, "grp", pairs)

    other_core = by_parity(1, -1)

    turn = 1 - 2 * core
    scalars = jnp.stack([band, turn, jnp.int32(nodes_here)])
    back2, back1, own, on1, on2 = band_sums(
        scalars,
        nodes_here,
        g2m_src,
        grid_in.T,
        w_in1,
        b_in.reshape(1, -1),
        w_in2,
        w_g2m,
        g2m_geom,
        w_geo,
        b_g2m.reshape(1, -1),
        g2m_dst.reshape(1, -1),
        g2m_node.reshape(1, -1),
    )
    crossing = other_core(back1)
    two = by_parity(-2, 2)(back2)
    one = by_parity(2, -2)((on2 + crossing.astype(F32)).astype(BF16))
    near = other_core(on1)
    mesh_lat, senders = encoder(own, near, one, two, mesh_emb, w_enc1, b_enc, w_enc2, w_snd)

    partner = other_core(senders)
    next_a = onward(senders)
    far = across(senders)
    next_b = onward(partner)
    low = along_groups(senders, 1)
    high = along_groups(senders, -1)
    shards = [senders, partner, next_a, next_b, far]
    shards = shards + [other_core(shard) for shard in shards[2:]] + [low, high]
    recv_rows, w_ep, lat_p2 = receiver_side(mesh_recv, mesh_lat, w_rcv, w_edge, w_p1, w_p2, b_p)
    before, after, opposite = [(place + by) % places for by in (-2 * turn, 2 * turn, 4)]
    where = [place, place + turn, before, before + turn, opposite]
    where = where + [after + turn, after, opposite + turn, places, places + 1]
    starts = jnp.stack([jnp.asarray(p, jnp.int32) for p in where]) * nodes_here
    return processor(
        starts, mesh_send, mesh_recv, b_edge, recv_rows, mesh_lat, lat_p2, w_ep, w_p3, shards
    )


def solution(mesh):
    split = P(BOTH)
    rows = P(BOTH, None)
    return jax.shard_map(
        on_device,
        mesh=mesh,
        in_specs=(rows, P(None, BOTH), split, rows, split, rows, split, split) + (P(),) * 17,
        out_specs=rows,
        check_vma=False,
    )
```

time: 90.2 us -> 77.5 us (0.86)
  the two profiles are of different devices: /device:TPU:92 before, /device:TPU:96 now
where the time goes in v3:
time: 77.5 us; the launch traced here: 76.4 us
  Pallas kernels  30.6 us (39%)
  waiting for transfers between devices  21.8 us (28%)
  starting transfers between devices  17.5 us (23%)
  local copies, waits for them, and re-layouts  4.35 us (6%)
  other arithmetic  1.85 us (2%)
    pallas_call x1, Pallas kernels, band_sums(): pl.pallas_call(message_kernel, out_shape=[jax.ShapeDtypeStruct((rows, wid...  19.9 us
    ppermute x8, waiting for transfers between devices, by_parity(): return lambda value: lax.ppermute(value, BOTH, pairs)  12.7 us
    ppermute x8, starting transfers between devices, by_parity(): return lambda value: lax.ppermute(value, BOTH, pairs)  9.57 us
    pallas_call x1, Pallas kernels, processor(): pl.pallas_call(processor_kernel, out_shape=jax.ShapeDtypeStruct((rows, wi...  7.52 us
    ppermute x2, waiting for transfers between devices, onward(): return lax.ppermute(value, 'inner', pairs)  6.91 us
    ppermute x2, starting transfers between devices, along_groups(): return lax.ppermute(value, 'grp', pairs)  5.84 us
    unnamed x30, local copies, waits for them, and re-layouts  4.25 us
    pallas_call x1, Pallas kernels, receiver_side(): pl.pallas_call(receiver_kernel, out_shape=[jax.ShapeDtypeStruct((edges, w...  2.25 us
  transfers between devices with their start and end apart: 13, of which 6 were waited for; matrix products, arithmetic and copies ran while one was open for 2% of the time, Pallas kernels for 3%

profile of v3, /device:TPU:96, one launch (start us, length us, event | category | flops | bytes accessed | tf_op | source)
XLA Modules:
  0.0 76.4 jit_solution(15254880334796825503)
XLA Ops:
  0.0 0.7 pad_add_fusion.scalars
  0.7 19.9 %band_sums.1 = (bf16[320,512]{1,0:T(8,128)(2,1)}, bf16[320,512]{1,0:T(8,128)(2,1)}, f32[320,512]{1,0:T(8,128)}, bf16[320,512]{1,0:T(8,128)(2,1)}, f32[320,512]{1,0:T(8,128)}) custom-call(s32[3]{0:T(128)} %pad_add_fusion.scalars, s32[4096]{0:T(1024)} %src_hbm.1, bf16[474,2048]{1,0:T(8,128)(2,1)} %bitcast.21, bf16[474,512]{1,0:T(8,128)(2,1)} %w_in1_hbm.1, ...), custom_call_target="tpu_custom_call" | custom-call | tf_op jit(solution)/shard_map/band_sums/pallas_call | solution.py:142
  20.7 0.0 copy-start.14
  20.7 0.0 copy-start.9
  20.7 0.0 copy-start.13
  20.7 0.1 collective-permute-start.1
  20.8 0.5 collective-permute-start
  21.3 7.0 %collective-permute-start.3 = (bf16[320,512]{1,0:T(8,128)(2,1)}, bf16[320,512]{1,0:T(8,128)(2,1)S(1)}, u32[]{:S(2)}, u32[]{:S(2)}) collective-permute-start(bf16[320,512]{1,0:T(8,128)(2,1)} %get-tuple-element.19), channel_id=1, source_target_pairs={{1,3},{2,0},{3,5},{4,2},{5,7},{6,4},{7,9},{8,6},{9,11},{10,8},{11,... | collective-permute-start | bytes 983048 | tf_op jit(solution)/shard_map/ppermute | solution.py:315
  28.3 1.2 %add_convert_fusion = bf16[320,512]{1,0:T(8,128)(2,1)S(1)} fusion(f32[320,512]{1,0:T(8,128)} %get-tuple-element.17, bf16[320,512]{1,0:T(8,128)(2,1)S(1)} %collective-permute-done.1), kind=kLoop, calls=%fused_computation | loop fusion | flops 491520 | bytes 1310720 | tf_op jit(solution)/shard_map/convert_element_type | solution.py:349
  29.5 1.9 %collective-permute-start.2 = (bf16[320,512]{1,0:T(8,128)(2,1)S(1)}, bf16[320,512]{1,0:T(8,128)(2,1)S(1)}, u32[]{:S(2)}, u32[]{:S(2)}) collective-permute-start(bf16[320,512]{1,0:T(8,128)(2,1)S(1)} %add_convert_fusion), channel_id=1, source_target_pairs={{0,2},{2,4},{3,1},{4,6},{5,3},{6,8},{7,5},{8,10},{9,7},{10,12},{11... | collective-permute-start | bytes 983048 | tf_op jit(solution)/shard_map/ppermute | solution.py:315
  31.4 2.3 %collective-permute-done.3.two = bf16[320,512]{1,0:T(8,128)(2,1)S(1)} collective-permute-done((bf16[320,512]{1,0:T(8,128)(2,1)}, bf16[320,512]{1,0:T(8,128)(2,1)S(1)}, u32[]{:S(2)}, u32[]{:S(2)}) %collective-permute-start.3) | collective-permute-done | bytes 327712 | tf_op jit(solution)/shard_map/ppermute | solution.py:315
  33.7 9.0 %collective-permute-done.2.one = bf16[320,512]{1,0:T(8,128)(2,1)S(1)} collective-permute-done((bf16[320,512]{1,0:T(8,128)(2,1)S(1)}, bf16[320,512]{1,0:T(8,128)(2,1)S(1)}, u32[]{:S(2)}, u32[]{:S(2)}) %collective-permute-start.2) | collective-permute-done | bytes 327712 | tf_op jit(solution)/shard_map/ppermute | solution.py:315
  42.7 1.1 %copy-done = f32[320,512]{1,0:T(8,128)S(1)} copy-done((f32[320,512]{1,0:T(8,128)S(1)}, f32[320,512]{1,0:T(8,128)}, u32[]{:S(2)}) %copy-start) | copy-done | bytes 655384
  43.8 0.9 %encoder.1 = (bf16[320,512]{1,0:T(8,128)(2,1)S(1)}, bf16[320,512]{1,0:T(8,128)(2,1)S(1)}) custom-call(f32[320,512]{1,0:T(8,128)S(1)} %copy-done, bf16[320,512]{1,0:T(8,128)(2,1)S(1)} %collective-permute-done.near, bf16[320,512]{1,0:T(8,128)(2,1)S(1)} %collective-permute-done.2.one, bf16[320,512]{1,0:T(8,128)(2,1)S(1)} %collective-permute-done.3.two, ...), custom_call_target="tpu_custom_call" | custom-call | tf_op jit(solution)/shard_map/encoder/pallas_call | solution.py:178
  44.6 0.1 collective-permute-start.4
  44.7 0.1 collective-permute-start.7
  44.8 0.1 collective-permute-start.5
  44.9 1.4 %collective-permute-done.4.refs_1_ = bf16[320,512]{1,0:T(8,128)(2,1)S(1)} collective-permute-done((bf16[320,512]{1,0:T(8,128)(2,1)S(1)}, bf16[320,512]{1,0:T(8,128)(2,1)S(1)}, u32[]{:S(2)}, u32[]{:S(2)}) %collective-permute-start.4) | collective-permute-done | bytes 327712 | tf_op jit(solution)/shard_map/ppermute | solution.py:315
  46.3 2.0 %collective-permute-start.6 = (bf16[320,512]{1,0:T(8,128)(2,1)S(1)}, bf16[320,512]{1,0:T(8,128)(2,1)S(1)}, u32[]{:S(2)}, u32[]{:S(2)}) collective-permute-start(bf16[320,512]{1,0:T(8,128)(2,1)S(1)} %collective-permute-done.4.refs_1_), channel_id=1, source_target_pairs={{0,2},{1,7},{2,4},{3,1},{4,6},{5,3},{6,0},{7,5},{8,10},{9,15},{10,... | collective-permute-start | bytes 983048 | tf_op jit(solution)/shard_map/ppermute | solution.py:319
  48.3 0.1 stack.44
  48.4 1.9 %collective-permute-start.12 = (bf16[320,512]{1,0:T(8,128)(2,1)S(1)}, bf16[320,512]{1,0:T(8,128)(2,1)S(1)}, u32[]{:S(2)}, u32[]{:S(2)}) collective-permute-start(bf16[320,512]{1,0:T(8,128)(2,1)S(1)} %get-tuple-element.24.refs_0_), channel_id=1, source_target_pairs={{8,0},{16,8},{24,16},{32,24},{40,32},{48,40},{56,48},{64,56},{72,6... | collective-permute-start | bytes 983048 | tf_op jit(solution)/shard_map/ppermute | solution.py:326
  50.3 3.9 %collective-permute-start.11 = (bf16[320,512]{1,0:T(8,128)(2,1)S(1)}, bf16[320,512]{1,0:T(8,128)(2,1)S(1)}, u32[]{:S(2)}, u32[]{:S(2)}) collective-permute-start(bf16[320,512]{1,0:T(8,128)(2,1)S(1)} %get-tuple-element.24.refs_0_), channel_id=1, source_target_pairs={{0,8},{8,16},{16,24},{24,32},{32,40},{40,48},{48,56},{56,64},{64,7... | collective-permute-start | bytes 983048 | tf_op jit(solution)/shard_map/ppermute | solution.py:326
  54.3 2.2 %collective-permute-done.7.refs_4_ = bf16[320,512]{1,0:T(8,128)(2,1)S(1)} collective-permute-done((bf16[320,512]{1,0:T(8,128)(2,1)S(1)}, bf16[320,512]{1,0:T(8,128)(2,1)S(1)}, u32[]{:S(2)}, u32[]{:S(2)}) %collective-permute-start.7) | collective-permute-done | bytes 327712 | tf_op jit(solution)/shard_map/ppermute | solution.py:322
  56.5 3.4 %collective-permute-done.5.refs_2_ = bf16[320,512]{1,0:T(8,128)(2,1)S(1)} collective-permute-done((bf16[320,512]{1,0:T(8,128)(2,1)S(1)}, bf16[320,512]{1,0:T(8,128)(2,1)S(1)}, u32[]{:S(2)}, u32[]{:S(2)}) %collective-permute-start.5) | collective-permute-done | bytes 327712 | tf_op jit(solution)/shard_map/ppermute | solution.py:319
  59.9 3.5 %collective-permute-done.6.refs_3_ = bf16[320,512]{1,0:T(8,128)(2,1)S(1)} collective-permute-done((bf16[320,512]{1,0:T(8,128)(2,1)S(1)}, bf16[320,512]{1,0:T(8,128)(2,1)S(1)}, u32[]{:S(2)}, u32[]{:S(2)}) %collective-permute-start.6) | collective-permute-done | bytes 327712 | tf_op jit(solution)/shard_map/ppermute | solution.py:319
  63.4 0.0 collective-permute-start.9
  63.4 0.0 copy-start.10
  63.4 1.0 %copy-done.10 = bf16[512,512]{1,0:T(8,128)(2,1)S(1)} copy-done((bf16[512,512]{1,0:T(8,128)(2,1)S(1)}, bf16[512,512]{1,0:T(8,128)(2,1)}, u32[]{:S(2)}) %copy-start.10) | copy-done | bytes 524312
  64.4 1.0 %copy-done.11 = bf16[512,512]{1,0:T(8,128)(2,1)S(1)} copy-done((bf16[512,512]{1,0:T(8,128)(2,1)S(1)}, bf16[512,512]{1,0:T(8,128)(2,1)}, u32[]{:S(2)}) %copy-start.11) | copy-done | bytes 524312
  65.5 1.0 %copy-done.12 = bf16[512,512]{1,0:T(8,128)(2,1)S(1)} copy-done((bf16[512,512]{1,0:T(8,128)(2,1)S(1)}, bf16[512,512]{1,0:T(8,128)(2,1)}, u32[]{:S(2)}) %copy-start.12) | copy-done | bytes 524312
  66.5 2.3 %receiver_side.1 = (bf16[2560,512]{1,0:T(8,128)(2,1)S(1)}, bf16[512,512]{1,0:T(8,128)(2,1)S(1)}, f32[320,512]{1,0:T(8,128)S(1)}) custom-call(s32[1,2560]{1,0:T(1,128)S(1)} %reshape.25.recv, bf16[320,512]{1,0:T(8,128)(2,1)S(1)} %get-tuple-element.20.lat, bf16[512,512]{1,0:T(8,128)(2,1)S(1)} %copy-done.9, bf16[512,512]{1,0:T(8,128)(2,1)S(1)} %copy-done.10, ...), custom_call_target="tpu_custom_call" | custom-call | flops 2000000000 | bytes 6000000 | tf_op jit(solution)/shard_map/receiver_side/pallas_call | solution.py:202
  68.9 7.5 %processor.1 = bf16[320,512]{1,0:T(8,128)(2,1)} custom-call(s32[10]{0:T(128)S(1)} %broadcast_multiply_fusion.place, s32[2560]{0:T(1024)S(1)} %copy-done.6, s32[1,2560]{1,0:T(1,128)S(1)} %reshape.25.recv, f32[1,512]{1,0:T(1,128)S(1)} %bitcast.19, bf16[2560,512]{1,0:T(8,128)(2,1)S(1)} %get-tuple-element.21.recv_rows, ...), custom_call_target="tpu_custom_call" | custom-call | tf_op jit(solution)/shard_map/processor/pallas_call | solution.py:259
  (33 shorter events, 0.1 us)
Async XLA Ops:
  0.0 42.6 %copy-start.4 = (bf16[512,512]{1,0:T(8,128)(2,1)S(1)}, bf16[512,512]{1,0:T(8,128)(2,1)}, u32[]{:S(2)}) copy-start(bf16[512,512]{1,0:T(8,128)(2,1)} %w_snd.1) | copy-start | bytes 1572868
  0.0 42.6 %copy-start.3 = (bf16[512,512]{1,0:T(8,128)(2,1)S(1)}, bf16[512,512]{1,0:T(8,128)(2,1)}, u32[]{:S(2)}) copy-start(bf16[512,512]{1,0:T(8,128)(2,1)} %w_enc2.1) | copy-start | bytes 1572868
  0.0 42.6 %copy-start.7 = (f32[512]{0:T(512)S(1)}, f32[512]{0:T(512)}, u32[]{:S(2)}) copy-start(f32[512]{0:T(512)} %param.40) | copy-start | bytes 6148
  0.0 42.6 %copy-start.2 = (bf16[512,512]{1,0:T(8,128)(2,1)S(1)}, bf16[512,512]{1,0:T(8,128)(2,1)}, u32[]{:S(2)}) copy-start(bf16[512,512]{1,0:T(8,128)(2,1)} %w_enc1.1) | copy-start | bytes 1572868
  0.0 42.6 %copy-start.5 = (bf16[320,512]{1,0:T(8,128)(2,1)S(1)}, bf16[320,512]{1,0:T(8,128)(2,1)}, u32[]{:S(2)}) copy-start(bf16[320,512]{1,0:T(8,128)(2,1)} %emb.1) | copy-start | bytes 983044
  20.7 27.6 %copy-start.14 = (s32[2560]{0:T(1024)S(1)}, s32[2560]{0:T(1024)}, u32[]{:S(2)}) copy-start(s32[2560]{0:T(1024)} %param.32) | copy-start | bytes 30724
  20.7 42.7 %copy-start.9 = (bf16[512,512]{1,0:T(8,128)(2,1)S(1)}, bf16[512,512]{1,0:T(8,128)(2,1)}, u32[]{:S(2)}) copy-start(bf16[512,512]{1,0:T(8,128)(2,1)} %w_rcv.1) | copy-start | bytes 1572868
  20.7 42.7 %copy-start.13 = (f32[512]{0:T(512)S(1)}, f32[512]{0:T(512)}, u32[]{:S(2)}) copy-start(f32[512]{0:T(512)} %param.48) | copy-start | bytes 6148
  20.7 7.6 %collective-permute-start.1 = (bf16[320,512]{1,0:T(8,128)(2,1)}, bf16[320,512]{1,0:T(8,128)(2,1)S(1)}, u32[]{:S(2)}, u32[]{:S(2)}) collective-permute-start(bf16[320,512]{1,0:T(8,128)(2,1)} %get-tuple-element.18), channel_id=1, source_target_pairs={{0,1},{1,0},{2,3},{3,2},{4,5},{5,4},{6,7},{7,6},{8,9},{9,8},{10,11... | collective-permute-start | bytes 983048 | tf_op jit(solution)/shard_map/ppermute | solution.py:315
  20.8 10.6 %collective-permute-start = (bf16[320,512]{1,0:T(8,128)(2,1)}, bf16[320,512]{1,0:T(8,128)(2,1)S(1)}, u32[]{:S(2)}, u32[]{:S(2)}) collective-permute-start(bf16[320,512]{1,0:T(8,128)(2,1)} %get-tuple-element.16), channel_id=1, source_target_pairs={{0,1},{1,0},{2,3},{3,2},{4,5},{5,4},{6,7},{7,6},{8,9},{9,8},{10,11... | collective-permute-start | bytes 983048 | tf_op jit(solution)/shard_map/ppermute | solution.py:315
  21.3 12.4 %collective-permute-start.3 = (bf16[320,512]{1,0:T(8,128)(2,1)}, bf16[320,512]{1,0:T(8,128)(2,1)S(1)}, u32[]{:S(2)}, u32[]{:S(2)}) collective-permute-start(bf16[320,512]{1,0:T(8,128)(2,1)} %get-tuple-element.19), channel_id=1, source_target_pairs={{1,3},{2,0},{3,5},{4,2},{5,7},{6,4},{7,9},{8,6},{9,11},{10,8},{11,... | collective-permute-start | bytes 983048 | tf_op jit(solution)/shard_map/ppermute | solution.py:315
  29.5 13.2 %collective-permute-start.2 = (bf16[320,512]{1,0:T(8,128)(2,1)S(1)}, bf16[320,512]{1,0:T(8,128)(2,1)S(1)}, u32[]{:S(2)}, u32[]{:S(2)}) collective-permute-start(bf16[320,512]{1,0:T(8,128)(2,1)S(1)} %add_convert_fusion), channel_id=1, source_target_pairs={{0,2},{2,4},{3,1},{4,6},{5,3},{6,8},{7,5},{8,10},{9,7},{10,12},{11... | collective-permute-start | bytes 983048 | tf_op jit(solution)/shard_map/ppermute | solution.py:315
  42.7 1.1 %copy-start = (f32[320,512]{1,0:T(8,128)S(1)}, f32[320,512]{1,0:T(8,128)}, u32[]{:S(2)}) copy-start(f32[320,512]{1,0:T(8,128)} %get-tuple-element.15.own) | copy-start | bytes 1966084
  44.6 1.7 %collective-permute-start.4 = (bf16[320,512]{1,0:T(8,128)(2,1)S(1)}, bf16[320,512]{1,0:T(8,128)(2,1)S(1)}, u32[]{:S(2)}, u32[]{:S(2)}) collective-permute-start(bf16[320,512]{1,0:T(8,128)(2,1)S(1)} %get-tuple-element.24.refs_0_), channel_id=1, source_target_pairs={{0,1},{1,0},{2,3},{3,2},{4,5},{5,4},{6,7},{7,6},{8,9},{9,8},{10,11... | collective-permute-start | bytes 983048 | tf_op jit(solution)/shard_map/ppermute | solution.py:315
  44.7 11.7 %collective-permute-start.7 = (bf16[320,512]{1,0:T(8,128)(2,1)S(1)}, bf16[320,512]{1,0:T(8,128)(2,1)S(1)}, u32[]{:S(2)}, u32[]{:S(2)}) collective-permute-start(bf16[320,512]{1,0:T(8,128)(2,1)S(1)} %get-tuple-element.24.refs_0_), channel_id=1, source_target_pairs={{0,4},{1,5},{2,6},{3,7},{4,0},{5,1},{6,2},{7,3},{8,12},{9,13},{10,... | collective-permute-start | bytes 983048 | tf_op jit(solution)/shard_map/ppermute | solution.py:322
  44.8 15.0 %collective-permute-start.5 = (bf16[320,512]{1,0:T(8,128)(2,1)S(1)}, bf16[320,512]{1,0:T(8,128)(2,1)S(1)}, u32[]{:S(2)}, u32[]{:S(2)}) collective-permute-start(bf16[320,512]{1,0:T(8,128)(2,1)S(1)} %get-tuple-element.24.refs_0_), channel_id=1, source_target_pairs={{0,2},{1,7},{2,4},{3,1},{4,6},{5,3},{6,0},{7,5},{8,10},{9,15},{10,... | collective-permute-start | bytes 983048 | tf_op jit(solution)/shard_map/ppermute | solution.py:319
  46.3 17.0 %collective-permute-start.6 = (bf16[320,512]{1,0:T(8,128)(2,1)S(1)}, bf16[320,512]{1,0:T(8,128)(2,1)S(1)}, u32[]{:S(2)}, u32[]{:S(2)}) collective-permute-start(bf16[320,512]{1,0:T(8,128)(2,1)S(1)} %collective-permute-done.4.refs_1_), channel_id=1, source_target_pairs={{0,2},{1,7},{2,4},{3,1},{4,6},{5,3},{6,0},{7,5},{8,10},{9,15},{10,... | collective-permute-start | bytes 983048 | tf_op jit(solution)/shard_map/ppermute | solution.py:319
  48.4 20.4 %collective-permute-start.12 = (bf16[320,512]{1,0:T(8,128)(2,1)S(1)}, bf16[320,512]{1,0:T(8,128)(2,1)S(1)}, u32[]{:S(2)}, u32[]{:S(2)}) collective-permute-start(bf16[320,512]{1,0:T(8,128)(2,1)S(1)} %get-tuple-element.24.refs_0_), channel_id=1, source_target_pairs={{8,0},{16,8},{24,16},{32,24},{40,32},{48,40},{56,48},{64,56},{72,6... | collective-permute-start | bytes 983048 | tf_op jit(solution)/shard_map/ppermute | solution.py:326
  50.3 18.5 %collective-permute-start.11 = (bf16[320,512]{1,0:T(8,128)(2,1)S(1)}, bf16[320,512]{1,0:T(8,128)(2,1)S(1)}, u32[]{:S(2)}, u32[]{:S(2)}) collective-permute-start(bf16[320,512]{1,0:T(8,128)(2,1)S(1)} %get-tuple-element.24.refs_0_), channel_id=1, source_target_pairs={{0,8},{8,16},{16,24},{24,32},{32,40},{40,48},{48,56},{56,64},{64,7... | collective-permute-start | bytes 983048 | tf_op jit(solution)/shard_map/ppermute | solution.py:326
  56.5 12.4 %collective-permute-start.10 = (bf16[320,512]{1,0:T(8,128)(2,1)S(1)}, bf16[320,512]{1,0:T(8,128)(2,1)S(1)}, u32[]{:S(2)}, u32[]{:S(2)}) collective-permute-start(bf16[320,512]{1,0:T(8,128)(2,1)S(1)} %collective-permute-done.7.refs_4_), channel_id=1, source_target_pairs={{0,1},{1,0},{2,3},{3,2},{4,5},{5,4},{6,7},{7,6},{8,9},{9,8},{10,11... | collective-permute-start | bytes 983048 | tf_op jit(solution)/shard_map/ppermute | solution.py:315
  59.9 9.0 %collective-permute-start.8 = (bf16[320,512]{1,0:T(8,128)(2,1)S(1)}, bf16[320,512]{1,0:T(8,128)(2,1)S(1)}, u32[]{:S(2)}, u32[]{:S(2)}) collective-permute-start(bf16[320,512]{1,0:T(8,128)(2,1)S(1)} %collective-permute-done.5.refs_2_), channel_id=1, source_target_pairs={{0,1},{1,0},{2,3},{3,2},{4,5},{5,4},{6,7},{7,6},{8,9},{9,8},{10,11... | collective-permute-start | bytes 983048 | tf_op jit(solution)/shard_map/ppermute | solution.py:315
  63.4 5.5 %collective-permute-start.9 = (bf16[320,512]{1,0:T(8,128)(2,1)S(1)}, bf16[320,512]{1,0:T(8,128)(2,1)S(1)}, u32[]{:S(2)}, u32[]{:S(2)}) collective-permute-start(bf16[320,512]{1,0:T(8,128)(2,1)S(1)} %collective-permute-done.6.refs_3_), channel_id=1, source_target_pairs={{0,1},{1,0},{2,3},{3,2},{4,5},{5,4},{6,7},{7,6},{8,9},{9,8},{10,11... | collective-permute-start | bytes 983048 | tf_op jit(solution)/shard_map/ppermute | solution.py:315
  63.4 1.0 %copy-start.10 = (bf16[512,512]{1,0:T(8,128)(2,1)S(1)}, bf16[512,512]{1,0:T(8,128)(2,1)}, u32[]{:S(2)}) copy-start(bf16[512,512]{1,0:T(8,128)(2,1)} %w_edge.1) | copy-start | bytes 1572868
  64.4 1.0 %copy-start.11 = (bf16[512,512]{1,0:T(8,128)(2,1)S(1)}, bf16[512,512]{1,0:T(8,128)(2,1)}, u32[]{:S(2)}) copy-start(bf16[512,512]{1,0:T(8,128)(2,1)} %w_p1.1) | copy-start | bytes 1572868
  65.5 1.0 %copy-start.12 = (bf16[512,512]{1,0:T(8,128)(2,1)S(1)}, bf16[512,512]{1,0:T(8,128)(2,1)}, u32[]{:S(2)}) copy-start(bf16[512,512]{1,0:T(8,128)(2,1)} %w_p2.1) | copy-start | bytes 1572868
  66.5 2.3 %copy-start.1 = (bf16[512,512]{1,0:T(8,128)(2,1)S(1)}, bf16[512,512]{1,0:T(8,128)(2,1)}, u32[]{:S(2)}) copy-start(bf16[512,512]{1,0:T(8,128)(2,1)} %w_p3.1) | copy-start | bytes 1572868
  66.5 2.3 %copy-start.6 = (s32[2560]{0:T(1024)S(1)}, s32[2560]{0:T(1024)}, u32[]{:S(2)}) copy-start(s32[2560]{0:T(1024)} %send.1) | copy-start | bytes 30724
  66.5 2.3 %copy-start.8 = (f32[512]{0:T(512)S(1)}, f32[512]{0:T(512)}, u32[]{:S(2)}) copy-start(f32[512]{0:T(512)} %param.44) | copy-start | bytes 6148

commit v4 on v3

v4 whole, which is shorter than its diff:
```python
import jax
import jax.numpy as jnp
from jax import lax
from jax.experimental import pallas as pl
from jax.experimental.pallas import tpu as pltpu
from jax.sharding import PartitionSpec as P

F32 = jnp.float32
BF16 = jnp.bfloat16
LANES = 128
EDGE_BLOCK = 256
BOTH = ("grp", "inner")
MESSAGE_VMEM = 57 * 2**20
PROCESSOR_VMEM = 40 * 2**20


def silu(v):
    half = v * 0.5
    return half + half * jnp.tanh(half)


def split3(v):
    high = v.astype(BF16).astype(F32)
    rest = v - high
    mid = rest.astype(BF16).astype(F32)
    return high, mid, (rest - mid).astype(BF16).astype(F32)


def dot(a, b):
    return jnp.dot(a, b, preferred_element_type=F32)


def dot_first(a, b):
    return lax.dot_general(a, b, (((0,), (0,)), ((), ())), preferred_element_type=F32)


def one_hot(ids, rows):
    numbers = lax.broadcasted_iota(jnp.int32, (rows, ids.shape[1]), 0)
    return jnp.where(numbers == ids, 1.0, 0.0).astype(BF16)


def put_rows(table, first, rows):
    parts = rows.shape[1] // LANES
    for j in range(parts):
        table[pl.ds(first * parts + j, rows.shape[0], stride=parts), :] = rows[
            :, j * LANES : (j + 1) * LANES
        ]


def message_kernel(
    src_hbm, grid_hbm, w_in1_hbm, b_in_hbm, w_in2_hbm, w_g2m_hbm, geom_hbm, w_geo_hbm, b_g2m_hbm, dst_hbm, node_hbm,
    back2, back1, own, on1, on2,
    src_rows, grid_in, w_in1, b_in, w_in2, w_g2m, geom, w_geo, b_g2m, dst, node, src, table, buf_a, buf_b, w8, g8, w48, w_both, msg_a, msg_b, sums, sems,
):
    nodes, edges = grid_in.shape[1], src.shape[0]
    places = lax.axis_size("inner")
    place = lax.axis_index("inner")
    band = lax.axis_index("grp") * places + place
    turn = 1 - 2 * lax.rem(place, 2)
    bands, rows = 5, own.shape[0]
    chunk = 512
    chunks = nodes // chunk
    here = [
        (w_in1_hbm, w_in1), (b_in_hbm, b_in), (w_in2_hbm, w_in2), (w_g2m_hbm, w_g2m), (src_hbm, src_rows),
        (geom_hbm, geom), (w_geo_hbm, w_geo), (b_g2m_hbm, b_g2m), (dst_hbm, dst), (node_hbm, node),
    ]
    copies = [pltpu.make_async_copy(a, b, sems.at[i]) for i, (a, b) in enumerate(here)]
    grids = []
    for k in range(chunks):
        part = pl.ds(k * chunk, chunk)
        grids.append(
            pltpu.make_async_copy(grid_hbm.at[:, part], grid_in.at[:, part], sems.at[len(here) + k])
        )
    for copy in [copies[0], grids[0], copies[1], copies[4], copies[2], copies[3]] + grids[1:] + copies[5:]:
        copy.start()
    copies[4].wait()
    src_rows[...] = src_rows[...] * 4
    to_scalars = pltpu.make_async_copy(src_rows.at[0], src, sems.at[len(here) + chunks])
    to_scalars.start()
    copies[0].wait()
    copies[1].wait()
    for k in range(chunks):
        grids[k].wait()
        hid = dot_first(grid_in[:, k * chunk : (k + 1) * chunk], w_in1[...])
        hid = silu(hid + b_in[...]).astype(BF16)
        if k == 0:
            copies[2].wait()
            copies[3].wait()
            w_both[...] = dot(w_in2[...], w_g2m[...]).astype(BF16)
        put_rows(table, k * chunk, dot(hid, w_both[...]))

    to_scalars.wait()
    for copy in copies[5:]:
        copy.wait()
    node[...] = ((dst[...] - band) * turn + 2) * rows + node[...]
    w8[...] = jnp.zeros_like(w8)
    w8[0:4, :] = w_geo[...]
    w8[4:5, :] = b_g2m[...]
    high, mid, low = split3(w8[...])
    w48[...] = jnp.concatenate([high, high, high, mid, mid, low], axis=0).astype(BF16)
    g8[...] = jnp.zeros_like(g8)
    g8[0:4, :] = geom[...]
    g8[4:5, :] = jnp.ones((1, g8.shape[1]), F32)
    sums[...] = jnp.zeros_like(sums)
    msg_b[...] = jnp.zeros_like(msg_b)

    def gather(base, buf):
        for e in range(EDGE_BLOCK):
            row = pl.multiple_of(src[base + e], 4)
            buf[4 * e : 4 * e + 4, :] = table[pl.ds(row, 4), :]

    def emit(base, half, buf):
        base = pl.multiple_of(base, EDGE_BLOCK)
        high, mid, low = split3(g8[:, pl.ds(base, EDGE_BLOCK)])
        g48 = jnp.concatenate([high, mid, low, high, mid, high], axis=0).astype(BF16)
        geo = dot_first(g48, w48[...])
        for j in range(4):
            lanes = slice(j * LANES, (j + 1) * LANES)
            v = buf[pl.ds(j, EDGE_BLOCK, stride=4), :] + geo[:, lanes]
            (msg_a, msg_b)[half][:, lanes] = silu(v).astype(BF16)

    def scatter(base, half):
        base = pl.multiple_of(jnp.maximum(base, 0), EDGE_BLOCK)
        select = one_hot(node[:, pl.ds(base, EDGE_BLOCK)], bands * rows)
        sums[...] += dot(select, (msg_a, msg_b)[half][...])

    blocks = edges // EDGE_BLOCK
    gather(0, buf_a)

    def step(t, carry):
        base = pl.multiple_of(t * (2 * EDGE_BLOCK), 2 * EDGE_BLOCK)
        gather(base + EDGE_BLOCK, buf_b)
        emit(base, 0, buf_a)
        scatter(base - EDGE_BLOCK, 1)
        gather(jnp.minimum(base + 2 * EDGE_BLOCK, (blocks - 1) * EDGE_BLOCK), buf_a)
        emit(base + EDGE_BLOCK, 1, buf_b)
        scatter(base, 0)
        return carry

    lax.fori_loop(0, blocks // 2, step, 0)
    scatter(edges - EDGE_BLOCK, 1)
    for which, out in enumerate((back2, back1, own, on1, on2)):
        out[...] = sums[which * rows : (which + 1) * rows, :].astype(out.dtype)


def band_sums(rows, *arrays):
    g2m_src, grid_in, w_in1 = arrays[:3]
    edges, nodes, width = g2m_src.shape[1], grid_in.shape[1], w_in1.shape[1]
    vmem = pl.BlockSpec(memory_space=pltpu.VMEM)
    hbm = pl.BlockSpec(memory_space=pltpu.HBM)
    return pl.pallas_call(
        message_kernel,
        out_shape=[jax.ShapeDtypeStruct((rows, width), dtype) for dtype in [BF16] * 5],
        in_specs=[hbm] * len(arrays),
        out_specs=[vmem] * 5,
        scratch_shapes=[pltpu.VMEM(a.shape, a.dtype) for a in arrays]
        + [
            pltpu.SMEM((edges,), jnp.int32),
            pltpu.VMEM((4 * nodes, LANES), F32),
            pltpu.VMEM((4 * EDGE_BLOCK, LANES), F32),
            pltpu.VMEM((4 * EDGE_BLOCK, LANES), F32),
            pltpu.VMEM((8, width), F32),
            pltpu.VMEM((8, edges), F32),
            pltpu.VMEM((48, width), BF16),
            pltpu.VMEM((width, width), BF16),
            pltpu.VMEM((EDGE_BLOCK, width), BF16),
            pltpu.VMEM((EDGE_BLOCK, width), BF16),
            pltpu.VMEM((5 * rows, width), F32),
            pltpu.SemaphoreType.DMA((len(arrays) + 4,)),
        ],
        compiler_params=pltpu.CompilerParams(vmem_limit_bytes=MESSAGE_VMEM),
        name="band_sums",
    )(*arrays)


def encoder_kernel(some, one, emb, w_enc1, b_enc, w_enc2, w_snd, lat, snd):
    total = some[...].astype(F32) + one[...].astype(F32)
    enc = silu(dot(total.astype(BF16), w_enc1[...]) + b_enc[...]).astype(BF16)
    mesh_lat = (emb[...].astype(F32) + dot(enc, w_enc2[...])).astype(BF16)
    lat[...] = mesh_lat
    snd[...] = dot(mesh_lat, w_snd[...]).astype(BF16)


def encoder(some, one, emb, w_enc1, b_enc, w_enc2, w_snd):
    vmem = pl.BlockSpec(memory_space=pltpu.VMEM)
    rows, width = emb.shape
    return pl.pallas_call(
        encoder_kernel,
        out_shape=[jax.ShapeDtypeStruct((rows, width), BF16)] * 2,
        in_specs=[vmem] * 7,
        out_specs=[vmem] * 2,
        compiler_params=pltpu.CompilerParams(vmem_limit_bytes=16 * 2**20),
        name="encoder",
    )(some, one, emb, w_enc1, b_enc.reshape(1, -1), w_enc2, w_snd)


def receiver_kernel(send, lat, w_rcv, w_edge, w_p1, w_p2, b_p, b_edge, w_p3, packed, packed32, offsets):
    offsets[...] = send[...] * 4
    rows, width = lat.shape
    packed[0:width, :] = dot(w_edge[...], w_p1[...]).astype(BF16)
    packed[width : 2 * width, :] = w_p3[...]
    packed[2 * width : 2 * width + rows, :] = lat[...]
    packed32[0:rows, :] = dot(lat[...], w_p2[...]) + b_p[...]
    packed32[rows : rows + 8, :] = jnp.broadcast_to(b_edge[...], (8, width))
    packed[2 * width + rows :, :] = dot(lat[...], w_rcv[...]).astype(BF16)


def receiver_side(send, lat, w_rcv, w_edge, w_p1, w_p2, b_p, b_edge, w_p3):
    vmem = pl.BlockSpec(memory_space=pltpu.VMEM)
    rows, width = lat.shape
    edges = send.shape[0]
    return pl.pallas_call(
        receiver_kernel,
        out_shape=[
            jax.ShapeDtypeStruct((2 * width + 2 * rows, width), BF16),
            jax.ShapeDtypeStruct((rows + 8, width), F32),
            jax.ShapeDtypeStruct((1, edges), jnp.int32),
        ],
        in_specs=[vmem] * 9,
        out_specs=[vmem] * 3,
        compiler_params=pltpu.CompilerParams(vmem_limit_bytes=12 * 2**20),
        cost_estimate=pl.CostEstimate(flops=10**9, bytes_accessed=6 * 10**6, transcendentals=0),
        name="receiver_side",
    )(
        send.reshape(1, -1), lat, w_rcv, w_edge, w_p1, w_p2,
        b_p.reshape(1, -1), b_edge.reshape(1, -1), w_p3,
    )


def processor_kernel(place, send, recv, packed_hbm, packed32_hbm, *refs):
    count = 10
    out, packed, packed32, shard, table, buf_a, buf_b, hid_a, hid_b, agg, sems = refs[count:]
    rows, width = out.shape
    shards = refs[:count]
    copies = [pltpu.make_async_copy(shards[k], shard.at[k], sems.at[k]) for k in range(count)]
    copies.append(pltpu.make_async_copy(packed32_hbm, packed32, sems.at[count]))
    copies.append(pltpu.make_async_copy(packed_hbm, packed, sems.at[count + 1]))
    for copy in copies:
        copy.start()
    lat = packed.at[2 * width : 2 * width + rows]
    receivers = packed.at[2 * width + rows : 2 * width + 2 * rows]
    agg[...] = jnp.zeros_like(agg)
    hid_b[...] = jnp.zeros_like(hid_b)
    for k in range(count):
        copies[k].wait()
        put_rows(table, place[k], shard[k].astype(F32))
    copies[count].wait()
    copies[count + 1].wait()

    def gather(base, buf):
        for e in range(EDGE_BLOCK):
            row = pl.multiple_of(send[0, base + e], 4)
            buf[4 * e : 4 * e + 4, :] = table[pl.ds(row, 4), :]

    def select(base):
        base = pl.multiple_of(base, EDGE_BLOCK)
        return one_hot(recv[:, pl.ds(base, EDGE_BLOCK)], rows)

    def emit(base, buf, hid):
        received = dot_first(select(base), receivers[...]) + packed32[rows : rows + 1, :]
        for j in range(4):
            lanes = slice(j * LANES, (j + 1) * LANES)
            v = buf[pl.ds(j, EDGE_BLOCK, stride=4), :] + received[:, lanes]
            hid[:, lanes] = silu(v).astype(BF16)

    def add_up(base, hid):
        agg[...] += dot(select(jnp.maximum(base, 0)), hid[...])

    blocks = send.shape[1] // EDGE_BLOCK
    gather(0, buf_a)

    def step(t, carry):
        base = t * (2 * EDGE_BLOCK)
        gather(base + EDGE_BLOCK, buf_b)
        emit(base, buf_a, hid_a)
        add_up(base - EDGE_BLOCK, hid_b)
        gather(jnp.minimum(base + 2 * EDGE_BLOCK, (blocks - 1) * EDGE_BLOCK), buf_a)
        emit(base + EDGE_BLOCK, buf_b, hid_b)
        add_up(base, hid_a)
        return carry

    lax.fori_loop(0, blocks // 2, step, 0)
    add_up((blocks - 1) * EDGE_BLOCK, hid_b)
    node = dot(agg[...].astype(BF16), packed[0:width, :]) + packed32[0:rows, :]
    change = dot(silu(node).astype(BF16), packed[width : 2 * width, :])
    out[...] = (lat[...].astype(F32) + change).astype(BF16)


def processor(place, send, recv, packed, packed32, shards):
    vmem = pl.BlockSpec(memory_space=pltpu.VMEM)
    smem = pl.BlockSpec(memory_space=pltpu.SMEM)
    hbm = pl.BlockSpec(memory_space=pltpu.HBM)
    rows, width = shards[0].shape
    return pl.pallas_call(
        processor_kernel,
        out_shape=jax.ShapeDtypeStruct((rows, width), BF16),
        in_specs=[smem, smem, vmem] + [hbm] * (2 + len(shards)),
        out_specs=vmem,
        scratch_shapes=[
            pltpu.VMEM(packed.shape, BF16),
            pltpu.VMEM(packed32.shape, F32),
            pltpu.VMEM((len(shards), rows, width), BF16),
            pltpu.VMEM((4 * len(shards) * rows, LANES), F32),
            pltpu.VMEM((4 * EDGE_BLOCK, LANES), F32),
            pltpu.VMEM((4 * EDGE_BLOCK, LANES), F32),
            pltpu.VMEM((EDGE_BLOCK, width), BF16),
            pltpu.VMEM((EDGE_BLOCK, width), BF16),
            pltpu.VMEM((rows, width), F32),
            pltpu.SemaphoreType.DMA((len(shards) + 2,)),
        ],
        compiler_params=pltpu.CompilerParams(vmem_limit_bytes=PROCESSOR_VMEM),
        name="processor",
    )(place, send, recv.reshape(1, -1), packed, packed32, *shards)


def on_device(
    grid_in,
    g2m_geom,
    g2m_src,
    g2m_dst,
    g2m_node,
    mesh_emb,
    mesh_send,
    mesh_recv,
    w_in1,
    b_in,
    w_in2,
    w_g2m,
    w_geo,
    b_g2m,
    w_enc1,
    b_enc,
    w_enc2,
    w_snd,
    w_rcv,
    b_edge,
    w_edge,
    w_p1,
    w_p2,
    b_p,
    w_p3,
):
    groups, places = lax.axis_size("grp"), lax.axis_size("inner")
    bands = groups * places
    nodes_here = mesh_emb.shape[0]
    place = lax.axis_index("inner")
    core = place % 2

    def by_parity(even, odd):
        pairs = [(b, b + (odd if b % 2 else even)) for b in range(bands)]
        pairs = [pair for pair in pairs if 0 <= pair[1] < bands]
        return lambda value: lax.ppermute(value, BOTH, pairs)

    def onward(value):
        pairs = [(i, (i + (-2 if i % 2 else 2)) % places) for i in range(places)]
        return lax.ppermute(value, "inner", pairs)

    def across(value):
        return lax.ppermute(value, "inner", [(i, (i + 4) % places) for i in range(places)])

    def along_groups(value, by):
        pairs = [(i, i + by) for i in range(groups) if 0 <= i + by < groups]
        return lax.ppermute(value, "grp", pairs)

    other_core = by_parity(1, -1)

    turn = 1 - 2 * core
    back2, back1, own, on1, on2 = band_sums(
        nodes_here,
        g2m_src.reshape(1, -1),
        grid_in.T,
        w_in1,
        b_in.reshape(1, -1),
        w_in2,
        w_g2m,
        g2m_geom,
        w_geo,
        b_g2m.reshape(1, -1),
        g2m_dst.reshape(1, -1),
        g2m_node.reshape(1, -1),
    )
    crossing = other_core(back1)
    two = by_parity(-2, 2)(back2)
    joint = (on2.astype(F32) + crossing.astype(F32)).astype(BF16)
    one = by_parity(2, -2)(joint)
    on1, _ = lax.optimization_barrier((on1, joint))
    near = other_core(on1)
    some = own.astype(F32) + near.astype(F32) + two.astype(F32)
    mesh_lat, senders = encoder(some.astype(BF16), one, mesh_emb, w_enc1, b_enc, w_enc2, w_snd)

    partner = other_core(senders)
    next_a = onward(senders)
    far = across(senders)
    next_b = onward(partner)
    low = along_groups(senders, 1)
    high = along_groups(senders, -1)
    packed, packed32, offsets = receiver_side(
        mesh_send, mesh_lat, w_rcv, w_edge, w_p1, w_p2, b_p, b_edge, w_p3
    )
    next_a, offsets = lax.optimization_barrier((next_a, offsets))
    shards = [senders, partner, next_a, next_b, far]
    shards = shards + [other_core(shard) for shard in shards[2:]] + [low, high]
    before, after, opposite = [(place + by) % places for by in (-2 * turn, 2 * turn, 4)]
    where = [place, place + turn, before, before + turn, opposite]
    where = where + [after + turn, after, opposite + turn, places, places + 1]
    starts = jnp.stack([jnp.asarray(p, jnp.int32) for p in where]) * nodes_here
    return processor(starts, offsets, mesh_recv, packed, packed32, shards)


def solution(mesh):
    split = P(BOTH)
    rows = P(BOTH, None)
    return jax.shard_map(
        on_device,
        mesh=mesh,
        in_specs=(rows, P(None, BOTH), split, rows, split, rows, split, split) + (P(),) * 17,
        out_specs=rows,
        check_vma=False,
    )
```

time: 77.5 us -> 71.6 us (0.924)
  local copies, waits for them, and re-layouts: 4.35 us -> 0.2 us
  Pallas kernels: 30.6 us -> 29.1 us
  waiting for transfers between devices: 21.8 us -> 20.7 us
  starting transfers between devices: 17.5 us -> 18.5 us
    unnamed x30 -> x28, local copies, waits for them, and re-layouts: 4.25 us -> 0.09 us
    ppermute x1, waiting for transfers between devices: 2.2 us -> 0.01 us  [across(): lax.ppermute(value, 'inner', [(i, (i + 4) % places) for i in range(places)])]
    pallas_call x1, Pallas kernels: 2.25 us -> 0.82 us  [receiver_side(): pl.pallas_call(receiver_kernel, out_shape=[jax.ShapeDtypeStruct((2 * widt...]
    pallas_call x1, Pallas kernels: 19.9 us -> 18.6 us  [band_sums(): pl.pallas_call(message_kernel, out_shape=[jax.ShapeDtypeStruct((rows, wid...]
    pallas_call x1, Pallas kernels: 7.52 us -> 8.84 us  [processor(): pl.pallas_call(processor_kernel, out_shape=jax.ShapeDtypeStruct((rows, wi...]
    ppermute x2, waiting for transfers between devices: 0.01 us -> 1.16 us  [along_groups(): return lax.ppermute(value, 'grp', pairs)]
    convert_element_type x1 -> x2, other arithmetic: 1.18 us -> 2.16 us  [the longest x1 1.1 us: on_device(): some.astype(BF16)]
  transfers between devices with their start and end apart: 13 -> 13, of which waited for: 6 -> 7; matrix products, arithmetic and copies ran while one was open for 2% -> 3% of each run, Pallas kernels for 3% -> 1%
where the time goes in v4:
time: 71.6 us; the launch traced here: 71 us
  Pallas kernels  29.1 us (41%)
  waiting for transfers between devices  20.7 us (29%)
  starting transfers between devices  18.5 us (26%)
  other arithmetic  2.16 us (3%)
    pallas_call x1, Pallas kernels, band_sums(): pl.pallas_call(message_kernel, out_shape=[jax.ShapeDtypeStruct((rows, wid...  18.6 us
    ppermute x8, waiting for transfers between devices, by_parity(): return lambda value: lax.ppermute(value, BOTH, pairs)  12.3 us
    ppermute x8, starting transfers between devices, by_parity(): return lambda value: lax.ppermute(value, BOTH, pairs)  9.94 us
    pallas_call x1, Pallas kernels, processor(): pl.pallas_call(processor_kernel, out_shape=jax.ShapeDtypeStruct((rows, wi...  8.84 us
    ppermute x2, waiting for transfers between devices, onward(): return lax.ppermute(value, 'inner', pairs)  7.29 us
    ppermute x2, starting transfers between devices, along_groups(): return lax.ppermute(value, 'grp', pairs)  5.84 us
    ppermute x2, starting transfers between devices, onward(): return lax.ppermute(value, 'inner', pairs)  2.63 us
  transfers between devices with their start and end apart: 13, of which 7 were waited for; matrix products, arithmetic and copies ran while one was open for 3% of the time, Pallas kernels for 1%

profile of v4, /device:TPU:96, one launch (start us, length us, event | category | flops | bytes accessed | tf_op | source)
XLA Modules:
  0.0 71.0 jit_solution(14219070215512797157)
XLA Ops:
  0.0 18.6 %band_sums.1 = (bf16[320,512]{1,0:T(8,128)(2,1)}, bf16[320,512]{1,0:T(8,128)(2,1)}, bf16[320,512]{1,0:T(8,128)(2,1)}, bf16[320,512]{1,0:T(8,128)(2,1)}, bf16[320,512]{1,0:T(8,128)(2,1)}) custom-call(s32[1,4096]{1,0:T(1,128)} %bitcast.21, bf16[474,2048]{1,0:T(8,128)(2,1)} %bitcast.20, bf16[474,512]{1,0:T(8,128)(2,1)} %w_in1_hbm.1, f32[1,512]{1,0:T(1,128)} %bitcast.24, ...), custom_call_target="tpu_custom_call" | custom-call | tf_op jit(solution)/shard_map/band_sums/pallas_call | solution.py:151
  18.6 0.0 copy-start
  18.6 0.0 copy-start.3
  18.6 0.0 copy-start.4
  18.7 0.1 collective-permute-start
  18.7 7.1 %collective-permute-start.2 = (bf16[320,512]{1,0:T(8,128)(2,1)}, bf16[320,512]{1,0:T(8,128)(2,1)S(1)}, u32[]{:S(2)}, u32[]{:S(2)}) collective-permute-start(bf16[320,512]{1,0:T(8,128)(2,1)} %get-tuple-element.23), channel_id=1, source_target_pairs={{1,3},{2,0},{3,5},{4,2},{5,7},{6,4},{7,9},{8,6},{9,11},{10,8},{11,... | collective-permute-start | bytes 983048 | tf_op jit(solution)/shard_map/ppermute | solution.py:352
  25.9 1.1 %add_convert_fusion.1 = bf16[320,512]{1,0:T(8,128)(2,1)S(1)} fusion(bf16[320,512]{1,0:T(8,128)(2,1)S(1)} %collective-permute-done, bf16[320,512]{1,0:T(8,128)(2,1)} %get-tuple-element.20), kind=kLoop, calls=%fused_computation.1 | loop fusion | flops 655360 | bytes 983040 | tf_op jit(solution)/shard_map/convert_element_type | solution.py:384
  27.0 0.0 copy-start.6
  27.0 0.0 copy-start.7
  27.0 0.0 copy-start.10
  27.0 0.0 copy-start.11
  27.0 0.1 collective-permute-start.1
  27.1 2.1 %collective-permute-start.3 = (bf16[320,512]{1,0:T(8,128)(2,1)S(1)}, bf16[320,512]{1,0:T(8,128)(2,1)S(1)}, u32[]{:S(2)}, u32[]{:S(2)}) collective-permute-start(bf16[320,512]{1,0:T(8,128)(2,1)S(1)} %add_convert_fusion.1), channel_id=1, source_target_pairs={{0,2},{2,4},{3,1},{4,6},{5,3},{6,8},{7,5},{8,10},{9,7},{10,12},{11... | collective-permute-start | bytes 983048 | tf_op jit(solution)/shard_map/ppermute | solution.py:352
  29.2 1.6 %collective-permute-done.2 = bf16[320,512]{1,0:T(8,128)(2,1)S(1)} collective-permute-done((bf16[320,512]{1,0:T(8,128)(2,1)}, bf16[320,512]{1,0:T(8,128)(2,1)S(1)}, u32[]{:S(2)}, u32[]{:S(2)}) %collective-permute-start.2) | collective-permute-done | bytes 327712 | tf_op jit(solution)/shard_map/ppermute | solution.py:352
  30.8 1.1 %add_convert_fusion.some = bf16[320,512]{1,0:T(8,128)(2,1)S(1)} fusion(bf16[320,512]{1,0:T(8,128)(2,1)S(1)} %collective-permute-done.2, bf16[320,512]{1,0:T(8,128)(2,1)S(1)} %collective-permute-done.1, bf16[320,512]{1,0:T(8,128)(2,1)} %get-tuple-element.18), kind=kLoop, calls=%fused_computation | loop fusion | flops 983040 | bytes 1310720 | tf_op jit(solution)/shard_map/convert_element_type | solution.py:389
  31.9 8.5 %collective-permute-done.3.one = bf16[320,512]{1,0:T(8,128)(2,1)S(1)} collective-permute-done((bf16[320,512]{1,0:T(8,128)(2,1)S(1)}, bf16[320,512]{1,0:T(8,128)(2,1)S(1)}, u32[]{:S(2)}, u32[]{:S(2)}) %collective-permute-start.3) | collective-permute-done | bytes 327712 | tf_op jit(solution)/shard_map/ppermute | solution.py:352
  40.5 0.9 %encoder.1 = (bf16[320,512]{1,0:T(8,128)(2,1)S(1)}, bf16[320,512]{1,0:T(8,128)(2,1)S(1)}) custom-call(bf16[320,512]{1,0:T(8,128)(2,1)S(1)} %add_convert_fusion.some, bf16[320,512]{1,0:T(8,128)(2,1)S(1)} %collective-permute-done.3.one, bf16[320,512]{1,0:T(8,128)(2,1)S(1)} %copy-done.3, bf16[512,512]{1,0:T(8,128)(2,1)S(1)} %copy-done, f32[1,512]{1,0:T(1,128)S(1)} %bitcast.17, ...), custom_call_target="tpu_custom_call" | custom-call | tf_op jit(solution)/shard_map/encoder/pallas_call | solution.py:187
  41.4 0.1 collective-permute-start.5
  41.5 0.1 collective-permute-start.4
  41.6 0.1 collective-permute-start.7
  41.7 1.4 %collective-permute-done.5.refs_1_ = bf16[320,512]{1,0:T(8,128)(2,1)S(1)} collective-permute-done((bf16[320,512]{1,0:T(8,128)(2,1)S(1)}, bf16[320,512]{1,0:T(8,128)(2,1)S(1)}, u32[]{:S(2)}, u32[]{:S(2)}) %collective-permute-start.5) | collective-permute-done | bytes 327712 | tf_op jit(solution)/shard_map/ppermute | solution.py:352
  43.1 2.6 %collective-permute-start.6 = (bf16[320,512]{1,0:T(8,128)(2,1)S(1)}, bf16[320,512]{1,0:T(8,128)(2,1)}, u32[]{:S(2)}, u32[]{:S(2)}) collective-permute-start(bf16[320,512]{1,0:T(8,128)(2,1)S(1)} %collective-permute-done.5.refs_1_), channel_id=1, source_target_pairs={{0,2},{1,7},{2,4},{3,1},{4,6},{5,3},{6,0},{7,5},{8,10},{9,15},{10,... | collective-permute-start | bytes 983048 | tf_op jit(solution)/shard_map/ppermute | solution.py:356
  45.7 1.9 %collective-permute-start.12 = (bf16[320,512]{1,0:T(8,128)(2,1)S(1)}, bf16[320,512]{1,0:T(8,128)(2,1)}, u32[]{:S(2)}, u32[]{:S(2)}) collective-permute-start(bf16[320,512]{1,0:T(8,128)(2,1)S(1)} %get-tuple-element.24.refs_0_), channel_id=1, source_target_pairs={{8,0},{16,8},{24,16},{32,24},{40,32},{48,40},{56,48},{64,56},{72,6... | collective-permute-start | bytes 983048 | tf_op jit(solution)/shard_map/ppermute | solution.py:363
  47.6 3.9 %collective-permute-start.11 = (bf16[320,512]{1,0:T(8,128)(2,1)S(1)}, bf16[320,512]{1,0:T(8,128)(2,1)}, u32[]{:S(2)}, u32[]{:S(2)}) collective-permute-start(bf16[320,512]{1,0:T(8,128)(2,1)S(1)} %get-tuple-element.24.refs_0_), channel_id=1, source_target_pairs={{0,8},{8,16},{16,24},{24,32},{32,40},{40,48},{48,56},{56,64},{64,7... | collective-permute-start | bytes 983048 | tf_op jit(solution)/shard_map/ppermute | solution.py:363
  51.6 0.8 %receiver_side.1 = (bf16[1664,512]{1,0:T(8,128)(2,1)S(1)}, f32[328,512]{1,0:T(8,128)S(1)}, s32[1,2560]{1,0:T(1,128)S(1)}) custom-call(s32[1,2560]{1,0:T(1,128)S(1)} %reshape.36.send, bf16[320,512]{1,0:T(8,128)(2,1)S(1)} %get-tuple-element.25.lat, bf16[512,512]{1,0:T(8,128)(2,1)S(1)} %copy-done.5, bf16[512,512]{1,0:T(8,128)(2,1)S(1)} %copy-done.6, ...), custom_call_target="tpu_custom_call" | custom-call | flops 1000000000 | bytes 6000000 | tf_op jit(solution)/shard_map/receiver_side/pallas_call | solution.py:212
  52.4 4.2 %collective-permute-done.4.refs_2_ = bf16[320,512]{1,0:T(8,128)(2,1)S(1)} collective-permute-done((bf16[320,512]{1,0:T(8,128)(2,1)S(1)}, bf16[320,512]{1,0:T(8,128)(2,1)S(1)}, u32[]{:S(2)}, u32[]{:S(2)}) %collective-permute-start.4) | collective-permute-done | bytes 327712 | tf_op jit(solution)/shard_map/ppermute | solution.py:356
  56.6 0.5 collective-permute-start.10
  57.1 3.1 %collective-permute-done.6.refs_3_ = bf16[320,512]{1,0:T(8,128)(2,1)} collective-permute-done((bf16[320,512]{1,0:T(8,128)(2,1)S(1)}, bf16[320,512]{1,0:T(8,128)(2,1)}, u32[]{:S(2)}, u32[]{:S(2)}) %collective-permute-start.6) | collective-permute-done | bytes 327712 | tf_op jit(solution)/shard_map/ppermute | solution.py:356
  60.3 0.1 stack.35
  60.4 1.2 %collective-permute-done.11.refs_8_ = bf16[320,512]{1,0:T(8,128)(2,1)} collective-permute-done((bf16[320,512]{1,0:T(8,128)(2,1)S(1)}, bf16[320,512]{1,0:T(8,128)(2,1)}, u32[]{:S(2)}, u32[]{:S(2)}) %collective-permute-start.11) | collective-permute-done | bytes 327712 | tf_op jit(solution)/shard_map/ppermute | solution.py:363
  61.5 0.7 collective-permute-done.9.refs_6_
  62.2 8.8 %processor.1 = bf16[320,512]{1,0:T(8,128)(2,1)} custom-call(s32[10]{0:T(128)S(1)} %broadcast_multiply_fusion.place, s32[1,2560]{1,0:T(1,128)S(1)} %get-tuple-element.27.send, s32[1,2560]{1,0:T(1,128)S(1)} %reshape.39.recv, bf16[1664,512]{1,0:T(8,128)(2,1)S(1)} %get-tuple-element.28.packed_hbm, f32[328,512]{1,0:T(8,128)S(1)} %get-tuple-element.29.packed32_hbm, ...), custom_call_target="tpu_custom_call" | custom-call | tf_op jit(solution)/shard_map/processor/pallas_call | solution.py:294
  (32 shorter events, 0.1 us)
Async XLA Ops:
  18.6 21.9 %copy-start = (bf16[512,512]{1,0:T(8,128)(2,1)S(1)}, bf16[512,512]{1,0:T(8,128)(2,1)}, u32[]{:S(2)}) copy-start(bf16[512,512]{1,0:T(8,128)(2,1)} %w_enc1.1) | copy-start | bytes 1572868
  18.6 21.9 %copy-start.1 = (bf16[512,512]{1,0:T(8,128)(2,1)S(1)}, bf16[512,512]{1,0:T(8,128)(2,1)}, u32[]{:S(2)}) copy-start(bf16[512,512]{1,0:T(8,128)(2,1)} %w_enc2.1) | copy-start | bytes 1572868
  18.6 21.8 %copy-start.2 = (bf16[512,512]{1,0:T(8,128)(2,1)S(1)}, bf16[512,512]{1,0:T(8,128)(2,1)}, u32[]{:S(2)}) copy-start(bf16[512,512]{1,0:T(8,128)(2,1)} %w_snd.1) | copy-start | bytes 1572868
  18.6 21.8 %copy-start.3 = (bf16[320,512]{1,0:T(8,128)(2,1)S(1)}, bf16[320,512]{1,0:T(8,128)(2,1)}, u32[]{:S(2)}) copy-start(bf16[320,512]{1,0:T(8,128)(2,1)} %emb.1) | copy-start | bytes 983044
  18.6 21.8 %copy-start.4 = (f32[512]{0:T(512)S(1)}, f32[512]{0:T(512)}, u32[]{:S(2)}) copy-start(f32[512]{0:T(512)} %param.40) | copy-start | bytes 6148
  18.7 7.2 %collective-permute-start = (bf16[320,512]{1,0:T(8,128)(2,1)}, bf16[320,512]{1,0:T(8,128)(2,1)S(1)}, u32[]{:S(2)}, u32[]{:S(2)}) collective-permute-start(bf16[320,512]{1,0:T(8,128)(2,1)} %get-tuple-element.21), channel_id=1, source_target_pairs={{0,1},{1,0},{2,3},{3,2},{4,5},{5,4},{6,7},{7,6},{8,9},{9,8},{10,11... | collective-permute-start | bytes 983048 | tf_op jit(solution)/shard_map/ppermute | solution.py:352
  18.7 12.1 %collective-permute-start.2 = (bf16[320,512]{1,0:T(8,128)(2,1)}, bf16[320,512]{1,0:T(8,128)(2,1)S(1)}, u32[]{:S(2)}, u32[]{:S(2)}) collective-permute-start(bf16[320,512]{1,0:T(8,128)(2,1)} %get-tuple-element.23), channel_id=1, source_target_pairs={{1,3},{2,0},{3,5},{4,2},{5,7},{6,4},{7,9},{8,6},{9,11},{10,8},{11,... | collective-permute-start | bytes 983048 | tf_op jit(solution)/shard_map/ppermute | solution.py:352
  26.9 18.7 %copy-start.12 = (s32[2560]{0:T(1024)S(1)}, s32[2560]{0:T(1024)}, u32[]{:S(2)}) copy-start(s32[2560]{0:T(1024)} %param.31) | copy-start | bytes 30724
  27.0 24.6 %copy-start.5 = (bf16[512,512]{1,0:T(8,128)(2,1)S(1)}, bf16[512,512]{1,0:T(8,128)(2,1)}, u32[]{:S(2)}) copy-start(bf16[512,512]{1,0:T(8,128)(2,1)} %w_rcv.1) | copy-start | bytes 1572868
  27.0 24.6 %copy-start.6 = (bf16[512,512]{1,0:T(8,128)(2,1)S(1)}, bf16[512,512]{1,0:T(8,128)(2,1)}, u32[]{:S(2)}) copy-start(bf16[512,512]{1,0:T(8,128)(2,1)} %w_edge.1) | copy-start | bytes 1572868
  27.0 24.6 %copy-start.7 = (bf16[512,512]{1,0:T(8,128)(2,1)S(1)}, bf16[512,512]{1,0:T(8,128)(2,1)}, u32[]{:S(2)}) copy-start(bf16[512,512]{1,0:T(8,128)(2,1)} %w_p1.1) | copy-start | bytes 1572868
  27.0 24.6 %copy-start.8 = (bf16[512,512]{1,0:T(8,128)(2,1)S(1)}, bf16[512,512]{1,0:T(8,128)(2,1)}, u32[]{:S(2)}) copy-start(bf16[512,512]{1,0:T(8,128)(2,1)} %w_p2.1) | copy-start | bytes 1572868
  27.0 24.6 %copy-start.9 = (bf16[512,512]{1,0:T(8,128)(2,1)S(1)}, bf16[512,512]{1,0:T(8,128)(2,1)}, u32[]{:S(2)}) copy-start(bf16[512,512]{1,0:T(8,128)(2,1)} %w_p3.1) | copy-start | bytes 1572868
  27.0 24.6 %copy-start.10 = (f32[512]{0:T(512)S(1)}, f32[512]{0:T(512)}, u32[]{:S(2)}) copy-start(f32[512]{0:T(512)} %param.48) | copy-start | bytes 6148
  27.0 24.6 %copy-start.11 = (f32[512]{0:T(512)S(1)}, f32[512]{0:T(512)}, u32[]{:S(2)}) copy-start(f32[512]{0:T(512)} %param.44) | copy-start | bytes 6148
  27.0 3.8 %collective-permute-start.1 = (bf16[320,512]{1,0:T(8,128)(2,1)}, bf16[320,512]{1,0:T(8,128)(2,1)S(1)}, u32[]{:S(2)}, u32[]{:S(2)}) collective-permute-start(bf16[320,512]{1,0:T(8,128)(2,1)} %get-tuple-element.22), channel_id=1, source_target_pairs={{0,1},{1,0},{2,3},{3,2},{4,5},{5,4},{6,7},{7,6},{8,9},{9,8},{10,11... | collective-permute-start | bytes 983048 | tf_op jit(solution)/shard_map/ppermute | solution.py:352
  27.1 13.3 %collective-permute-start.3 = (bf16[320,512]{1,0:T(8,128)(2,1)S(1)}, bf16[320,512]{1,0:T(8,128)(2,1)S(1)}, u32[]{:S(2)}, u32[]{:S(2)}) collective-permute-start(bf16[320,512]{1,0:T(8,128)(2,1)S(1)} %add_convert_fusion.1), channel_id=1, source_target_pairs={{0,2},{2,4},{3,1},{4,6},{5,3},{6,8},{7,5},{8,10},{9,7},{10,12},{11... | collective-permute-start | bytes 983048 | tf_op jit(solution)/shard_map/ppermute | solution.py:352
  41.4 18.9 %copy-start.13 = (s32[2560]{0:T(1024)S(1)}, s32[2560]{0:T(1024)}, u32[]{:S(2)}) copy-start(s32[2560]{0:T(1024)} %param.32) | copy-start | bytes 30724
  41.4 1.7 %collective-permute-start.5 = (bf16[320,512]{1,0:T(8,128)(2,1)S(1)}, bf16[320,512]{1,0:T(8,128)(2,1)S(1)}, u32[]{:S(2)}, u32[]{:S(2)}) collective-permute-start(bf16[320,512]{1,0:T(8,128)(2,1)S(1)} %get-tuple-element.24.refs_0_), channel_id=1, source_target_pairs={{0,1},{1,0},{2,3},{3,2},{4,5},{5,4},{6,7},{7,6},{8,9},{9,8},{10,11... | collective-permute-start | bytes 983048 | tf_op jit(solution)/shard_map/ppermute | solution.py:352
  41.5 15.1 %collective-permute-start.4 = (bf16[320,512]{1,0:T(8,128)(2,1)S(1)}, bf16[320,512]{1,0:T(8,128)(2,1)S(1)}, u32[]{:S(2)}, u32[]{:S(2)}) collective-permute-start(bf16[320,512]{1,0:T(8,128)(2,1)S(1)} %get-tuple-element.24.refs_0_), channel_id=1, source_target_pairs={{0,2},{1,7},{2,4},{3,1},{4,6},{5,3},{6,0},{7,5},{8,10},{9,15},{10,... | collective-permute-start | bytes 983048 | tf_op jit(solution)/shard_map/ppermute | solution.py:356
  41.6 15.1 %collective-permute-start.7 = (bf16[320,512]{1,0:T(8,128)(2,1)S(1)}, bf16[320,512]{1,0:T(8,128)(2,1)}, u32[]{:S(2)}, u32[]{:S(2)}) collective-permute-start(bf16[320,512]{1,0:T(8,128)(2,1)S(1)} %get-tuple-element.24.refs_0_), channel_id=1, source_target_pairs={{0,4},{1,5},{2,6},{3,7},{4,0},{5,1},{6,2},{7,3},{8,12},{9,13},{10,... | collective-permute-start | bytes 983048 | tf_op jit(solution)/shard_map/ppermute | solution.py:359
  43.1 17.1 %collective-permute-start.6 = (bf16[320,512]{1,0:T(8,128)(2,1)S(1)}, bf16[320,512]{1,0:T(8,128)(2,1)}, u32[]{:S(2)}, u32[]{:S(2)}) collective-permute-start(bf16[320,512]{1,0:T(8,128)(2,1)S(1)} %collective-permute-done.5.refs_1_), channel_id=1, source_target_pairs={{0,2},{1,7},{2,4},{3,1},{4,6},{5,3},{6,0},{7,5},{8,10},{9,15},{10,... | collective-permute-start | bytes 983048 | tf_op jit(solution)/shard_map/ppermute | solution.py:356
  45.7 14.7 %collective-permute-start.12 = (bf16[320,512]{1,0:T(8,128)(2,1)S(1)}, bf16[320,512]{1,0:T(8,128)(2,1)}, u32[]{:S(2)}, u32[]{:S(2)}) collective-permute-start(bf16[320,512]{1,0:T(8,128)(2,1)S(1)} %get-tuple-element.24.refs_0_), channel_id=1, source_target_pairs={{8,0},{16,8},{24,16},{32,24},{40,32},{48,40},{56,48},{64,56},{72,6... | collective-permute-start | bytes 983048 | tf_op jit(solution)/shard_map/ppermute | solution.py:363
  47.6 13.9 %collective-permute-start.11 = (bf16[320,512]{1,0:T(8,128)(2,1)S(1)}, bf16[320,512]{1,0:T(8,128)(2,1)}, u32[]{:S(2)}, u32[]{:S(2)}) collective-permute-start(bf16[320,512]{1,0:T(8,128)(2,1)S(1)} %get-tuple-element.24.refs_0_), channel_id=1, source_target_pairs={{0,8},{8,16},{16,24},{24,32},{32,40},{40,48},{48,56},{56,64},{64,7... | collective-permute-start | bytes 983048 | tf_op jit(solution)/shard_map/ppermute | solution.py:363
  56.6 4.9 %collective-permute-start.8 = (bf16[320,512]{1,0:T(8,128)(2,1)S(1)}, bf16[320,512]{1,0:T(8,128)(2,1)}, u32[]{:S(2)}, u32[]{:S(2)}) collective-permute-start(bf16[320,512]{1,0:T(8,128)(2,1)S(1)} %collective-permute-done.4.refs_2_), channel_id=1, source_target_pairs={{0,1},{1,0},{2,3},{3,2},{4,5},{5,4},{6,7},{7,6},{8,9},{9,8},{10,11... | collective-permute-start | bytes 983048 | tf_op jit(solution)/shard_map/ppermute | solution.py:352
  56.6 4.9 %collective-permute-start.10 = (bf16[320,512]{1,0:T(8,128)(2,1)}, bf16[320,512]{1,0:T(8,128)(2,1)}, u32[]{:S(2)}, u32[]{:S(2)}) collective-permute-start(bf16[320,512]{1,0:T(8,128)(2,1)} %collective-permute-done.7.refs_4_), channel_id=1, source_target_pairs={{0,1},{1,0},{2,3},{3,2},{4,5},{5,4},{6,7},{7,6},{8,9},{9,8},{10,11... | collective-permute-start | bytes 983048 | tf_op jit(solution)/shard_map/ppermute | solution.py:352
  60.2 2.0 %collective-permute-start.9 = (bf16[320,512]{1,0:T(8,128)(2,1)}, bf16[320,512]{1,0:T(8,128)(2,1)}, u32[]{:S(2)}, u32[]{:S(2)}) collective-permute-start(bf16[320,512]{1,0:T(8,128)(2,1)} %collective-permute-done.6.refs_3_), channel_id=1, source_target_pairs={{0,1},{1,0},{2,3},{3,2},{4,5},{5,4},{6,7},{7,6},{8,9},{9,8},{10,11... | collective-permute-start | bytes 983048 | tf_op jit(solution)/shard_map/ppermute | solution.py:352

commit v5 on v4

--- a/solution.py
+++ b/solution.py
@@ -12,6 +12,7 @@
 BOTH = ("grp", "inner")
 MESSAGE_VMEM = 57 * 2**20
 PROCESSOR_VMEM = 40 * 2**20
+NEAR_SHARDS = 3
 
 
 def silu(v):
@@ -58,7 +59,7 @@
     band = lax.axis_index("grp") * places + place
     turn = 1 - 2 * lax.rem(place, 2)
     bands, rows = 5, own.shape[0]
-    chunk = 512
+    chunk = 1024
     chunks = nodes // chunk
     here = [
         (w_in1_hbm, w_in1), (b_in_hbm, b_in), (w_in2_hbm, w_in2), (w_g2m_hbm, w_g2m), (src_hbm, src_rows),
@@ -227,25 +228,23 @@
     )
 
 
-def processor_kernel(place, send, recv, packed_hbm, packed32_hbm, *refs):
-    count = 10
-    out, packed, packed32, shard, table, buf_a, buf_b, hid_a, hid_b, agg, sems = refs[count:]
+def processor_kernel(place, send, recv, packed, packed32, *refs):
+    count, near = 10, NEAR_SHARDS
+    out, shard, table, buf_a, buf_b, hid_a, hid_b, agg, sems = refs[count:]
     rows, width = out.shape
-    shards = refs[:count]
-    copies = [pltpu.make_async_copy(shards[k], shard.at[k], sems.at[k]) for k in range(count)]
-    copies.append(pltpu.make_async_copy(packed32_hbm, packed32, sems.at[count]))
-    copies.append(pltpu.make_async_copy(packed_hbm, packed, sems.at[count + 1]))
-    for copy in copies:
-        copy.start()
     lat = packed.at[2 * width : 2 * width + rows]
     receivers = packed.at[2 * width + rows : 2 * width + 2 * rows]
+    copies = []
+    for k in range(near, count):
+        copies.append(pltpu.make_async_copy(refs[k], shard.at[k - near], sems.at[k - near]))
+        copies[-1].start()
     agg[...] = jnp.zeros_like(agg)
     hid_b[...] = jnp.zeros_like(hid_b)
-    for k in range(count):
-        copies[k].wait()
-        put_rows(table, place[k], shard[k].astype(F32))
-    copies[count].wait()
-    copies[count + 1].wait()
+    for k in range(near):
+        put_rows(table, place[k], refs[k][...].astype(F32))
+    for k in range(near, count):
+        copies[k - near].wait()
+        put_rows(table, place[k], shard[k - near].astype(F32))
 
     def gather(base, buf):
         for e in range(EDGE_BLOCK):
@@ -294,19 +293,17 @@
     return pl.pallas_call(
         processor_kernel,
         out_shape=jax.ShapeDtypeStruct((rows, width), BF16),
-        in_specs=[smem, smem, vmem] + [hbm] * (2 + len(shards)),
+        in_specs=[smem, smem] + [vmem] * (3 + NEAR_SHARDS) + [hbm] * (len(shards) - NEAR_SHARDS),
         out_specs=vmem,
         scratch_shapes=[
-            pltpu.VMEM(packed.shape, BF16),
-            pltpu.VMEM(packed32.shape, F32),
-            pltpu.VMEM((len(shards), rows, width), BF16),
+            pltpu.VMEM((len(shards) - NEAR_SHARDS, rows, width), BF16),
             pltpu.VMEM((4 * len(shards) * rows, LANES), F32),
             pltpu.VMEM((4 * EDGE_BLOCK, LANES), F32),
             pltpu.VMEM((4 * EDGE_BLOCK, LANES), F32),
             pltpu.VMEM((EDGE_BLOCK, width), BF16),
             pltpu.VMEM((EDGE_BLOCK, width), BF16),
             pltpu.VMEM((rows, width), F32),
-            pltpu.SemaphoreType.DMA((len(shards) + 2,)),
+            pltpu.SemaphoreType.DMA((len(shards) - NEAR_SHARDS,)),
         ],
         compiler_params=pltpu.CompilerParams(vmem_limit_bytes=PROCESSOR_VMEM),
         name="processor",

time: 71.6 us -> 70.8 us (0.989)
  Pallas kernels: 29.1 us -> 28.3 us
where the time goes in v5:
time: 70.8 us; the launch traced here: 70.2 us
  Pallas kernels  28.3 us (40%)
  waiting for transfers between devices  20.7 us (29%)
  starting transfers between devices  18.5 us (26%)
  other arithmetic  2.16 us (3%)
    pallas_call x1, Pallas kernels, band_sums(): pl.pallas_call(message_kernel, out_shape=[jax.ShapeDtypeStruct((rows, wid...  18.2 us
    ppermute x8, waiting for transfers between devices, by_parity(): return lambda value: lax.ppermute(value, BOTH, pairs)  12.3 us
    ppermute x8, starting transfers between devices, by_parity(): return lambda value: lax.ppermute(value, BOTH, pairs)  9.92 us
    pallas_call x1, Pallas kernels, processor(): pl.pallas_call(processor_kernel, out_shape=jax.ShapeDtypeStruct((rows, wi...  8.38 us
    ppermute x2, waiting for transfers between devices, onward(): return lax.ppermute(value, 'inner', pairs)  7.29 us
    ppermute x2, starting transfers between devices, along_groups(): return lax.ppermute(value, 'grp', pairs)  5.84 us
    ppermute x2, starting transfers between devices, onward(): return lax.ppermute(value, 'inner', pairs)  2.63 us
  transfers between devices with their start and end apart: 13, of which 7 were waited for; matrix products, arithmetic and copies ran while one was open for 3% of the time, Pallas kernels for 1%

profile of v5, /device:TPU:96, one launch (start us, length us, event | category | flops | bytes accessed | tf_op | source)
XLA Modules:
  0.0 70.2 jit_solution(3462569884832005280)
XLA Ops:
  0.0 18.2 %band_sums.1 = (bf16[320,512]{1,0:T(8,128)(2,1)}, bf16[320,512]{1,0:T(8,128)(2,1)}, bf16[320,512]{1,0:T(8,128)(2,1)}, bf16[320,512]{1,0:T(8,128)(2,1)}, bf16[320,512]{1,0:T(8,128)(2,1)}) custom-call(s32[1,4096]{1,0:T(1,128)} %bitcast.21, bf16[474,2048]{1,0:T(8,128)(2,1)} %bitcast.20, bf16[474,512]{1,0:T(8,128)(2,1)} %w_in1_hbm.1, f32[1,512]{1,0:T(1,128)} %bitcast.24, ...), custom_call_target="tpu_custom_call" | custom-call | tf_op jit(solution)/shard_map/band_sums/pallas_call | solution.py:152
  18.2 0.0 copy-start
  18.3 0.0 copy-start.3
  18.3 0.0 copy-start.4
  18.3 0.1 collective-permute-start
  18.4 7.1 %collective-permute-start.2 = (bf16[320,512]{1,0:T(8,128)(2,1)}, bf16[320,512]{1,0:T(8,128)(2,1)S(1)}, u32[]{:S(2)}, u32[]{:S(2)}) collective-permute-start(bf16[320,512]{1,0:T(8,128)(2,1)} %get-tuple-element.23), channel_id=1, source_target_pairs={{1,3},{2,0},{3,5},{4,2},{5,7},{6,4},{7,9},{8,6},{9,11},{10,8},{11,... | collective-permute-start | bytes 983048 | tf_op jit(solution)/shard_map/ppermute | solution.py:349
  25.5 1.1 %add_convert_fusion.1 = bf16[320,512]{1,0:T(8,128)(2,1)S(1)} fusion(bf16[320,512]{1,0:T(8,128)(2,1)S(1)} %collective-permute-done, bf16[320,512]{1,0:T(8,128)(2,1)} %get-tuple-element.20), kind=kLoop, calls=%fused_computation.1 | loop fusion | flops 655360 | bytes 983040 | tf_op jit(solution)/shard_map/convert_element_type | solution.py:381
  26.6 0.0 copy-start.12
  26.6 0.0 copy-start.5
  26.6 0.0 copy-start.7
  26.6 0.0 copy-start.8
  26.7 0.1 collective-permute-start.1
  26.8 2.1 %collective-permute-start.3 = (bf16[320,512]{1,0:T(8,128)(2,1)S(1)}, bf16[320,512]{1,0:T(8,128)(2,1)S(1)}, u32[]{:S(2)}, u32[]{:S(2)}) collective-permute-start(bf16[320,512]{1,0:T(8,128)(2,1)S(1)} %add_convert_fusion.1), channel_id=1, source_target_pairs={{0,2},{2,4},{3,1},{4,6},{5,3},{6,8},{7,5},{8,10},{9,7},{10,12},{11... | collective-permute-start | bytes 983048 | tf_op jit(solution)/shard_map/ppermute | solution.py:349
  28.8 1.6 %collective-permute-done.2 = bf16[320,512]{1,0:T(8,128)(2,1)S(1)} collective-permute-done((bf16[320,512]{1,0:T(8,128)(2,1)}, bf16[320,512]{1,0:T(8,128)(2,1)S(1)}, u32[]{:S(2)}, u32[]{:S(2)}) %collective-permute-start.2) | collective-permute-done | bytes 327712 | tf_op jit(solution)/shard_map/ppermute | solution.py:349
  30.4 1.1 %add_convert_fusion.some = bf16[320,512]{1,0:T(8,128)(2,1)S(1)} fusion(bf16[320,512]{1,0:T(8,128)(2,1)S(1)} %collective-permute-done.2, bf16[320,512]{1,0:T(8,128)(2,1)S(1)} %collective-permute-done.1, bf16[320,512]{1,0:T(8,128)(2,1)} %get-tuple-element.18), kind=kLoop, calls=%fused_computation | loop fusion | flops 983040 | bytes 1310720 | tf_op jit(solution)/shard_map/convert_element_type | solution.py:386
  31.5 8.6 %collective-permute-done.3.one = bf16[320,512]{1,0:T(8,128)(2,1)S(1)} collective-permute-done((bf16[320,512]{1,0:T(8,128)(2,1)S(1)}, bf16[320,512]{1,0:T(8,128)(2,1)S(1)}, u32[]{:S(2)}, u32[]{:S(2)}) %collective-permute-start.3) | collective-permute-done | bytes 327712 | tf_op jit(solution)/shard_map/ppermute | solution.py:349
  40.1 0.9 %encoder.1 = (bf16[320,512]{1,0:T(8,128)(2,1)S(1)}, bf16[320,512]{1,0:T(8,128)(2,1)S(1)}) custom-call(bf16[320,512]{1,0:T(8,128)(2,1)S(1)} %add_convert_fusion.some, bf16[320,512]{1,0:T(8,128)(2,1)S(1)} %collective-permute-done.3.one, bf16[320,512]{1,0:T(8,128)(2,1)S(1)} %copy-done.3, bf16[512,512]{1,0:T(8,128)(2,1)S(1)} %copy-done, f32[1,512]{1,0:T(1,128)S(1)} %bitcast.17, ...), custom_call_target="tpu_custom_call" | custom-call | tf_op jit(solution)/shard_map/encoder/pallas_call | solution.py:188
  41.0 0.1 collective-permute-start.5
  41.1 0.1 collective-permute-start.4
  41.2 0.1 collective-permute-start.7
  41.3 1.4 %collective-permute-done.5.refs_1_ = bf16[320,512]{1,0:T(8,128)(2,1)S(1)} collective-permute-done((bf16[320,512]{1,0:T(8,128)(2,1)S(1)}, bf16[320,512]{1,0:T(8,128)(2,1)S(1)}, u32[]{:S(2)}, u32[]{:S(2)}) %collective-permute-start.5) | collective-permute-done | bytes 327712 | tf_op jit(solution)/shard_map/ppermute | solution.py:349
  42.7 2.6 %collective-permute-start.6 = (bf16[320,512]{1,0:T(8,128)(2,1)S(1)}, bf16[320,512]{1,0:T(8,128)(2,1)}, u32[]{:S(2)}, u32[]{:S(2)}) collective-permute-start(bf16[320,512]{1,0:T(8,128)(2,1)S(1)} %collective-permute-done.5.refs_1_), channel_id=1, source_target_pairs={{0,2},{1,7},{2,4},{3,1},{4,6},{5,3},{6,0},{7,5},{8,10},{9,15},{10,... | collective-permute-start | bytes 983048 | tf_op jit(solution)/shard_map/ppermute | solution.py:353
  45.3 1.9 %collective-permute-start.12 = (bf16[320,512]{1,0:T(8,128)(2,1)S(1)}, bf16[320,512]{1,0:T(8,128)(2,1)}, u32[]{:S(2)}, u32[]{:S(2)}) collective-permute-start(bf16[320,512]{1,0:T(8,128)(2,1)S(1)} %get-tuple-element.24.refs_0_), channel_id=1, source_target_pairs={{8,0},{16,8},{24,16},{32,24},{40,32},{48,40},{56,48},{64,56},{72,6... | collective-permute-start | bytes 983048 | tf_op jit(solution)/shard_map/ppermute | solution.py:360
  47.2 3.9 %collective-permute-start.11 = (bf16[320,512]{1,0:T(8,128)(2,1)S(1)}, bf16[320,512]{1,0:T(8,128)(2,1)}, u32[]{:S(2)}, u32[]{:S(2)}) collective-permute-start(bf16[320,512]{1,0:T(8,128)(2,1)S(1)} %get-tuple-element.24.refs_0_), channel_id=1, source_target_pairs={{0,8},{8,16},{16,24},{24,32},{32,40},{40,48},{48,56},{56,64},{64,7... | collective-permute-start | bytes 983048 | tf_op jit(solution)/shard_map/ppermute | solution.py:360
  51.2 0.8 %receiver_side.1 = (bf16[1664,512]{1,0:T(8,128)(2,1)S(1)}, f32[328,512]{1,0:T(8,128)S(1)}, s32[1,2560]{1,0:T(1,128)S(1)}) custom-call(s32[1,2560]{1,0:T(1,128)S(1)} %reshape.36.send, bf16[320,512]{1,0:T(8,128)(2,1)S(1)} %get-tuple-element.25.lat, bf16[512,512]{1,0:T(8,128)(2,1)S(1)} %copy-done.5, bf16[512,512]{1,0:T(8,128)(2,1)S(1)} %copy-done.6, ...), custom_call_target="tpu_custom_call" | custom-call | flops 1000000000 | bytes 6000000 | tf_op jit(solution)/shard_map/receiver_side/pallas_call | solution.py:213
  52.1 4.2 %collective-permute-done.4.refs_2_ = bf16[320,512]{1,0:T(8,128)(2,1)S(1)} collective-permute-done((bf16[320,512]{1,0:T(8,128)(2,1)S(1)}, bf16[320,512]{1,0:T(8,128)(2,1)S(1)}, u32[]{:S(2)}, u32[]{:S(2)}) %collective-permute-start.4) | collective-permute-done | bytes 327712 | tf_op jit(solution)/shard_map/ppermute | solution.py:353
  56.3 0.5 collective-permute-start.10
  56.8 3.1 %collective-permute-done.6.refs_3_ = bf16[320,512]{1,0:T(8,128)(2,1)} collective-permute-done((bf16[320,512]{1,0:T(8,128)(2,1)S(1)}, bf16[320,512]{1,0:T(8,128)(2,1)}, u32[]{:S(2)}, u32[]{:S(2)}) %collective-permute-start.6) | collective-permute-done | bytes 327712 | tf_op jit(solution)/shard_map/ppermute | solution.py:353
  59.9 0.1 stack.35
  60.0 1.2 %collective-permute-done.11.refs_8_ = bf16[320,512]{1,0:T(8,128)(2,1)} collective-permute-done((bf16[320,512]{1,0:T(8,128)(2,1)S(1)}, bf16[320,512]{1,0:T(8,128)(2,1)}, u32[]{:S(2)}, u32[]{:S(2)}) %collective-permute-start.11) | collective-permute-done | bytes 327712 | tf_op jit(solution)/shard_map/ppermute | solution.py:360
  61.1 0.7 collective-permute-done.9.refs_6_
  61.8 8.4 %processor.1 = bf16[320,512]{1,0:T(8,128)(2,1)} custom-call(s32[10]{0:T(128)S(1)} %broadcast_multiply_fusion.place, s32[1,2560]{1,0:T(1,128)S(1)} %get-tuple-element.27.send, s32[1,2560]{1,0:T(1,128)S(1)} %reshape.39.recv, bf16[1664,512]{1,0:T(8,128)(2,1)S(1)} %get-tuple-element.28.packed, f32[328,512]{1,0:T(8,128)S(1)} %get-tuple-element.29.packed32, ...), custom_call_target="tpu_custom_call" | custom-call | tf_op jit(solution)/shard_map/processor/pallas_call | solution.py:293
  (32 shorter events, 0.1 us)
Async XLA Ops:
  18.2 21.8 %copy-start = (bf16[512,512]{1,0:T(8,128)(2,1)S(1)}, bf16[512,512]{1,0:T(8,128)(2,1)}, u32[]{:S(2)}) copy-start(bf16[512,512]{1,0:T(8,128)(2,1)} %w_enc1.1) | copy-start | bytes 1572868
  18.3 21.8 %copy-start.1 = (bf16[512,512]{1,0:T(8,128)(2,1)S(1)}, bf16[512,512]{1,0:T(8,128)(2,1)}, u32[]{:S(2)}) copy-start(bf16[512,512]{1,0:T(8,128)(2,1)} %w_enc2.1) | copy-start | bytes 1572868
  18.3 21.8 %copy-start.2 = (bf16[512,512]{1,0:T(8,128)(2,1)S(1)}, bf16[512,512]{1,0:T(8,128)(2,1)}, u32[]{:S(2)}) copy-start(bf16[512,512]{1,0:T(8,128)(2,1)} %w_snd.1) | copy-start | bytes 1572868
  18.3 21.8 %copy-start.3 = (bf16[320,512]{1,0:T(8,128)(2,1)S(1)}, bf16[320,512]{1,0:T(8,128)(2,1)}, u32[]{:S(2)}) copy-start(bf16[320,512]{1,0:T(8,128)(2,1)} %emb.1) | copy-start | bytes 983044
  18.3 21.8 %copy-start.4 = (f32[512]{0:T(512)S(1)}, f32[512]{0:T(512)}, u32[]{:S(2)}) copy-start(f32[512]{0:T(512)} %param.40) | copy-start | bytes 6148
  18.3 7.2 %collective-permute-start = (bf16[320,512]{1,0:T(8,128)(2,1)}, bf16[320,512]{1,0:T(8,128)(2,1)S(1)}, u32[]{:S(2)}, u32[]{:S(2)}) collective-permute-start(bf16[320,512]{1,0:T(8,128)(2,1)} %get-tuple-element.21), channel_id=1, source_target_pairs={{0,1},{1,0},{2,3},{3,2},{4,5},{5,4},{6,7},{7,6},{8,9},{9,8},{10,11... | collective-permute-start | bytes 983048 | tf_op jit(solution)/shard_map/ppermute | solution.py:349
  18.4 12.0 %collective-permute-start.2 = (bf16[320,512]{1,0:T(8,128)(2,1)}, bf16[320,512]{1,0:T(8,128)(2,1)S(1)}, u32[]{:S(2)}, u32[]{:S(2)}) collective-permute-start(bf16[320,512]{1,0:T(8,128)(2,1)} %get-tuple-element.23), channel_id=1, source_target_pairs={{1,3},{2,0},{3,5},{4,2},{5,7},{6,4},{7,9},{8,6},{9,11},{10,8},{11,... | collective-permute-start | bytes 983048 | tf_op jit(solution)/shard_map/ppermute | solution.py:349
  26.6 18.7 %copy-start.12 = (s32[2560]{0:T(1024)S(1)}, s32[2560]{0:T(1024)}, u32[]{:S(2)}) copy-start(s32[2560]{0:T(1024)} %param.31) | copy-start | bytes 30724
  26.6 24.6 %copy-start.5 = (bf16[512,512]{1,0:T(8,128)(2,1)S(1)}, bf16[512,512]{1,0:T(8,128)(2,1)}, u32[]{:S(2)}) copy-start(bf16[512,512]{1,0:T(8,128)(2,1)} %w_rcv.1) | copy-start | bytes 1572868
  26.6 24.6 %copy-start.6 = (bf16[512,512]{1,0:T(8,128)(2,1)S(1)}, bf16[512,512]{1,0:T(8,128)(2,1)}, u32[]{:S(2)}) copy-start(bf16[512,512]{1,0:T(8,128)(2,1)} %w_edge.1) | copy-start | bytes 1572868
  26.6 24.6 %copy-start.7 = (bf16[512,512]{1,0:T(8,128)(2,1)S(1)}, bf16[512,512]{1,0:T(8,128)(2,1)}, u32[]{:S(2)}) copy-start(bf16[512,512]{1,0:T(8,128)(2,1)} %w_p1.1) | copy-start | bytes 1572868
  26.6 24.6 %copy-start.8 = (bf16[512,512]{1,0:T(8,128)(2,1)S(1)}, bf16[512,512]{1,0:T(8,128)(2,1)}, u32[]{:S(2)}) copy-start(bf16[512,512]{1,0:T(8,128)(2,1)} %w_p2.1) | copy-start | bytes 1572868
  26.6 24.6 %copy-start.9 = (bf16[512,512]{1,0:T(8,128)(2,1)S(1)}, bf16[512,512]{1,0:T(8,128)(2,1)}, u32[]{:S(2)}) copy-start(bf16[512,512]{1,0:T(8,128)(2,1)} %w_p3.1) | copy-start | bytes 1572868
  26.6 24.6 %copy-start.10 = (f32[512]{0:T(512)S(1)}, f32[512]{0:T(512)}, u32[]{:S(2)}) copy-start(f32[512]{0:T(512)} %param.48) | copy-start | bytes 6148
  26.7 24.6 %copy-start.11 = (f32[512]{0:T(512)S(1)}, f32[512]{0:T(512)}, u32[]{:S(2)}) copy-start(f32[512]{0:T(512)} %param.44) | copy-start | bytes 6148
  26.7 3.7 %collective-permute-start.1 = (bf16[320,512]{1,0:T(8,128)(2,1)}, bf16[320,512]{1,0:T(8,128)(2,1)S(1)}, u32[]{:S(2)}, u32[]{:S(2)}) collective-permute-start(bf16[320,512]{1,0:T(8,128)(2,1)} %get-tuple-element.22), channel_id=1, source_target_pairs={{0,1},{1,0},{2,3},{3,2},{4,5},{5,4},{6,7},{7,6},{8,9},{9,8},{10,11... | collective-permute-start | bytes 983048 | tf_op jit(solution)/shard_map/ppermute | solution.py:349
  26.8 13.3 %collective-permute-start.3 = (bf16[320,512]{1,0:T(8,128)(2,1)S(1)}, bf16[320,512]{1,0:T(8,128)(2,1)S(1)}, u32[]{:S(2)}, u32[]{:S(2)}) collective-permute-start(bf16[320,512]{1,0:T(8,128)(2,1)S(1)} %add_convert_fusion.1), channel_id=1, source_target_pairs={{0,2},{2,4},{3,1},{4,6},{5,3},{6,8},{7,5},{8,10},{9,7},{10,12},{11... | collective-permute-start | bytes 983048 | tf_op jit(solution)/shard_map/ppermute | solution.py:349
  41.0 18.9 %copy-start.13 = (s32[2560]{0:T(1024)S(1)}, s32[2560]{0:T(1024)}, u32[]{:S(2)}) copy-start(s32[2560]{0:T(1024)} %param.32) | copy-start | bytes 30724
  41.0 1.7 %collective-permute-start.5 = (bf16[320,512]{1,0:T(8,128)(2,1)S(1)}, bf16[320,512]{1,0:T(8,128)(2,1)S(1)}, u32[]{:S(2)}, u32[]{:S(2)}) collective-permute-start(bf16[320,512]{1,0:T(8,128)(2,1)S(1)} %get-tuple-element.24.refs_0_), channel_id=1, source_target_pairs={{0,1},{1,0},{2,3},{3,2},{4,5},{5,4},{6,7},{7,6},{8,9},{9,8},{10,11... | collective-permute-start | bytes 983048 | tf_op jit(solution)/shard_map/ppermute | solution.py:349
  41.1 15.1 %collective-permute-start.4 = (bf16[320,512]{1,0:T(8,128)(2,1)S(1)}, bf16[320,512]{1,0:T(8,128)(2,1)S(1)}, u32[]{:S(2)}, u32[]{:S(2)}) collective-permute-start(bf16[320,512]{1,0:T(8,128)(2,1)S(1)} %get-tuple-element.24.refs_0_), channel_id=1, source_target_pairs={{0,2},{1,7},{2,4},{3,1},{4,6},{5,3},{6,0},{7,5},{8,10},{9,15},{10,... | collective-permute-start | bytes 983048 | tf_op jit(solution)/shard_map/ppermute | solution.py:353
  41.2 15.1 %collective-permute-start.7 = (bf16[320,512]{1,0:T(8,128)(2,1)S(1)}, bf16[320,512]{1,0:T(8,128)(2,1)}, u32[]{:S(2)}, u32[]{:S(2)}) collective-permute-start(bf16[320,512]{1,0:T(8,128)(2,1)S(1)} %get-tuple-element.24.refs_0_), channel_id=1, source_target_pairs={{0,4},{1,5},{2,6},{3,7},{4,0},{5,1},{6,2},{7,3},{8,12},{9,13},{10,... | collective-permute-start | bytes 983048 | tf_op jit(solution)/shard_map/ppermute | solution.py:356
  42.7 17.1 %collective-permute-start.6 = (bf16[320,512]{1,0:T(8,128)(2,1)S(1)}, bf16[320,512]{1,0:T(8,128)(2,1)}, u32[]{:S(2)}, u32[]{:S(2)}) collective-permute-start(bf16[320,512]{1,0:T(8,128)(2,1)S(1)} %collective-permute-done.5.refs_1_), channel_id=1, source_target_pairs={{0,2},{1,7},{2,4},{3,1},{4,6},{5,3},{6,0},{7,5},{8,10},{9,15},{10,... | collective-permute-start | bytes 983048 | tf_op jit(solution)/shard_map/ppermute | solution.py:353
  45.3 14.7 %collective-permute-start.12 = (bf16[320,512]{1,0:T(8,128)(2,1)S(1)}, bf16[320,512]{1,0:T(8,128)(2,1)}, u32[]{:S(2)}, u32[]{:S(2)}) collective-permute-start(bf16[320,512]{1,0:T(8,128)(2,1)S(1)} %get-tuple-element.24.refs_0_), channel_id=1, source_target_pairs={{8,0},{16,8},{24,16},{32,24},{40,32},{48,40},{56,48},{64,56},{72,6... | collective-permute-start | bytes 983048 | tf_op jit(solution)/shard_map/ppermute | solution.py:360
  47.2 13.9 %collective-permute-start.11 = (bf16[320,512]{1,0:T(8,128)(2,1)S(1)}, bf16[320,512]{1,0:T(8,128)(2,1)}, u32[]{:S(2)}, u32[]{:S(2)}) collective-permute-start(bf16[320,512]{1,0:T(8,128)(2,1)S(1)} %get-tuple-element.24.refs_0_), channel_id=1, source_target_pairs={{0,8},{8,16},{16,24},{24,32},{32,40},{40,48},{48,56},{56,64},{64,7... | collective-permute-start | bytes 983048 | tf_op jit(solution)/shard_map/ppermute | solution.py:360
  56.2 4.9 %collective-permute-start.8 = (bf16[320,512]{1,0:T(8,128)(2,1)S(1)}, bf16[320,512]{1,0:T(8,128)(2,1)}, u32[]{:S(2)}, u32[]{:S(2)}) collective-permute-start(bf16[320,512]{1,0:T(8,128)(2,1)S(1)} %collective-permute-done.4.refs_2_), channel_id=1, source_target_pairs={{0,1},{1,0},{2,3},{3,2},{4,5},{5,4},{6,7},{7,6},{8,9},{9,8},{10,11... | collective-permute-start | bytes 983048 | tf_op jit(solution)/shard_map/ppermute | solution.py:349
  56.3 4.9 %collective-permute-start.10 = (bf16[320,512]{1,0:T(8,128)(2,1)}, bf16[320,512]{1,0:T(8,128)(2,1)}, u32[]{:S(2)}, u32[]{:S(2)}) collective-permute-start(bf16[320,512]{1,0:T(8,128)(2,1)} %collective-permute-done.7.refs_4_), channel_id=1, source_target_pairs={{0,1},{1,0},{2,3},{3,2},{4,5},{5,4},{6,7},{7,6},{8,9},{9,8},{10,11... | collective-permute-start | bytes 983048 | tf_op jit(solution)/shard_map/ppermute | solution.py:349
  59.9 2.0 %collective-permute-start.9 = (bf16[320,512]{1,0:T(8,128)(2,1)}, bf16[320,512]{1,0:T(8,128)(2,1)}, u32[]{:S(2)}, u32[]{:S(2)}) collective-permute-start(bf16[320,512]{1,0:T(8,128)(2,1)} %collective-permute-done.6.refs_3_), channel_id=1, source_target_pairs={{0,1},{1,0},{2,3},{3,2},{4,5},{5,4},{6,7},{7,6},{8,9},{9,8},{10,11... | collective-permute-start | bytes 983048 | tf_op jit(solution)/shard_map/ppermute | solution.py:349

commit v6 on v5

--- a/solution.py
+++ b/solution.py
@@ -240,11 +240,12 @@
         copies[-1].start()
     agg[...] = jnp.zeros_like(agg)
     hid_b[...] = jnp.zeros_like(hid_b)
+    b_edge = packed32[rows : rows + 1, :]
     for k in range(near):
-        put_rows(table, place[k], refs[k][...].astype(F32))
+        put_rows(table, place[k], refs[k][...].astype(F32) + b_edge)
     for k in range(near, count):
         copies[k - near].wait()
-        put_rows(table, place[k], shard[k - near].astype(F32))
+        put_rows(table, place[k], shard[k - near].astype(F32) + b_edge)
 
     def gather(base, buf):
         for e in range(EDGE_BLOCK):
@@ -256,7 +257,7 @@
         return one_hot(recv[:, pl.ds(base, EDGE_BLOCK)], rows)
 
     def emit(base, buf, hid):
-        received = dot_first(select(base), receivers[...]) + packed32[rows : rows + 1, :]
+        received = dot_first(select(base), receivers[...])
         for j in range(4):
             lanes = slice(j * LANES, (j + 1) * LANES)
             v = buf[pl.ds(j, EDGE_BLOCK, stride=4), :] + received[:, lanes]

time: 70.8 us -> 70.8 us (level)
  no operation moved by 1% of the time
where the time goes in v6:
time: 70.8 us; the launch traced here: 70.2 us
  Pallas kernels  28.3 us (40%)
  waiting for transfers between devices  20.7 us (29%)
  starting transfers between devices  18.5 us (26%)
  other arithmetic  2.16 us (3%)
    pallas_call x1, Pallas kernels, band_sums(): pl.pallas_call(message_kernel, out_shape=[jax.ShapeDtypeStruct((rows, wid...  18.3 us
    ppermute x8, waiting for transfers between devices, by_parity(): return lambda value: lax.ppermute(value, BOTH, pairs)  12.3 us
    ppermute x8, starting transfers between devices, by_parity(): return lambda value: lax.ppermute(value, BOTH, pairs)  9.9 us
    pallas_call x1, Pallas kernels, processor(): pl.pallas_call(processor_kernel, out_shape=jax.ShapeDtypeStruct((rows, wi...  8.31 us
    ppermute x2, waiting for transfers between devices, onward(): return lax.ppermute(value, 'inner', pairs)  7.29 us
    ppermute x2, starting transfers between devices, along_groups(): return lax.ppermute(value, 'grp', pairs)  5.84 us
    ppermute x2, starting transfers between devices, onward(): return lax.ppermute(value, 'inner', pairs)  2.63 us
  transfers between devices with their start and end apart: 13, of which 7 were waited for; matrix products, arithmetic and copies ran while one was open for 3% of the time, Pallas kernels for 1%

profile of v6, /device:TPU:96, one launch (start us, length us, event | category | flops | bytes accessed | tf_op | source)
XLA Modules:
  0.0 70.2 jit_solution(9268373082975748062)
XLA Ops:
  0.0 18.3 %band_sums.1 = (bf16[320,512]{1,0:T(8,128)(2,1)}, bf16[320,512]{1,0:T(8,128)(2,1)}, bf16[320,512]{1,0:T(8,128)(2,1)}, bf16[320,512]{1,0:T(8,128)(2,1)}, bf16[320,512]{1,0:T(8,128)(2,1)}) custom-call(s32[1,4096]{1,0:T(1,128)} %bitcast.21, bf16[474,2048]{1,0:T(8,128)(2,1)} %bitcast.20, bf16[474,512]{1,0:T(8,128)(2,1)} %w_in1_hbm.1, f32[1,512]{1,0:T(1,128)} %bitcast.24, ...), custom_call_target="tpu_custom_call" | custom-call | tf_op jit(solution)/shard_map/band_sums/pallas_call | solution.py:152
  18.3 0.0 copy-start
  18.3 0.0 copy-start.2
  18.3 0.0 copy-start.3
  18.4 0.1 collective-permute-start
  18.5 7.1 %collective-permute-start.2 = (bf16[320,512]{1,0:T(8,128)(2,1)}, bf16[320,512]{1,0:T(8,128)(2,1)S(1)}, u32[]{:S(2)}, u32[]{:S(2)}) collective-permute-start(bf16[320,512]{1,0:T(8,128)(2,1)} %get-tuple-element.23), channel_id=1, source_target_pairs={{1,3},{2,0},{3,5},{4,2},{5,7},{6,4},{7,9},{8,6},{9,11},{10,8},{11,... | collective-permute-start | bytes 983048 | tf_op jit(solution)/shard_map/ppermute | solution.py:350
  25.6 1.1 %add_convert_fusion.1 = bf16[320,512]{1,0:T(8,128)(2,1)S(1)} fusion(bf16[320,512]{1,0:T(8,128)(2,1)S(1)} %collective-permute-done, bf16[320,512]{1,0:T(8,128)(2,1)} %get-tuple-element.20), kind=kLoop, calls=%fused_computation.1 | loop fusion | flops 655360 | bytes 983040 | tf_op jit(solution)/shard_map/convert_element_type | solution.py:382
  26.6 0.0 copy-start.12
  26.6 0.0 copy-start.6
  26.7 0.0 copy-start.7
  26.7 0.0 copy-start.10
  26.7 0.1 collective-permute-start.1
  26.8 2.1 %collective-permute-start.3 = (bf16[320,512]{1,0:T(8,128)(2,1)S(1)}, bf16[320,512]{1,0:T(8,128)(2,1)S(1)}, u32[]{:S(2)}, u32[]{:S(2)}) collective-permute-start(bf16[320,512]{1,0:T(8,128)(2,1)S(1)} %add_convert_fusion.1), channel_id=1, source_target_pairs={{0,2},{2,4},{3,1},{4,6},{5,3},{6,8},{7,5},{8,10},{9,7},{10,12},{11... | collective-permute-start | bytes 983048 | tf_op jit(solution)/shard_map/ppermute | solution.py:350
  28.9 1.6 %collective-permute-done.2 = bf16[320,512]{1,0:T(8,128)(2,1)S(1)} collective-permute-done((bf16[320,512]{1,0:T(8,128)(2,1)}, bf16[320,512]{1,0:T(8,128)(2,1)S(1)}, u32[]{:S(2)}, u32[]{:S(2)}) %collective-permute-start.2) | collective-permute-done | bytes 327712 | tf_op jit(solution)/shard_map/ppermute | solution.py:350
  30.5 1.1 %add_convert_fusion.some = bf16[320,512]{1,0:T(8,128)(2,1)S(1)} fusion(bf16[320,512]{1,0:T(8,128)(2,1)S(1)} %collective-permute-done.2, bf16[320,512]{1,0:T(8,128)(2,1)S(1)} %collective-permute-done.1, bf16[320,512]{1,0:T(8,128)(2,1)} %get-tuple-element.18), kind=kLoop, calls=%fused_computation | loop fusion | flops 983040 | bytes 1310720 | tf_op jit(solution)/shard_map/convert_element_type | solution.py:387
  31.6 8.6 %collective-permute-done.3.one = bf16[320,512]{1,0:T(8,128)(2,1)S(1)} collective-permute-done((bf16[320,512]{1,0:T(8,128)(2,1)S(1)}, bf16[320,512]{1,0:T(8,128)(2,1)S(1)}, u32[]{:S(2)}, u32[]{:S(2)}) %collective-permute-start.3) | collective-permute-done | bytes 327712 | tf_op jit(solution)/shard_map/ppermute | solution.py:350
  40.2 0.9 %encoder.1 = (bf16[320,512]{1,0:T(8,128)(2,1)S(1)}, bf16[320,512]{1,0:T(8,128)(2,1)S(1)}) custom-call(bf16[320,512]{1,0:T(8,128)(2,1)S(1)} %add_convert_fusion.some, bf16[320,512]{1,0:T(8,128)(2,1)S(1)} %collective-permute-done.3.one, bf16[320,512]{1,0:T(8,128)(2,1)S(1)} %copy-done.3, bf16[512,512]{1,0:T(8,128)(2,1)S(1)} %copy-done, f32[1,512]{1,0:T(1,128)S(1)} %bitcast.17, ...), custom_call_target="tpu_custom_call" | custom-call | tf_op jit(solution)/shard_map/encoder/pallas_call | solution.py:188
  41.1 0.1 collective-permute-start.5
  41.2 0.1 collective-permute-start.4
  41.2 0.1 collective-permute-start.7
  41.3 1.4 %collective-permute-done.5.refs_1_ = bf16[320,512]{1,0:T(8,128)(2,1)S(1)} collective-permute-done((bf16[320,512]{1,0:T(8,128)(2,1)S(1)}, bf16[320,512]{1,0:T(8,128)(2,1)S(1)}, u32[]{:S(2)}, u32[]{:S(2)}) %collective-permute-start.5) | collective-permute-done | bytes 327712 | tf_op jit(solution)/shard_map/ppermute | solution.py:350
  42.8 2.6 %collective-permute-start.6 = (bf16[320,512]{1,0:T(8,128)(2,1)S(1)}, bf16[320,512]{1,0:T(8,128)(2,1)}, u32[]{:S(2)}, u32[]{:S(2)}) collective-permute-start(bf16[320,512]{1,0:T(8,128)(2,1)S(1)} %collective-permute-done.5.refs_1_), channel_id=1, source_target_pairs={{0,2},{1,7},{2,4},{3,1},{4,6},{5,3},{6,0},{7,5},{8,10},{9,15},{10,... | collective-permute-start | bytes 983048 | tf_op jit(solution)/shard_map/ppermute | solution.py:354
  45.3 1.9 %collective-permute-start.12 = (bf16[320,512]{1,0:T(8,128)(2,1)S(1)}, bf16[320,512]{1,0:T(8,128)(2,1)}, u32[]{:S(2)}, u32[]{:S(2)}) collective-permute-start(bf16[320,512]{1,0:T(8,128)(2,1)S(1)} %get-tuple-element.24.refs_0_), channel_id=1, source_target_pairs={{8,0},{16,8},{24,16},{32,24},{40,32},{48,40},{56,48},{64,56},{72,6... | collective-permute-start | bytes 983048 | tf_op jit(solution)/shard_map/ppermute | solution.py:361
  47.3 3.9 %collective-permute-start.11 = (bf16[320,512]{1,0:T(8,128)(2,1)S(1)}, bf16[320,512]{1,0:T(8,128)(2,1)}, u32[]{:S(2)}, u32[]{:S(2)}) collective-permute-start(bf16[320,512]{1,0:T(8,128)(2,1)S(1)} %get-tuple-element.24.refs_0_), channel_id=1, source_target_pairs={{0,8},{8,16},{16,24},{24,32},{32,40},{40,48},{48,56},{56,64},{64,7... | collective-permute-start | bytes 983048 | tf_op jit(solution)/shard_map/ppermute | solution.py:361
  51.3 0.8 %receiver_side.1 = (bf16[1664,512]{1,0:T(8,128)(2,1)S(1)}, f32[328,512]{1,0:T(8,128)S(1)}, s32[1,2560]{1,0:T(1,128)S(1)}) custom-call(s32[1,2560]{1,0:T(1,128)S(1)} %reshape.36.send, bf16[320,512]{1,0:T(8,128)(2,1)S(1)} %get-tuple-element.25.lat, bf16[512,512]{1,0:T(8,128)(2,1)S(1)} %copy-done.5, bf16[512,512]{1,0:T(8,128)(2,1)S(1)} %copy-done.6, ...), custom_call_target="tpu_custom_call" | custom-call | flops 1000000000 | bytes 6000000 | tf_op jit(solution)/shard_map/receiver_side/pallas_call | solution.py:213
  52.1 4.2 %collective-permute-done.4.refs_2_ = bf16[320,512]{1,0:T(8,128)(2,1)S(1)} collective-permute-done((bf16[320,512]{1,0:T(8,128)(2,1)S(1)}, bf16[320,512]{1,0:T(8,128)(2,1)S(1)}, u32[]{:S(2)}, u32[]{:S(2)}) %collective-permute-start.4) | collective-permute-done | bytes 327712 | tf_op jit(solution)/shard_map/ppermute | solution.py:354
  56.3 0.5 collective-permute-start.10
  56.8 3.1 %collective-permute-done.6.refs_3_ = bf16[320,512]{1,0:T(8,128)(2,1)} collective-permute-done((bf16[320,512]{1,0:T(8,128)(2,1)S(1)}, bf16[320,512]{1,0:T(8,128)(2,1)}, u32[]{:S(2)}, u32[]{:S(2)}) %collective-permute-start.6) | collective-permute-done | bytes 327712 | tf_op jit(solution)/shard_map/ppermute | solution.py:354
  59.9 0.1 stack.35
  60.0 1.2 %collective-permute-done.11.refs_8_ = bf16[320,512]{1,0:T(8,128)(2,1)} collective-permute-done((bf16[320,512]{1,0:T(8,128)(2,1)S(1)}, bf16[320,512]{1,0:T(8,128)(2,1)}, u32[]{:S(2)}, u32[]{:S(2)}) %collective-permute-start.11) | collective-permute-done | bytes 327712 | tf_op jit(solution)/shard_map/ppermute | solution.py:361
  61.2 0.7 collective-permute-done.9.refs_6_
  61.9 8.3 %processor.1 = bf16[320,512]{1,0:T(8,128)(2,1)} custom-call(s32[10]{0:T(128)S(1)} %broadcast_multiply_fusion.place, s32[1,2560]{1,0:T(1,128)S(1)} %get-tuple-element.27.send, s32[1,2560]{1,0:T(1,128)S(1)} %reshape.39.recv, bf16[1664,512]{1,0:T(8,128)(2,1)S(1)} %get-tuple-element.28.packed, f32[328,512]{1,0:T(8,128)S(1)} %get-tuple-element.29.packed32, ...), custom_call_target="tpu_custom_call" | custom-call | tf_op jit(solution)/shard_map/processor/pallas_call | solution.py:294
  (32 shorter events, 0.1 us)
Async XLA Ops:
  18.3 21.8 %copy-start = (bf16[512,512]{1,0:T(8,128)(2,1)S(1)}, bf16[512,512]{1,0:T(8,128)(2,1)}, u32[]{:S(2)}) copy-start(bf16[512,512]{1,0:T(8,128)(2,1)} %w_enc1.1) | copy-start | bytes 1572868
  18.3 21.8 %copy-start.1 = (bf16[512,512]{1,0:T(8,128)(2,1)S(1)}, bf16[512,512]{1,0:T(8,128)(2,1)}, u32[]{:S(2)}) copy-start(bf16[512,512]{1,0:T(8,128)(2,1)} %w_enc2.1) | copy-start | bytes 1572868
  18.3 21.8 %copy-start.2 = (bf16[512,512]{1,0:T(8,128)(2,1)S(1)}, bf16[512,512]{1,0:T(8,128)(2,1)}, u32[]{:S(2)}) copy-start(bf16[512,512]{1,0:T(8,128)(2,1)} %w_snd.1) | copy-start | bytes 1572868
  18.3 21.8 %copy-start.3 = (bf16[320,512]{1,0:T(8,128)(2,1)S(1)}, bf16[320,512]{1,0:T(8,128)(2,1)}, u32[]{:S(2)}) copy-start(bf16[320,512]{1,0:T(8,128)(2,1)} %emb.1) | copy-start | bytes 983044
  18.4 21.8 %copy-start.4 = (f32[512]{0:T(512)S(1)}, f32[512]{0:T(512)}, u32[]{:S(2)}) copy-start(f32[512]{0:T(512)} %param.40) | copy-start | bytes 6148
  18.4 7.2 %collective-permute-start = (bf16[320,512]{1,0:T(8,128)(2,1)}, bf16[320,512]{1,0:T(8,128)(2,1)S(1)}, u32[]{:S(2)}, u32[]{:S(2)}) collective-permute-start(bf16[320,512]{1,0:T(8,128)(2,1)} %get-tuple-element.21), channel_id=1, source_target_pairs={{0,1},{1,0},{2,3},{3,2},{4,5},{5,4},{6,7},{7,6},{8,9},{9,8},{10,11... | collective-permute-start | bytes 983048 | tf_op jit(solution)/shard_map/ppermute | solution.py:350
  18.5 12.0 %collective-permute-start.2 = (bf16[320,512]{1,0:T(8,128)(2,1)}, bf16[320,512]{1,0:T(8,128)(2,1)S(1)}, u32[]{:S(2)}, u32[]{:S(2)}) collective-permute-start(bf16[320,512]{1,0:T(8,128)(2,1)} %get-tuple-element.23), channel_id=1, source_target_pairs={{1,3},{2,0},{3,5},{4,2},{5,7},{6,4},{7,9},{8,6},{9,11},{10,8},{11,... | collective-permute-start | bytes 983048 | tf_op jit(solution)/shard_map/ppermute | solution.py:350
  26.6 18.7 %copy-start.12 = (s32[2560]{0:T(1024)S(1)}, s32[2560]{0:T(1024)}, u32[]{:S(2)}) copy-start(s32[2560]{0:T(1024)} %param.31) | copy-start | bytes 30724
  26.6 24.6 %copy-start.5 = (bf16[512,512]{1,0:T(8,128)(2,1)S(1)}, bf16[512,512]{1,0:T(8,128)(2,1)}, u32[]{:S(2)}) copy-start(bf16[512,512]{1,0:T(8,128)(2,1)} %w_rcv.1) | copy-start | bytes 1572868
  26.6 24.6 %copy-start.6 = (bf16[512,512]{1,0:T(8,128)(2,1)S(1)}, bf16[512,512]{1,0:T(8,128)(2,1)}, u32[]{:S(2)}) copy-start(bf16[512,512]{1,0:T(8,128)(2,1)} %w_edge.1) | copy-start | bytes 1572868
  26.7 24.6 %copy-start.7 = (bf16[512,512]{1,0:T(8,128)(2,1)S(1)}, bf16[512,512]{1,0:T(8,128)(2,1)}, u32[]{:S(2)}) copy-start(bf16[512,512]{1,0:T(8,128)(2,1)} %w_p1.1) | copy-start | bytes 1572868
  26.7 24.6 %copy-start.8 = (bf16[512,512]{1,0:T(8,128)(2,1)S(1)}, bf16[512,512]{1,0:T(8,128)(2,1)}, u32[]{:S(2)}) copy-start(bf16[512,512]{1,0:T(8,128)(2,1)} %w_p2.1) | copy-start | bytes 1572868
  26.7 24.6 %copy-start.9 = (bf16[512,512]{1,0:T(8,128)(2,1)S(1)}, bf16[512,512]{1,0:T(8,128)(2,1)}, u32[]{:S(2)}) copy-start(bf16[512,512]{1,0:T(8,128)(2,1)} %w_p3.1) | copy-start | bytes 1572868
  26.7 24.6 %copy-start.10 = (f32[512]{0:T(512)S(1)}, f32[512]{0:T(512)}, u32[]{:S(2)}) copy-start(f32[512]{0:T(512)} %param.48) | copy-start | bytes 6148
  26.7 24.6 %copy-start.11 = (f32[512]{0:T(512)S(1)}, f32[512]{0:T(512)}, u32[]{:S(2)}) copy-start(f32[512]{0:T(512)} %param.44) | copy-start | bytes 6148
  26.7 3.8 %collective-permute-start.1 = (bf16[320,512]{1,0:T(8,128)(2,1)}, bf16[320,512]{1,0:T(8,128)(2,1)S(1)}, u32[]{:S(2)}, u32[]{:S(2)}) collective-permute-start(bf16[320,512]{1,0:T(8,128)(2,1)} %get-tuple-element.22), channel_id=1, source_target_pairs={{0,1},{1,0},{2,3},{3,2},{4,5},{5,4},{6,7},{7,6},{8,9},{9,8},{10,11... | collective-permute-start | bytes 983048 | tf_op jit(solution)/shard_map/ppermute | solution.py:350
  26.8 13.3 %collective-permute-start.3 = (bf16[320,512]{1,0:T(8,128)(2,1)S(1)}, bf16[320,512]{1,0:T(8,128)(2,1)S(1)}, u32[]{:S(2)}, u32[]{:S(2)}) collective-permute-start(bf16[320,512]{1,0:T(8,128)(2,1)S(1)} %add_convert_fusion.1), channel_id=1, source_target_pairs={{0,2},{2,4},{3,1},{4,6},{5,3},{6,8},{7,5},{8,10},{9,7},{10,12},{11... | collective-permute-start | bytes 983048 | tf_op jit(solution)/shard_map/ppermute | solution.py:350
  41.1 18.9 %copy-start.13 = (s32[2560]{0:T(1024)S(1)}, s32[2560]{0:T(1024)}, u32[]{:S(2)}) copy-start(s32[2560]{0:T(1024)} %param.32) | copy-start | bytes 30724
  41.1 1.7 %collective-permute-start.5 = (bf16[320,512]{1,0:T(8,128)(2,1)S(1)}, bf16[320,512]{1,0:T(8,128)(2,1)S(1)}, u32[]{:S(2)}, u32[]{:S(2)}) collective-permute-start(bf16[320,512]{1,0:T(8,128)(2,1)S(1)} %get-tuple-element.24.refs_0_), channel_id=1, source_target_pairs={{0,1},{1,0},{2,3},{3,2},{4,5},{5,4},{6,7},{7,6},{8,9},{9,8},{10,11... | collective-permute-start | bytes 983048 | tf_op jit(solution)/shard_map/ppermute | solution.py:350
  41.2 15.1 %collective-permute-start.4 = (bf16[320,512]{1,0:T(8,128)(2,1)S(1)}, bf16[320,512]{1,0:T(8,128)(2,1)S(1)}, u32[]{:S(2)}, u32[]{:S(2)}) collective-permute-start(bf16[320,512]{1,0:T(8,128)(2,1)S(1)} %get-tuple-element.24.refs_0_), channel_id=1, source_target_pairs={{0,2},{1,7},{2,4},{3,1},{4,6},{5,3},{6,0},{7,5},{8,10},{9,15},{10,... | collective-permute-start | bytes 983048 | tf_op jit(solution)/shard_map/ppermute | solution.py:354
  41.2 15.1 %collective-permute-start.7 = (bf16[320,512]{1,0:T(8,128)(2,1)S(1)}, bf16[320,512]{1,0:T(8,128)(2,1)}, u32[]{:S(2)}, u32[]{:S(2)}) collective-permute-start(bf16[320,512]{1,0:T(8,128)(2,1)S(1)} %get-tuple-element.24.refs_0_), channel_id=1, source_target_pairs={{0,4},{1,5},{2,6},{3,7},{4,0},{5,1},{6,2},{7,3},{8,12},{9,13},{10,... | collective-permute-start | bytes 983048 | tf_op jit(solution)/shard_map/ppermute | solution.py:357
  42.8 17.1 %collective-permute-start.6 = (bf16[320,512]{1,0:T(8,128)(2,1)S(1)}, bf16[320,512]{1,0:T(8,128)(2,1)}, u32[]{:S(2)}, u32[]{:S(2)}) collective-permute-start(bf16[320,512]{1,0:T(8,128)(2,1)S(1)} %collective-permute-done.5.refs_1_), channel_id=1, source_target_pairs={{0,2},{1,7},{2,4},{3,1},{4,6},{5,3},{6,0},{7,5},{8,10},{9,15},{10,... | collective-permute-start | bytes 983048 | tf_op jit(solution)/shard_map/ppermute | solution.py:354
  45.3 14.7 %collective-permute-start.12 = (bf16[320,512]{1,0:T(8,128)(2,1)S(1)}, bf16[320,512]{1,0:T(8,128)(2,1)}, u32[]{:S(2)}, u32[]{:S(2)}) collective-permute-start(bf16[320,512]{1,0:T(8,128)(2,1)S(1)} %get-tuple-element.24.refs_0_), channel_id=1, source_target_pairs={{8,0},{16,8},{24,16},{32,24},{40,32},{48,40},{56,48},{64,56},{72,6... | collective-permute-start | bytes 983048 | tf_op jit(solution)/shard_map/ppermute | solution.py:361
  47.3 13.9 %collective-permute-start.11 = (bf16[320,512]{1,0:T(8,128)(2,1)S(1)}, bf16[320,512]{1,0:T(8,128)(2,1)}, u32[]{:S(2)}, u32[]{:S(2)}) collective-permute-start(bf16[320,512]{1,0:T(8,128)(2,1)S(1)} %get-tuple-element.24.refs_0_), channel_id=1, source_target_pairs={{0,8},{8,16},{16,24},{24,32},{32,40},{40,48},{48,56},{56,64},{64,7... | collective-permute-start | bytes 983048 | tf_op jit(solution)/shard_map/ppermute | solution.py:361
  56.3 4.9 %collective-permute-start.8 = (bf16[320,512]{1,0:T(8,128)(2,1)S(1)}, bf16[320,512]{1,0:T(8,128)(2,1)}, u32[]{:S(2)}, u32[]{:S(2)}) collective-permute-start(bf16[320,512]{1,0:T(8,128)(2,1)S(1)} %collective-permute-done.4.refs_2_), channel_id=1, source_target_pairs={{0,1},{1,0},{2,3},{3,2},{4,5},{5,4},{6,7},{7,6},{8,9},{9,8},{10,11... | collective-permute-start | bytes 983048 | tf_op jit(solution)/shard_map/ppermute | solution.py:350
  56.3 4.9 %collective-permute-start.10 = (bf16[320,512]{1,0:T(8,128)(2,1)}, bf16[320,512]{1,0:T(8,128)(2,1)}, u32[]{:S(2)}, u32[]{:S(2)}) collective-permute-start(bf16[320,512]{1,0:T(8,128)(2,1)} %collective-permute-done.7.refs_4_), channel_id=1, source_target_pairs={{0,1},{1,0},{2,3},{3,2},{4,5},{5,4},{6,7},{7,6},{8,9},{9,8},{10,11... | collective-permute-start | bytes 983048 | tf_op jit(solution)/shard_map/ppermute | solution.py:350
  59.9 2.0 %collective-permute-start.9 = (bf16[320,512]{1,0:T(8,128)(2,1)}, bf16[320,512]{1,0:T(8,128)(2,1)}, u32[]{:S(2)}, u32[]{:S(2)}) collective-permute-start(bf16[320,512]{1,0:T(8,128)(2,1)} %collective-permute-done.6.refs_3_), channel_id=1, source_target_pairs={{0,1},{1,0},{2,3},{3,2},{4,5},{5,4},{6,7},{7,6},{8,9},{9,8},{10,11... | collective-permute-start | bytes 983048 | tf_op jit(solution)/shard_map/ppermute | solution.py:350
